TPU v7x, 32 devices: a whole 2x2x4 slice. The times are simulated.
32 devices in a mesh: rep: 2 (over y), tp: 8 (over z, x), grp: 2 (over core).
Axes of the slice: x: 2, y: 2, z: 4, core: 2. Of those that a mesh axis runs over, the one named last changes fastest.
Arguments:
- hidden: bfloat16 [1024, 28672], P(('rep', 'grp'), 'tp'), parts along dimension 0, may hold values from -6 to 6
- row_adapter_index: int32 [1024, 1], P(('rep', 'grp')), parts along dimension 0, may hold values from 0 to 15; in each aligned block of 256 rows (0 to 255, 256 to 511, ...) at most 64 rows name the same one
- down_projection_weight: bfloat16 [28672, 8192], P('tp'), may hold values from -0.046875 to 0.046875
- adapter_first_factor: bfloat16 [16, 28672, 64], P(('tp', 'grp')), may hold values from -0.03125 to 0.03125
- adapter_second_factor: bfloat16 [16, 64, 8192], P(('tp', 'grp')), may hold values from -0.75 to 0.75
Outputs:
- output: bfloat16 [1024, 8192], P(('rep', 'grp'), 'tp'), parts along dimension 0
There are 2 independent parts, one for each index of `rep`. A program takes and returns all parts, laid end to end along the dimension named above; an argument that names none is the same for every part. Nothing has to cross between parts.
Inputs may be any that keep to these rules, and one draw needn't show every extreme that they name: `row_adapter_index`: in each row group (aligned blocks of 256 rows) no adapter is named by more than 64 rows, a bound that some block reaches.
All inputs are finite; a program needn't handle non-finite values.
Results may differ from a plain program's by a relative error of at most 0.0043.
Values may be sent and summed in bfloat16 or wider, within the bound.
No kernel may reach another device: no remote copies, remote signals or barrier semaphores. Data moves between devices by JAX's collectives and lax.ppermute only.
A program may use at most 192 MiB of HBM per device.

v0:
```python
import jax
import jax.numpy as jnp
from jax import lax
from jax.sharding import PartitionSpec as P


def local(
    hidden, row_adapter_index, down_projection_weight, adapter_first_factor, adapter_second_factor
):
    tensor_parallel_count = lax.axis_size("tp")
    grp_count = lax.axis_size("grp")
    owners = tensor_parallel_count * grp_count
    row_count = hidden.shape[0]
    local_hidden_units = hidden.shape[1]
    model_width = down_projection_weight.shape[1]
    adapter_rank_width = adapter_first_factor.shape[2]
    capacity = 4 * row_count // owners
    local_columns = model_width // tensor_parallel_count
    targets = row_adapter_index[:, 0]
    onehot = (targets[:, None] == jnp.arange(owners, dtype=jnp.int32)[None, :]).astype(jnp.int32)
    before = jnp.cumsum(onehot, axis=0) - onehot
    slot_index = jnp.sum(before * onehot, axis=1)
    position = targets * capacity + slot_index
    outgoing = (
        jnp.zeros((owners * capacity, local_hidden_units), jnp.bfloat16).at[position].set(hidden)
    )
    received_blocks = lax.all_to_all(
        outgoing.reshape(owners, capacity, local_hidden_units),
        ("tp", "grp"),
        split_axis=0,
        concat_axis=0,
        tiled=True,
    )
    received_blocks = received_blocks.reshape(
        tensor_parallel_count, grp_count, capacity, local_hidden_units
    )
    first_factor_local = adapter_first_factor[0].reshape(
        tensor_parallel_count, local_hidden_units, adapter_rank_width
    )
    adapter_latent = jnp.einsum(
        "dlwm,dme->lwe", received_blocks, first_factor_local, preferred_element_type=jnp.float32
    ).astype(jnp.bfloat16)
    second_factor_local = adapter_second_factor[0].reshape(
        adapter_rank_width, tensor_parallel_count, local_columns
    )
    update = jnp.einsum(
        "oba,aui->uobi", adapter_latent, second_factor_local, preferred_element_type=jnp.float32
    ).astype(jnp.bfloat16)
    returned = lax.all_to_all(
        update.reshape(owners, capacity, local_columns),
        ("tp", "grp"),
        split_axis=0,
        concat_axis=0,
        tiled=True,
    )
    column_delta = returned.reshape(owners * capacity, local_columns)[position]
    added_delta = column_delta.astype(jnp.float32)
    partial_value = jnp.dot(hidden, down_projection_weight, preferred_element_type=jnp.float32)
    reduced = lax.psum_scatter(partial_value, "tp", scatter_dimension=1, tiled=True)
    return (reduced + added_delta).astype(jnp.bfloat16)


def solution(mesh):
    return jax.shard_map(
        local,
        mesh=mesh,
        in_specs=(
            P(("rep", "grp"), "tp"),
            P(("rep", "grp"), None),
            P("tp", None),
            P(("tp", "grp"), None, None),
            P(("tp", "grp"), None, None),
        ),
        out_specs=P(("rep", "grp"), "tp"),
        check_vma=False,
    )
```

profile of v0, /device:TPU:0, one launch (start us, length us, event | category | flops | bytes accessed | tf_op | source)
XLA Modules:
  0.0 356.3 jit_solution(6801654328629117398)
XLA Ops:
  6.5 0.7 fusion.18
  7.2 0.6 reduce-window.6
  7.8 0.2 slice_reduce_fusion
  8.0 0.8 fusion.17
  8.8 0.7 compare_select_fusion
  9.5 8.4 %scatter_custom_fusion = bf16[1024,3584]{1,0:T(8,128)(2,1)} fusion(s32[256]{0:T(256)S(1)} %bitcast.76, bf16[256,3584]{1,0:T(8,128)(2,1)} %param.5, bf16[]{:T(256)} %constant.4.clone.1), kind=kCustom, calls=%fused_computation.4 | custom fusion | bytes 7340544 | tf_op jit(solution)/shard_map/scatter | solution.py:25
  17.9 0.0 copy-start.1
  17.9 7.5 %all-to-all-start = ((bf16[16,64,3584]{2,1,0:T(8,128)(2,1)}), bf16[16,64,3584]{2,1,0:T(8,128)(2,1)}, u32[]{:S(2)}, u32[]{:S(2)}) async-start(bf16[16,64,3584]{2,1,0:T(8,128)(2,1)} %bitcast.68), calls=%async_computation.1 | async-start | bytes 14680064 | tf_op jit(solution)/shard_map/all_to_all | solution.py:27
  25.4 0.2 reduce-scatter.2.cloned.1.call-start
  25.6 0.0 copy-done.1
  25.7 26.9 %fusion.19 = f32[256,8192]{1,0:T(8,128)} fusion(bf16[256,3584]{1,0:T(8,128)(2,1)S(1)} %copy-done.1, bf16[3584,8192]{1,0:T(8,128)(2,1)} %param.7), kind=kOutput, calls=%fused_computation.24 | convolution fusion | flops 15032385536 | bytes 68943872 | tf_op jit(solution)/shard_map/dot_general | solution.py:58
  52.6 0.0 reduce-scatter.2.cloned.1.call-update
  52.6 0.0 copy-start
  52.6 5.1 %copy.13 = bf16[8,8,8,3584]{3,2,1,0:T(8,128)(2,1)} copy(bf16[8,8,8,3584]{3,1,2,0:T(8,128)(2,1)} %bitcast.72) | data formatting | bytes 7340032
  57.7 0.0 copy-done
  57.7 0.6 copy.14
  58.3 167.2 %all-to-all-done = bf16[16,64,3584]{2,1,0:T(8,128)(2,1)} async-done(((bf16[16,64,3584]{2,1,0:T(8,128)(2,1)}), bf16[16,64,3584]{2,1,0:T(8,128)(2,1)}, u32[]{:S(2)}, u32[]{:S(2)}) %all-to-all-start) | async-done | bytes 7340064 | tf_op jit(solution)/shard_map/all_to_all | solution.py:27
  225.5 8.7 %convert_bitcast_fusion = bf16[8,2,64,1024]{3,2,0,1:T(8,128)(2,1)S(1)} fusion(bf16[64,8,1024]{2,1,0:T(8,128)(2,1)S(1)} %bitcast.71, bf16[8,2,64,3584]{3,2,1,0:T(8,128)(2,1)} %bitcast.6, bf16[8,3584,64,1]{1,0,2,3:T(8,128)(2,1)} %bitcast.67), kind=kOutput, calls=%fused_computation.6 | convolution fusion | flops 605036544 | bytes 14155776 | tf_op jit(solution)/shard_map/oba,aui->uobi/dot_general | solution.py:46
  234.2 1.7 copy.9
  235.9 32.0 %all-to-all-start.1 = ((bf16[16,64,1024]{2,1,0:T(8,128)(2,1)}), bf16[16,64,1024]{2,1,0:T(8,128)(2,1)S(1)}, u32[]{:S(2)}, u32[]{:S(2)}) async-start(bf16[16,64,1024]{2,1,0:T(8,128)(2,1)} %bitcast.70), calls=%async_computation.2 | async-start | bytes 4194304 | tf_op jit(solution)/shard_map/all_to_all | solution.py:49
  267.8 67.7 %all-to-all-done.1 = bf16[16,64,1024]{2,1,0:T(8,128)(2,1)S(1)} async-done(((bf16[16,64,1024]{2,1,0:T(8,128)(2,1)}), bf16[16,64,1024]{2,1,0:T(8,128)(2,1)S(1)}, u32[]{:S(2)}, u32[]{:S(2)}) %all-to-all-start.1) | async-done | bytes 2097184 | tf_op jit(solution)/shard_map/all_to_all | solution.py:49
  335.5 1.2 gather_fusion
  336.7 10.6 %reduce-scatter.2.cloned.1.call-done = f32[256,1024]{1,0:T(8,128)} async-done(((f32[256,8192]{1,0:T(8,128)}), f32[256,1024]{1,0:T(8,128)}) %reduce-scatter.2.cloned.1.call-update) | async-done | bytes 1048592 | tf_op jit(solution)/shard_map/reduce_scatter | solution.py:59
  347.2 2.2 add_convert_fusion
  (3 shorter events, 0.0 us)
Async XLA Ops:
  17.9 7.8 %copy-start.1 = (bf16[256,3584]{1,0:T(8,128)(2,1)S(1)}, bf16[256,3584]{1,0:T(8,128)(2,1)}, u32[]{:S(2)}) copy-start(bf16[256,3584]{1,0:T(8,128)(2,1)} %param.5) | copy-start | bytes 5505028
  17.9 207.6 %all-to-all-start = ((bf16[16,64,3584]{2,1,0:T(8,128)(2,1)}), bf16[16,64,3584]{2,1,0:T(8,128)(2,1)}, u32[]{:S(2)}, u32[]{:S(2)}) async-start(bf16[16,64,3584]{2,1,0:T(8,128)(2,1)} %bitcast.68), calls=%async_computation.1 | async-start | bytes 14680064 | tf_op jit(solution)/shard_map/all_to_all | solution.py:27
  25.4 321.8 %reduce-scatter.2.cloned.1.call-start = ((), (), s32[]{:S(2)}) async-start(), calls=%async_computation.3 | async-start | bytes 9437184 | tf_op jit(solution)/shard_map/reduce_scatter | solution.py:59
  52.6 5.2 %copy-start = (bf16[1,64,8192]{2,1,0:T(8,128)(2,1)S(1)}, bf16[1,64,8192]{2,1,0:T(8,128)(2,1)}, u32[]{:S(2)}) copy-start(bf16[1,64,8192]{2,1,0:T(8,128)(2,1)} %param.9) | copy-start | bytes 3145732
  235.9 99.6 %all-to-all-start.1 = ((bf16[16,64,1024]{2,1,0:T(8,128)(2,1)}), bf16[16,64,1024]{2,1,0:T(8,128)(2,1)S(1)}, u32[]{:S(2)}, u32[]{:S(2)}) async-start(bf16[16,64,1024]{2,1,0:T(8,128)(2,1)} %bitcast.70), calls=%async_computation.2 | async-start | bytes 4194304 | tf_op jit(solution)/shard_map/all_to_all | solution.py:49
Sparse Core Ops, SparseCore 0:
  52.7 294.5 reduce-scatter.1
where the time goes:
time: 359 us; the launch traced here: 356 us
  waiting for transfers between devices  245 us (68%)
  starting transfers between devices  39.7 us (11%)
  matrix products  35.6 us (10%)
  local copies, waits for them, and re-layouts  17.2 us (5%)
  between operations  13.5 us (4%)
  other arithmetic  4.92 us (1%)
    all_to_all x1, waiting for transfers between devices, local(): lax.all_to_all(outgoing.reshape(owners, capacity, local_hidden_units), ('...  167 us
    all_to_all x1, waiting for transfers between devices, local(): lax.all_to_all(update.reshape(owners, capacity, local_columns), ('tp', 'g...  67.7 us
    all_to_all x1, starting transfers between devices, local(): lax.all_to_all(update.reshape(owners, capacity, local_columns), ('tp', 'g...  32 us
    dot_general x1, matrix products, local(): jnp.dot(hidden, down_projection_weight, preferred_element_type=jnp.float32)  26.9 us
    reduce_scatter x1, waiting for transfers between devices, local(): lax.psum_scatter(partial_value, 'tp', scatter_dimension=1, tiled=True)  10.6 us
    dot_general x1, matrix products, local(): jnp.einsum('oba,aui->uobi', adapter_latent, second_factor_local, preferre...  8.66 us
    scatter x1, local copies, waits for them, and re-layouts, local(): jnp.zeros((owners * capacity, local_hidden_units), jnp.bfloat16)  8.4 us
    all_to_all x1, starting transfers between devices, local(): lax.all_to_all(outgoing.reshape(owners, capacity, local_hidden_units), ('...  7.53 us
  transfers between devices with their start and end apart: 3, of which 3 were waited for; matrix products, arithmetic and copies ran while one was open for 12% of the time, Pallas kernels for 0%

commit v1 on v0

v1 whole, which is shorter than its diff:
```python
import jax
import jax.numpy as jnp
from jax import lax
from jax.experimental import pallas as pl
from jax.experimental.pallas import tpu as pltpu
from jax.sharding import PartitionSpec as P

SWAP = ((0, 1), (1, 0))


def block_products(hidden, weight, block_ids, block_count, block_columns, out_dtype):
    rows, depth = hidden.shape

    def kernel(ids_ref, hidden_ref, weight_ref, out_ref):
        out_ref[0] = jnp.dot(
            hidden_ref[...], weight_ref[...], preferred_element_type=jnp.float32
        ).astype(out_dtype)

    return pl.pallas_call(
        kernel,
        out_shape=jax.ShapeDtypeStruct((block_count, rows, block_columns), out_dtype),
        grid_spec=pltpu.PrefetchScalarGridSpec(
            num_scalar_prefetch=1,
            grid=(block_count,),
            in_specs=[
                pl.BlockSpec((rows, depth), lambda b, ids: (0, 0)),
                pl.BlockSpec((depth, block_columns), lambda b, ids: (0, ids[b])),
            ],
            out_specs=pl.BlockSpec((1, rows, block_columns), lambda b, ids: (b, 0, 0)),
        ),
        compiler_params=pltpu.CompilerParams(vmem_limit_bytes=40 * 2**20),
        cost_estimate=pl.CostEstimate(
            flops=2 * rows * depth * block_columns * block_count,
            bytes_accessed=2 * depth * block_columns * block_count,
            transcendentals=0,
        ),
    )(block_ids, hidden, weight)


def local(
    hidden, row_adapter_index, down_projection_weight, adapter_first_factor, adapter_second_factor
):
    tp = lax.axis_size("tp")
    t = lax.axis_index("tp")
    y = lax.axis_index("rep")
    g = lax.axis_index("grp")
    rows, depth = hidden.shape
    rank = adapter_first_factor.shape[2]
    columns = down_projection_weight.shape[1] // tp
    half = depth // 2
    lanes = 2 * rank

    first = adapter_first_factor[0].T.reshape(rank, tp, 2, half)
    first = lax.dynamic_index_in_dim(first, y, 2, keepdims=False).transpose(1, 0, 2)
    first = lax.all_to_all(first, "tp", split_axis=0, concat_axis=0, tiled=True)
    first = first.reshape(tp * rank, half)

    tag = jnp.broadcast_to(row_adapter_index.astype(jnp.bfloat16), (rows, 128))

    def piece(which):
        return jnp.concatenate(
            [lax.dynamic_slice(hidden, (0, which * half), (rows, half)), tag], axis=1
        )

    mine = piece(y)
    from_rep = lax.ppermute(piece(1 - y), "rep", SWAP)
    pair = jnp.concatenate([mine, from_rep], axis=0)
    from_grp = lax.ppermute(pair, "grp", SWAP)

    def latents(block):
        full = lax.dot_general(
            block[:, :half], first, (((1,), (1,)), ((), ())), preferred_element_type=jnp.float32
        )
        adapter = block[:, half:].astype(jnp.int32)
        place = lax.broadcasted_iota(jnp.int32, (block.shape[0], lanes), 1) // rank
        adapter = adapter[:, :lanes]
        total = jnp.zeros((block.shape[0], lanes), jnp.float32)
        for two in range(tp // 2):
            total += jnp.where(
                adapter == (2 * two + place) * 2 + g, full[:, two * lanes : (two + 1) * lanes], 0.0
            )
        return total

    near = latents(pair)
    far = latents(from_grp)
    to_rep = jnp.stack([near[rows:], far[rows:]])
    got = lax.ppermute(to_rep, "rep", SWAP)
    latent = near[:rows] + got[0]
    latent = latent + lax.ppermute(far[:rows] + got[1], "grp", SWAP)
    step = 1
    while step < tp:
        latent = latent + lax.ppermute(latent, "tp", [(i, i ^ step) for i in range(tp)])
        step *= 2
    latent = latent.astype(jnp.bfloat16)

    second = adapter_second_factor[0].reshape(rank, tp, 2, columns // 2)
    second = lax.dynamic_index_in_dim(second, y, 2, keepdims=False).transpose(1, 0, 2)
    second = lax.all_to_all(second, "tp", split_axis=0, concat_axis=0, tiled=True)
    second = second.reshape(tp * rank, columns // 2)
    other = lax.ppermute(second, "rep", SWAP)
    second = jnp.where(
        y == 0,
        jnp.concatenate([second, other], axis=1),
        jnp.concatenate([other, second], axis=1),
    )
    second_twin = lax.ppermute(second, "grp", SWAP)

    place = lax.broadcasted_iota(jnp.int32, (rows, tp * rank), 1) // rank
    wide = jnp.tile(latent, (1, tp // 2))
    zero = jnp.zeros((), jnp.bfloat16)
    delta = jnp.dot(
        jnp.where(row_adapter_index == place * 2 + g, wide, zero),
        second,
        preferred_element_type=jnp.float32,
    ) + jnp.dot(
        jnp.where(row_adapter_index == place * 2 + 1 - g, wide, zero),
        second_twin,
        preferred_element_type=jnp.float32,
    )

    part = {}
    for j in range(tp - 1, 0, -2):
        part[j] = block_products(
            hidden, down_projection_weight, (t ^ j).reshape(1), 1, columns, jnp.bfloat16
        )[0]
    kept = list(range(tp - 2, -1, -2))
    products = block_products(
        hidden,
        down_projection_weight,
        jnp.stack([t ^ j for j in kept]),
        len(kept),
        columns,
        jnp.float32,
    )
    for i, j in enumerate(kept):
        part[j] = products[i]
    step = 1
    while step < tp:
        for j in range(tp - step, 0, -2 * step):
            sent = lax.ppermute(
                part[j].astype(jnp.bfloat16), "tp", [(i, i ^ step) for i in range(tp)]
            )
            part[j ^ step] = part[j ^ step] + sent.astype(jnp.float32)
        step *= 2
    return (part[0] + delta.astype(jnp.bfloat16).astype(jnp.float32)).astype(jnp.bfloat16)


def solution(mesh):
    return jax.shard_map(
        local,
        mesh=mesh,
        in_specs=(
            P(("rep", "grp"), "tp"),
            P(("rep", "grp"), None),
            P("tp", None),
            P(("tp", "grp"), None, None),
            P(("tp", "grp"), None, None),
        ),
        out_specs=P(("rep", "grp"), "tp"),
        check_vma=False,
    )
```

time: 359 us -> 162 us (0.45)
  waiting for transfers between devices: 245 us -> 51.5 us
  Pallas kernels: 0 us -> 33.9 us
  matrix products: 35.6 us -> 9.41 us
  between operations: 13.5 us -> 0.29 us
  starting transfers between devices: 39.7 us -> 30.1 us
  other arithmetic: 4.92 us -> 12.7 us
  local copies, waits for them, and re-layouts: 17.2 us -> 23 us
    all_to_all x2, waiting for transfers between devices: 235 us -> 0.01 us  [the longest x1 0.01 us: local(): first = lax.all_to_all(first, 'tp', split_axis=0, concat_axis=0, tiled=True)]
    ppermute x0 -> x16, waiting for transfers between devices: none -> 51.5 us  [the longest x1 21.7 us: local(): from_rep = lax.ppermute(piece(1 - y), 'rep', SWAP)]
    pallas_call x0 -> x5, Pallas kernels: none -> 33.9 us  [block_products(): pl.pallas_call(kernel, out_shape=jax.ShapeDtypeStruct((block_count, rows,...]
    all_to_all x2, starting transfers between devices: 39.5 us -> 11.9 us  [the longest x1 7.38 us: local(): first = lax.all_to_all(first, 'tp', split_axis=0, concat_axis=0, tiled=True)]
    dot_general x2 -> x4, matrix products: 35.6 us -> 9.41 us  [the longest x2 6.38 us: latents(): lax.dot_general(block[:, :half], first, (((1,), (1,)), ((), ())), preferr...]
    ppermute x0 -> x16, starting transfers between devices: none -> 18.2 us  [the longest x7 8.76 us: local(): lax.ppermute(part[j].astype(jnp.bfloat16), 'tp', [(i, i ^ step) for i in...]
    reduce_scatter x1 -> x0, waiting for transfers between devices: 10.6 us -> none  [local(): lax.psum_scatter(partial_value, 'tp', scatter_dimension=1, tiled=True)]
    scatter x1 -> x0, local copies, waits for them, and re-layouts: 8.4 us -> none  [local(): jnp.zeros((owners * capacity, local_hidden_units), jnp.bfloat16)]
  transfers between devices with their start and end apart: 3 -> 18, of which waited for: 3 -> 5; matrix products, arithmetic and copies ran while one was open for 12% -> 17% of each run, Pallas kernels for 0% -> 21%
where the time goes in v1:
time: 162 us; the launch traced here: 161 us
  waiting for transfers between devices  51.5 us (32%)
  Pallas kernels  33.9 us (21%)
  starting transfers between devices  30.1 us (19%)
  local copies, waits for them, and re-layouts  23 us (14%)
  other arithmetic  12.7 us (8%)
  matrix products  9.41 us (6%)
    pallas_call x5, Pallas kernels, block_products(): pl.pallas_call(kernel, out_shape=jax.ShapeDtypeStruct((block_count, rows,...  33.9 us
    ppermute x1, waiting for transfers between devices, local(): from_rep = lax.ppermute(piece(1 - y), 'rep', SWAP)  21.7 us
    ppermute x7, waiting for transfers between devices, local(): lax.ppermute(part[j].astype(jnp.bfloat16), 'tp', [(i, i ^ step) for i in...  15.2 us
    ppermute x3, waiting for transfers between devices, local(): lax.ppermute(latent, 'tp', [(i, i ^ step) for i in range(tp)])  10.6 us
    ppermute x7, starting transfers between devices, local(): lax.ppermute(part[j].astype(jnp.bfloat16), 'tp', [(i, i ^ step) for i in...  8.76 us
    all_to_all x1, starting transfers between devices, local(): first = lax.all_to_all(first, 'tp', split_axis=0, concat_axis=0, tiled=True)  7.38 us
    dot_general x2, matrix products, latents(): lax.dot_general(block[:, :half], first, (((1,), (1,)), ((), ())), preferr...  6.38 us
    dynamic_slice x1, local copies, waits for them, and re-layouts, local(): lax.dynamic_index_in_dim(first, y, 2, keepdims=False).transpose(1, 0, 2)  5.81 us
  transfers between devices with their start and end apart: 18, of which 5 were waited for; matrix products, arithmetic and copies ran while one was open for 17% of the time, Pallas kernels for 21%

profile of v1, /device:TPU:0, one launch (start us, length us, event | category | flops | bytes accessed | tf_op | source)
XLA Modules:
  0.0 160.9 jit_solution(98240661602887808)
XLA Ops:
  0.0 5.7 %reshape.29 = bf16[64,8,2,1792]{3,2,1,0:T(2,128)(2,1)} reshape(bf16[64,28672]{1,0:T(8,128)(2,1)} %bitcast.95) | data formatting | bytes 7340032 | tf_op jit(solution)/shard_map/reshape | solution.py:53
  5.7 5.8 %constant_dynamic-slice_fusion.1 = bf16[64,8,1,1792]{3,2,1,0:T(2,128)(2,1)S(1)} fusion(bf16[64,8,2,1792]{3,2,1,0:T(2,128)(2,1)} %reshape.29, s32[]{:T(128)S(6)} %select_n.75), kind=kLoop, calls=%fused_computation.108 | loop fusion | bytes 3670020 | tf_op jit(solution)/shard_map/jit(dynamic_index_in_dim)/dynamic_slice | solution.py:54
  11.5 2.2 %copy.27 = bf16[64,8,1,1792]{3,0,1,2:T(8,128)(2,1)} copy(bf16[64,8,1,1792]{3,2,1,0:T(2,128)(2,1)S(1)} %constant_dynamic-slice_fusion.1) | data formatting | bytes 3670016 | tf_op jit(solution)/shard_map/transpose | solution.py:54
  13.8 7.4 %all-to-all-start = ((bf16[8,64,1792]{2,1,0:T(8,128)(2,1)}), bf16[8,64,1792]{2,1,0:T(8,128)(2,1)}, u32[]{:S(2)}, u32[]{:S(2)}) async-start(bf16[8,64,1792]{2,1,0:T(8,128)(2,1)} %bitcast.94), calls=%async_computation | async-start | bytes 3670016 | tf_op jit(solution)/shard_map/all_to_all | solution.py:55
  21.2 0.1 constant_dynamic-slice_fusion.3
  21.3 0.5 copy-done.7
  21.9 0.1 broadcast_in_dim.24
  22.0 1.6 collective-permute-start.7
  23.6 21.7 %collective-permute-done.7 = bf16[256,1920]{1,0:T(8,128)(2,1)S(1)} collective-permute-done((bf16[256,1920]{1,0:T(8,128)(2,1)S(1)}, bf16[256,1920]{1,0:T(8,128)(2,1)S(1)}, u32[]{:S(2)}, u32[]{:S(2)}) %collective-permute-start.7) | collective-permute-done | bytes 983072 | tf_op jit(solution)/shard_map/ppermute | solution.py:66
  45.3 1.4 pad_maximum_fusion
  46.7 5.1 %shard_map.57 = bf16[1,256,1024]{2,1,0:T(8,128)(2,1)S(1)} custom-call(s32[1]{0:T(128)} %bitcast.8.ids_ref, bf16[256,3584]{1,0:T(8,128)(2,1)S(1)} %copy-done, bf16[3584,8192]{1,0:T(8,128)(2,1)} %weight_ref.9), custom_call_target="tpu_custom_call" | custom-call | flops 1879048192 | bytes 7340032 | tf_op jit(solution)/shard_map/pallas_call | solution.py:19
  51.9 1.8 %collective-permute-start.1 = (bf16[256,1024]{1,0:T(8,128)(2,1)S(1)}, bf16[256,1024]{1,0:T(8,128)(2,1)}, u32[]{:S(2)}, u32[]{:S(2)}) collective-permute-start(bf16[256,1024]{1,0:T(8,128)(2,1)S(1)} %bitcast.91), channel_id=1, source_target_pairs={{0,2},{2,0},{4,6},{6,4},{8,10},{10,8},{12,14},{14,12},{1,3},{3,1},... | collective-permute-start | bytes 1572872 | tf_op jit(solution)/shard_map/ppermute | solution.py:140
  53.7 5.1 %shard_map.59 = bf16[1,256,1024]{2,1,0:T(8,128)(2,1)S(1)} custom-call(s32[1]{0:T(128)} %bitcast.14.ids_ref, bf16[256,3584]{1,0:T(8,128)(2,1)S(1)} %copy-done, bf16[3584,8192]{1,0:T(8,128)(2,1)} %weight_ref.9), custom_call_target="tpu_custom_call" | custom-call | flops 1879048192 | bytes 7340032 | tf_op jit(solution)/shard_map/pallas_call | solution.py:19
  58.8 0.3 collective-permute-start.4
  59.2 5.1 %shard_map.58 = bf16[1,256,1024]{2,1,0:T(8,128)(2,1)S(1)} custom-call(s32[1]{0:T(128)} %bitcast.11.ids_ref, bf16[256,3584]{1,0:T(8,128)(2,1)S(1)} %copy-done, bf16[3584,8192]{1,0:T(8,128)(2,1)} %weight_ref.9), custom_call_target="tpu_custom_call" | custom-call | flops 1879048192 | bytes 7340032 | tf_op jit(solution)/shard_map/pallas_call | solution.py:19
  64.3 1.8 %collective-permute-start.3 = (bf16[256,1024]{1,0:T(8,128)(2,1)S(1)}, bf16[256,1024]{1,0:T(8,128)(2,1)}, u32[]{:S(2)}, u32[]{:S(2)}) collective-permute-start(bf16[256,1024]{1,0:T(8,128)(2,1)S(1)} %bitcast.90), channel_id=1, source_target_pairs={{0,2},{2,0},{4,6},{6,4},{8,10},{10,8},{12,14},{14,12},{1,3},{3,1},... | collective-permute-start | bytes 1572872 | tf_op jit(solution)/shard_map/ppermute | solution.py:140
  66.1 2.6 %reshape_squeeze.3 = bf16[64,8,2,512]{3,2,1,0:T(2,128)(2,1)} reshape(bf16[1,64,8192]{2,1,0:T(8,128)(2,1)} %param.9) | data formatting | bytes 2097152 | tf_op jit(solution)/shard_map/reshape;squeeze | solution.py:96
  68.8 2.4 %constant_dynamic-slice_fusion = bf16[64,8,1,512]{3,2,1,0:T(2,128)(2,1)S(1)} fusion(bf16[64,8,2,512]{3,2,1,0:T(2,128)(2,1)} %reshape_squeeze.3, s32[]{:T(128)S(6)} %select_n.75), kind=kLoop, calls=%fused_computation.107 | loop fusion | bytes 1048580 | tf_op jit(solution)/shard_map/jit(dynamic_index_in_dim)/dynamic_slice | solution.py:97
  71.2 1.4 copy.28
  72.7 4.5 %all-to-all-start.1 = ((bf16[8,64,512]{2,1,0:T(8,128)(2,1)}), bf16[8,64,512]{2,1,0:T(8,128)(2,1)}, u32[]{:S(2)}, u32[]{:S(2)}) async-start(bf16[8,64,512]{2,1,0:T(8,128)(2,1)} %bitcast.96), calls=%async_computation.1 | async-start | bytes 1048576 | tf_op jit(solution)/shard_map/all_to_all | solution.py:98
  77.2 3.2 %fusion.2 = f32[512,512]{1,0:T(8,128)S(1)} fusion(bf16[512,1792]{1,0:T(8,128)(2,1)} %bitcast.20, bf16[512,1920]{1,0:T(8,128)(2,1)} %pad_maximum_fusion), kind=kOutput, calls=%fused_computation.3 | convolution fusion | flops 939524096 | bytes 4718592 | tf_op jit(solution)/shard_map/dot_general | solution.py:71
  80.4 3.2 %fusion = f32[512,512]{1,0:T(8,128)S(1)} fusion(bf16[512,1792]{1,0:T(8,128)(2,1)} %bitcast.20, bf16[512,1920]{1,0:T(8,128)(2,1)} %collective-permute-done.8), kind=kOutput, calls=%fused_computation.1 | convolution fusion | flops 939524096 | bytes 4718592 | tf_op jit(solution)/shard_map/dot_general | solution.py:71
  83.6 1.2 fusion.37
  84.9 0.8 pad_maximum_fusion.2
  85.8 1.5 collective-permute-start.9
  87.3 13.2 %shard_map.55 = f32[4,256,1024]{2,1,0:T(8,128)S(1)} custom-call(s32[4]{0:T(128)S(1)} %pad_add_fusion.ids_ref, bf16[256,3584]{1,0:T(8,128)(2,1)S(1)} %copy-done, bf16[3584,8192]{1,0:T(8,128)(2,1)} %weight_ref.9), custom_call_target="tpu_custom_call" | custom-call | flops 7516192768 | bytes 29360128 | tf_op jit(solution)/shard_map/pallas_call | solution.py:19
  100.5 1.9 %copy-done.1 = f32[4,256,1024]{2,1,0:T(8,128)} copy-done((f32[4,256,1024]{2,1,0:T(8,128)}, f32[4,256,1024]{2,1,0:T(8,128)S(1)}, u32[]{:S(2)}) %copy-start.1) | copy-done | bytes 4194328
  102.4 0.5 collective-permute-start.14
  103.0 1.0 fusion.55
  104.1 3.2 %fusion.12 = (bf16[256,1024]{1,0:T(8,128)(2,1)}, bf16[256,1024]{1,0:T(8,128)(2,1)}) fusion(f32[4,256,1024]{2,1,0:T(8,128)} %copy-done.1, bf16[256,1024]{1,0:T(8,128)(2,1)} %collective-permute-done.1, bf16[256,1024]{1,0:T(8,128)(2,1)} %collective-permute-done.4), kind=kLoop, calls=%fused_computation.18 | loop fusion | flops 1572864 | bytes 4194304 | tf_op jit(solution)/shard_map/convert_element_type | solution.py:141
  107.2 2.0 %collective-permute-start.5 = (bf16[256,1024]{1,0:T(8,128)(2,1)}, bf16[256,1024]{1,0:T(8,128)(2,1)}, u32[]{:S(2)}, u32[]{:S(2)}) collective-permute-start(bf16[256,1024]{1,0:T(8,128)(2,1)} %get-tuple-element.6), channel_id=1, source_target_pairs={{0,4},{2,6},{4,0},{6,2},{8,12},{10,14},{12,8},{14,10},{1,5},{3,7},... | collective-permute-start | bytes 1572872 | tf_op jit(solution)/shard_map/ppermute | solution.py:140
  109.2 0.9 fusion.57
  110.2 1.5 collective-permute-start.11
  111.7 4.0 %collective-permute-done.14 = bf16[512,512]{1,0:T(8,128)(2,1)S(1)} collective-permute-done((bf16[512,512]{1,0:T(8,128)(2,1)}, bf16[512,512]{1,0:T(8,128)(2,1)S(1)}, u32[]{:S(2)}, u32[]{:S(2)}) %collective-permute-start.14) | collective-permute-done | bytes 524320 | tf_op jit(solution)/shard_map/ppermute | solution.py:100
  115.7 1.5 maximum_select_fusion
  117.3 0.9 add.156
  118.3 1.7 %collective-permute-start.12 = (f32[256,128]{1,0:T(8,128)S(1)}, f32[256,128]{1,0:T(8,128)S(1)}, u32[]{:S(2)}, u32[]{:S(2)}) collective-permute-start(f32[256,128]{1,0:T(8,128)S(1)} %add.156), channel_id=1, source_target_pairs={{0,4},{2,6},{4,0},{6,2},{8,12},{10,14},{12,8},{14,10},{1,5},{3,7},... | collective-permute-start | bytes 393224 | tf_op jit(solution)/shard_map/ppermute | solution.py:92
  120.0 5.3 %shard_map.56 = bf16[1,256,1024]{2,1,0:T(8,128)(2,1)S(1)} custom-call(s32[1]{0:T(128)} %bitcast.5.ids_ref, bf16[256,3584]{1,0:T(8,128)(2,1)S(1)} %copy-done, bf16[3584,8192]{1,0:T(8,128)(2,1)} %weight_ref.9), custom_call_target="tpu_custom_call" | custom-call | flops 1879048192 | bytes 7340032 | tf_op jit(solution)/shard_map/pallas_call | solution.py:19
  125.3 1.5 collective-permute-start
  126.8 0.6 collective-permute-start.2
  127.5 2.4 %collective-permute-start.13 = (f32[256,128]{1,0:T(8,128)S(1)}, f32[256,128]{1,0:T(8,128)S(1)}, u32[]{:S(2)}, u32[]{:S(2)}) collective-permute-start(f32[256,128]{1,0:T(8,128)S(1)} %add.157), channel_id=1, source_target_pairs={{0,8},{2,10},{4,12},{6,14},{8,0},{10,2},{12,4},{14,6},{1,9},{3,11}... | collective-permute-start | bytes 393224 | tf_op jit(solution)/shard_map/ppermute | solution.py:92
  129.9 1.4 fusion.10
  131.3 0.6 collective-permute-start.6
  132.0 10.6 %collective-permute-done.13 = f32[256,128]{1,0:T(8,128)S(1)} collective-permute-done((f32[256,128]{1,0:T(8,128)S(1)}, f32[256,128]{1,0:T(8,128)S(1)}, u32[]{:S(2)}, u32[]{:S(2)}) %collective-permute-start.13) | collective-permute-done | bytes 131104 | tf_op jit(solution)/shard_map/ppermute | solution.py:92
  142.7 1.7 %fusion.23 = f32[256,1024]{1,0:T(8,128)S(1)} fusion(bf16[512,1024]{1,0:T(8,128)(2,1)} %collective-permute-done.15, s32[]{:T(128)S(6)} %axis_index.35, s32[512]{0:T(512)S(1)} %get-tuple-element.13, s32[512]{0:T(512)S(1)} %get-tuple-element.14, s32[256]{0:T(256)S(1)} %bitcast.99, pred[512]{0:T(512)(128)(4,1)S(1)} %fusion.62, ...), kind=kOutput, calls=%fused_computation.45 | convolution fusion | flops 269221888 | bytes 2364932 | tf_op jit(solution)/shard_map/dot_general | solution.py:115
  144.4 7.2 %collective-permute-done.2 = bf16[256,1024]{1,0:T(8,128)(2,1)S(1)} collective-permute-done((bf16[256,1024]{1,0:T(8,128)(2,1)S(1)}, bf16[256,1024]{1,0:T(8,128)(2,1)S(1)}, u32[]{:S(2)}, u32[]{:S(2)}) %collective-permute-start.2) | collective-permute-done | bytes 524320 | tf_op jit(solution)/shard_map/ppermute | solution.py:140
  151.7 7.9 %collective-permute-done.6 = bf16[256,1024]{1,0:T(8,128)(2,1)S(1)} collective-permute-done((bf16[256,1024]{1,0:T(8,128)(2,1)S(1)}, bf16[256,1024]{1,0:T(8,128)(2,1)S(1)}, u32[]{:S(2)}, u32[]{:S(2)}) %collective-permute-start.6) | collective-permute-done | bytes 524320 | tf_op jit(solution)/shard_map/ppermute | solution.py:140
  159.6 1.3 fusion.17
  (42 shorter events, 0.6 us)
Async XLA Ops:
  13.8 7.4 %copy-start = (bf16[256,3584]{1,0:T(8,128)(2,1)S(1)}, bf16[256,3584]{1,0:T(8,128)(2,1)}, u32[]{:S(2)}) copy-start(bf16[256,3584]{1,0:T(8,128)(2,1)} %hidden_ref.9) | copy-start | bytes 5505028
  13.8 58.9 %all-to-all-start = ((bf16[8,64,1792]{2,1,0:T(8,128)(2,1)}), bf16[8,64,1792]{2,1,0:T(8,128)(2,1)}, u32[]{:S(2)}, u32[]{:S(2)}) async-start(bf16[8,64,1792]{2,1,0:T(8,128)(2,1)} %bitcast.94), calls=%async_computation | async-start | bytes 3670016 | tf_op jit(solution)/shard_map/all_to_all | solution.py:55
  21.2 0.7 copy-start.7
  22.0 23.3 %collective-permute-start.7 = (bf16[256,1920]{1,0:T(8,128)(2,1)S(1)}, bf16[256,1920]{1,0:T(8,128)(2,1)S(1)}, u32[]{:S(2)}, u32[]{:S(2)}) collective-permute-start(bf16[256,1920]{1,0:T(8,128)(2,1)S(1)} %pad_maximum_fusion.1), channel_id=1, source_target_pairs={{0,16},{16,0},{1,17},{17,1},{2,18},{18,2},{3,19},{19,3},{4,20},{20... | collective-permute-start | bytes 2949128 | tf_op jit(solution)/shard_map/ppermute | solution.py:66
  46.7 33.7 %collective-permute-start.8 = (bf16[512,1920]{1,0:T(8,128)(2,1)}, bf16[512,1920]{1,0:T(8,128)(2,1)}, u32[]{:S(2)}, u32[]{:S(2)}) collective-permute-start(bf16[512,1920]{1,0:T(8,128)(2,1)} %pad_maximum_fusion), channel_id=1, source_target_pairs={{0,1},{1,0},{2,3},{3,2},{4,5},{5,4},{6,7},{7,6},{8,9},{9,8},{10,11... | collective-permute-start | bytes 5898248 | tf_op jit(solution)/shard_map/ppermute | solution.py:68
  51.9 52.1 %collective-permute-start.1 = (bf16[256,1024]{1,0:T(8,128)(2,1)S(1)}, bf16[256,1024]{1,0:T(8,128)(2,1)}, u32[]{:S(2)}, u32[]{:S(2)}) collective-permute-start(bf16[256,1024]{1,0:T(8,128)(2,1)S(1)} %bitcast.91), channel_id=1, source_target_pairs={{0,2},{2,0},{4,6},{6,4},{8,10},{10,8},{12,14},{14,12},{1,3},{3,1},... | collective-permute-start | bytes 1572872 | tf_op jit(solution)/shard_map/ppermute | solution.py:140
  58.8 45.2 %collective-permute-start.4 = (bf16[256,1024]{1,0:T(8,128)(2,1)S(1)}, bf16[256,1024]{1,0:T(8,128)(2,1)}, u32[]{:S(2)}, u32[]{:S(2)}) collective-permute-start(bf16[256,1024]{1,0:T(8,128)(2,1)S(1)} %bitcast.92), channel_id=1, source_target_pairs={{0,2},{2,0},{4,6},{6,4},{8,10},{10,8},{12,14},{14,12},{1,3},{3,1},... | collective-permute-start | bytes 1572872 | tf_op jit(solution)/shard_map/ppermute | solution.py:140
  64.3 63.1 %collective-permute-start.3 = (bf16[256,1024]{1,0:T(8,128)(2,1)S(1)}, bf16[256,1024]{1,0:T(8,128)(2,1)}, u32[]{:S(2)}, u32[]{:S(2)}) collective-permute-start(bf16[256,1024]{1,0:T(8,128)(2,1)S(1)} %bitcast.90), channel_id=1, source_target_pairs={{0,2},{2,0},{4,6},{6,4},{8,10},{10,8},{12,14},{14,12},{1,3},{3,1},... | collective-permute-start | bytes 1572872 | tf_op jit(solution)/shard_map/ppermute | solution.py:140
  72.7 29.8 %all-to-all-start.1 = ((bf16[8,64,512]{2,1,0:T(8,128)(2,1)}), bf16[8,64,512]{2,1,0:T(8,128)(2,1)}, u32[]{:S(2)}, u32[]{:S(2)}) async-start(bf16[8,64,512]{2,1,0:T(8,128)(2,1)} %bitcast.96), calls=%async_computation.1 | async-start | bytes 1048576 | tf_op jit(solution)/shard_map/all_to_all | solution.py:98
  84.9 0.9 copy-start.3
  84.9 0.9 copy-start.4
  85.8 17.2 %collective-permute-start.9 = (f32[2,256,128]{2,1,0:T(8,128)}, f32[2,256,128]{2,1,0:T(8,128)}, u32[]{:S(2)}, u32[]{:S(2)}) collective-permute-start(f32[2,256,128]{2,1,0:T(8,128)} %pad_maximum_fusion.2), channel_id=1, source_target_pairs={{0,16},{16,0},{1,17},{17,1},{2,18},{18,2},{3,19},{19,3},{4,20},{20... | collective-permute-start | bytes 786440 | tf_op jit(solution)/shard_map/ppermute | solution.py:87
  100.5 2.0 %copy-start.1 = (f32[4,256,1024]{2,1,0:T(8,128)}, f32[4,256,1024]{2,1,0:T(8,128)S(1)}, u32[]{:S(2)}) copy-start(f32[4,256,1024]{2,1,0:T(8,128)S(1)} %shard_map.55) | copy-start | bytes 12582916
  102.4 13.3 %collective-permute-start.14 = (bf16[512,512]{1,0:T(8,128)(2,1)}, bf16[512,512]{1,0:T(8,128)(2,1)S(1)}, u32[]{:S(2)}, u32[]{:S(2)}) collective-permute-start(bf16[512,512]{1,0:T(8,128)(2,1)} %bitcast.26), channel_id=1, source_target_pairs={{0,16},{16,0},{1,17},{17,1},{2,18},{18,2},{3,19},{19,3},{4,20},{20... | collective-permute-start | bytes 1572872 | tf_op jit(solution)/shard_map/ppermute | solution.py:100
  103.9 5.3 %copy-start.5 = (f32[512,128]{1,0:T(8,128)S(1)}, f32[512,128]{1,0:T(8,128)}, u32[]{:S(2)}) copy-start(f32[512,128]{1,0:T(8,128)} %copy-done.4) | copy-start | bytes 786436
  104.0 5.3 %collective-permute-start.10 = (f32[256,128]{1,0:T(8,128)S(1)}, f32[256,128]{1,0:T(8,128)S(1)}, u32[]{:S(2)}, u32[]{:S(2)}) collective-permute-start(f32[256,128]{1,0:T(8,128)S(1)} %fusion.55), channel_id=1, source_target_pairs={{0,1},{1,0},{2,3},{3,2},{4,5},{5,4},{6,7},{7,6},{8,9},{9,8},{10,11... | collective-permute-start | bytes 393224 | tf_op jit(solution)/shard_map/ppermute | solution.py:89
  107.2 22.7 %collective-permute-start.5 = (bf16[256,1024]{1,0:T(8,128)(2,1)}, bf16[256,1024]{1,0:T(8,128)(2,1)}, u32[]{:S(2)}, u32[]{:S(2)}) collective-permute-start(bf16[256,1024]{1,0:T(8,128)(2,1)} %get-tuple-element.6), channel_id=1, source_target_pairs={{0,4},{2,6},{4,0},{6,2},{8,12},{10,14},{12,8},{14,10},{1,5},{3,7},... | collective-permute-start | bytes 1572872 | tf_op jit(solution)/shard_map/ppermute | solution.py:140
  110.2 7.2 %collective-permute-start.11 = (f32[256,128]{1,0:T(8,128)S(1)}, f32[256,128]{1,0:T(8,128)}, u32[]{:S(2)}, u32[]{:S(2)}) collective-permute-start(f32[256,128]{1,0:T(8,128)S(1)} %fusion.57), channel_id=1, source_target_pairs={{0,2},{2,0},{4,6},{6,4},{8,10},{10,8},{12,14},{14,12},{1,3},{3,1},... | collective-permute-start | bytes 393224 | tf_op jit(solution)/shard_map/ppermute | solution.py:92
  117.3 25.4 %collective-permute-start.15 = (bf16[512,1024]{1,0:T(8,128)(2,1)S(1)}, bf16[512,1024]{1,0:T(8,128)(2,1)}, u32[]{:S(2)}, u32[]{:S(2)}) collective-permute-start(bf16[512,1024]{1,0:T(8,128)(2,1)S(1)} %maximum_select_fusion), channel_id=1, source_target_pairs={{0,1},{1,0},{2,3},{3,2},{4,5},{5,4},{6,7},{7,6},{8,9},{9,8},{10,11... | collective-permute-start | bytes 3145736 | tf_op jit(solution)/shard_map/ppermute | solution.py:106
  118.3 8.5 %collective-permute-start.12 = (f32[256,128]{1,0:T(8,128)S(1)}, f32[256,128]{1,0:T(8,128)S(1)}, u32[]{:S(2)}, u32[]{:S(2)}) collective-permute-start(f32[256,128]{1,0:T(8,128)S(1)} %add.156), channel_id=1, source_target_pairs={{0,4},{2,6},{4,0},{6,2},{8,12},{10,14},{12,8},{14,10},{1,5},{3,7},... | collective-permute-start | bytes 393224 | tf_op jit(solution)/shard_map/ppermute | solution.py:92
  120.0 6.8 %copy-start.6 = (bf16[256,1024]{1,0:T(8,128)(2,1)S(1)}, bf16[256,1024]{1,0:T(8,128)(2,1)}, u32[]{:S(2)}) copy-start(bf16[256,1024]{1,0:T(8,128)(2,1)} %get-tuple-element.5) | copy-start | bytes 1572868
  120.0 9.9 %copy-start.2 = (f32[4,256,1024]{2,1,0:T(8,128)S(1)}, f32[4,256,1024]{2,1,0:T(8,128)}, u32[]{:S(2)}) copy-start(f32[4,256,1024]{2,1,0:T(8,128)} %copy-done.1) | copy-start | bytes 12582916
  125.3 19.2 %collective-permute-start = (bf16[256,1024]{1,0:T(8,128)(2,1)S(1)}, bf16[256,1024]{1,0:T(8,128)(2,1)S(1)}, u32[]{:S(2)}, u32[]{:S(2)}) collective-permute-start(bf16[256,1024]{1,0:T(8,128)(2,1)S(1)} %bitcast.93), channel_id=1, source_target_pairs={{0,2},{2,0},{4,6},{6,4},{8,10},{10,8},{12,14},{14,12},{1,3},{3,1},... | collective-permute-start | bytes 1572872 | tf_op jit(solution)/shard_map/ppermute | solution.py:140
  126.8 24.8 %collective-permute-start.2 = (bf16[256,1024]{1,0:T(8,128)(2,1)S(1)}, bf16[256,1024]{1,0:T(8,128)(2,1)S(1)}, u32[]{:S(2)}, u32[]{:S(2)}) collective-permute-start(bf16[256,1024]{1,0:T(8,128)(2,1)S(1)} %copy-done.6), channel_id=1, source_target_pairs={{0,4},{2,6},{4,0},{6,2},{8,12},{10,14},{12,8},{14,10},{1,5},{3,7},... | collective-permute-start | bytes 1572872 | tf_op jit(solution)/shard_map/ppermute | solution.py:140
  127.5 15.1 %collective-permute-start.13 = (f32[256,128]{1,0:T(8,128)S(1)}, f32[256,128]{1,0:T(8,128)S(1)}, u32[]{:S(2)}, u32[]{:S(2)}) collective-permute-start(f32[256,128]{1,0:T(8,128)S(1)} %add.157), channel_id=1, source_target_pairs={{0,8},{2,10},{4,12},{6,14},{8,0},{10,2},{12,4},{14,6},{1,9},{3,11}... | collective-permute-start | bytes 393224 | tf_op jit(solution)/shard_map/ppermute | solution.py:92
  131.3 28.3 %collective-permute-start.6 = (bf16[256,1024]{1,0:T(8,128)(2,1)S(1)}, bf16[256,1024]{1,0:T(8,128)(2,1)S(1)}, u32[]{:S(2)}, u32[]{:S(2)}) collective-permute-start(bf16[256,1024]{1,0:T(8,128)(2,1)S(1)} %fusion.10), channel_id=1, source_target_pairs={{0,8},{2,10},{4,12},{6,14},{8,0},{10,2},{12,4},{14,6},{1,9},{3,11}... | collective-permute-start | bytes 1572872 | tf_op jit(solution)/shard_map/ppermute | solution.py:140

commit v2 on v0

v2 whole, which is shorter than its diff:
```python
import jax
import jax.numpy as jnp
from jax import lax
from jax.experimental import pallas as pl
from jax.experimental.pallas import tpu as pltpu
from jax.sharding import PartitionSpec as P

SWAP = ((0, 1), (1, 0))
ANY = pl.BlockSpec(memory_space=pl.ANY)
VMEM = pl.BlockSpec(memory_space=pltpu.VMEM)
TAG_ROWS = 16


def params():
    return pltpu.CompilerParams(vmem_limit_bytes=48 * 2**20)


def block_products(hidden, weight, block_ids, block_columns, out_dtype, after):
    rows, depth = hidden.shape
    count = len(block_ids)

    def kernel(ids_ref, hidden_ref, weight_ref, after_ref, *out_refs):
        for i, out_ref in enumerate(out_refs):

            @pl.when(pl.program_id(0) == i)
            def _():
                out_ref[...] = jnp.dot(
                    hidden_ref[...], weight_ref[...], preferred_element_type=jnp.float32
                ).astype(out_dtype)

    return pl.pallas_call(
        kernel,
        out_shape=[jax.ShapeDtypeStruct((rows, block_columns), out_dtype)] * count,
        grid_spec=pltpu.PrefetchScalarGridSpec(
            num_scalar_prefetch=1,
            grid=(count,),
            in_specs=[
                pl.BlockSpec((rows, depth), lambda b, ids: (0, 0)),
                pl.BlockSpec((depth, block_columns), lambda b, ids: (0, ids[b])),
                ANY,
            ],
            out_specs=[pl.BlockSpec((rows, block_columns), lambda b, ids: (0, 0))] * count,
        ),
        compiler_params=params(),
        cost_estimate=pl.CostEstimate(
            flops=2 * rows * depth * block_columns * count,
            bytes_accessed=2 * depth * block_columns * count,
            transcendentals=0,
        ),
    )(jnp.stack(block_ids), hidden, weight, after)


def pack_columns(source, pieces, width, y, after):
    rows = source.shape[0]
    if width % 128:
        parts = source.reshape(rows, pieces, 2, width)
        return lax.dynamic_index_in_dim(parts, y, 2, keepdims=False).transpose(1, 0, 2)

    def kernel(y_ref, source_ref, after_ref, out_ref, buffer, in_sem, out_sem):
        def fetch(i):
            start = pl.multiple_of((2 * i + y_ref[0]) * width, 128)
            return pltpu.make_async_copy(
                source_ref.at[:, pl.ds(start, width)], buffer.at[i], in_sem.at[i]
            )

        def store(i):
            return pltpu.make_async_copy(buffer.at[i], out_ref.at[i], out_sem.at[i])

        for i in range(pieces):
            fetch(i).start()
        for i in range(pieces):
            fetch(i).wait()
            store(i).start()
        for i in range(pieces):
            store(i).wait()

    return pl.pallas_call(
        kernel,
        out_shape=jax.ShapeDtypeStruct((pieces, rows, width), source.dtype),
        in_specs=[pl.BlockSpec(memory_space=pltpu.SMEM), ANY, ANY],
        out_specs=ANY,
        scratch_shapes=[
            pltpu.VMEM((pieces, rows, width), source.dtype),
            pltpu.SemaphoreType.DMA((pieces,)),
            pltpu.SemaphoreType.DMA((pieces,)),
        ],
        compiler_params=params(),
        cost_estimate=pl.CostEstimate(
            flops=0, bytes_accessed=4 * pieces * rows * width, transcendentals=0
        ),
    )(y.reshape(1), source, after)


def pack_hidden(hidden, tags, half, y, after):
    rows = hidden.shape[0]
    if half % 128 or half < rows:
        return [
            jnp.concatenate(
                [lax.dynamic_slice(hidden, (0, which * half), (rows, half)), tags], axis=0
            )
            for which in (y, 1 - y)
        ]
    chunks = 4
    step = rows // chunks

    def kernel(y_ref, hidden_ref, tags_ref, after_ref, mine_ref, other_ref, buffer, in_sem, out_sem):
        def fetch(which, i):
            half_index = y_ref[0] if which == 0 else 1 - y_ref[0]
            return pltpu.make_async_copy(
                hidden_ref.at[
                    pl.ds(i * step, step), pl.ds(pl.multiple_of(half_index * half, 128), half)
                ],
                buffer.at[which, pl.ds(i * step, step)],
                in_sem.at[which, i],
            )

        def store(which):
            out_ref = (mine_ref, other_ref)[which]
            return pltpu.make_async_copy(buffer.at[which], out_ref, out_sem.at[which])

        for which in (1, 0):
            for i in range(chunks):
                fetch(which, i).start()
        for which in (1, 0):
            buffer[which, rows:] = tags_ref[...]
        for which in (1, 0):
            for i in range(chunks):
                fetch(which, i).wait()
            store(which).start()
        for which in (1, 0):
            store(which).wait()

    shape = jax.ShapeDtypeStruct((rows + TAG_ROWS, half), hidden.dtype)
    return pl.pallas_call(
        kernel,
        out_shape=[shape, shape],
        in_specs=[pl.BlockSpec(memory_space=pltpu.SMEM), ANY, VMEM, ANY],
        out_specs=[ANY, ANY],
        scratch_shapes=[
            pltpu.VMEM((2, rows + TAG_ROWS, half), hidden.dtype),
            pltpu.SemaphoreType.DMA((2, chunks)),
            pltpu.SemaphoreType.DMA((2,)),
        ],
        compiler_params=params(),
        cost_estimate=pl.CostEstimate(
            flops=0, bytes_accessed=8 * rows * half, transcendentals=0
        ),
    )(y.reshape(1), hidden, tags, after)


def latent_terms(first, blocks, rows, rank, g, after):
    count, half = first.shape
    tp = count // rank

    def term(factor, rows_held, adapter, core):
        full = lax.dot_general(
            factor, rows_held, (((1,), (1,)), ((), ())), preferred_element_type=jnp.float32
        )
        total = jnp.zeros((rank, rows), jnp.float32)
        for place in range(tp):
            total += jnp.where(
                adapter == place * 2 + core, full[place * rank : (place + 1) * rank], 0.0
            )
        return total

    if half % 128 or half < rows:
        return [
            term(
                first, block[:rows], block[rows:].reshape(-1)[:rows][None].astype(jnp.int32), g
            )
            for block in blocks
        ]

    def kernel(g_ref, first_ref, *refs):
        block_refs, out_refs = refs[: len(blocks)], refs[len(blocks) + 1 :]
        for block_ref, out_ref in zip(block_refs, out_refs):
            tag = block_ref[rows:, :rows].astype(jnp.float32)[0:1].astype(jnp.int32)
            out_ref[...] = term(first_ref[...], block_ref[:rows, :], tag, g_ref[0])

    return pl.pallas_call(
        kernel,
        out_shape=[jax.ShapeDtypeStruct((rank, rows), jnp.float32)] * len(blocks),
        in_specs=[pl.BlockSpec(memory_space=pltpu.SMEM), VMEM] + [VMEM] * len(blocks) + [ANY],
        out_specs=[VMEM] * len(blocks),
        compiler_params=params(),
        cost_estimate=pl.CostEstimate(
            flops=2 * count * half * rows * len(blocks),
            bytes_accessed=2 * half * (count + rows * len(blocks)),
            transcendentals=0,
        ),
    )(g.reshape(1), first, *blocks, after)


def finish(latent, adapter, seconds, base, received, y, g):
    rows, columns = base.shape
    rank = latent.shape[0]
    tp = seconds[0].shape[0] // rank
    half = columns // 2

    def spread(held, ids, core):
        zero = jnp.zeros_like(held)
        return jnp.concatenate(
            [jnp.where(ids == place * 2 + core, held, zero) for place in range(tp)], axis=0
        )

    def product(left, right):
        return lax.dot_general(
            left, right, (((0,), (0,)), ((), ())), preferred_element_type=jnp.float32
        )

    if half % 128:
        near = spread(latent, adapter, g).astype(jnp.bfloat16)
        far = spread(latent, adapter, 1 - g).astype(jnp.bfloat16)
        mine = product(near, seconds[0]) + product(far, seconds[2])
        other = product(near, seconds[1]) + product(far, seconds[3])
        delta = jnp.where(
            y == 0,
            jnp.concatenate([mine, other], axis=1),
            jnp.concatenate([other, mine], axis=1),
        )
        total = base
        for block in received:
            total = total + block.astype(jnp.float32)
        return (total + delta.astype(jnp.bfloat16).astype(jnp.float32)).astype(jnp.bfloat16)

    def kernel(y_ref, g_ref, latent_ref, adapter_ref, *refs):
        second_refs, base_ref, received_refs, out_ref = refs[:4], refs[4], refs[5:-1], refs[-1]
        held = latent_ref[...].astype(jnp.bfloat16).astype(jnp.float32)
        near = spread(held, adapter_ref[...], g_ref[0]).astype(jnp.bfloat16)
        far = spread(held, adapter_ref[...], 1 - g_ref[0]).astype(jnp.bfloat16)
        for which in range(2):
            index = y_ref[0] if which == 0 else 1 - y_ref[0]
            lanes = pl.ds(pl.multiple_of(index * half, 128), half)
            delta = product(near, second_refs[which][...])
            delta += product(far, second_refs[2 + which][...])
            total = base_ref[:, lanes]
            for received_ref in received_refs:
                total += received_ref[:, lanes].astype(jnp.float32)
            total += delta.astype(jnp.bfloat16).astype(jnp.float32)
            out_ref[:, lanes] = total.astype(jnp.bfloat16)

    smem = pl.BlockSpec(memory_space=pltpu.SMEM)
    return pl.pallas_call(
        kernel,
        out_shape=jax.ShapeDtypeStruct((rows, columns), jnp.bfloat16),
        in_specs=[smem, smem] + [VMEM] * (7 + len(received)),
        out_specs=VMEM,
        compiler_params=params(),
        cost_estimate=pl.CostEstimate(
            flops=4 * tp * rank * rows * columns,
            bytes_accessed=rows * columns * (6 + 2 * len(received)) + 4 * tp * rank * columns,
            transcendentals=0,
        ),
    )(y.reshape(1), g.reshape(1), latent, adapter, *seconds, base, *received)


def local(
    hidden, row_adapter_index, down_projection_weight, adapter_first_factor, adapter_second_factor
):
    tp = lax.axis_size("tp")
    t = lax.axis_index("tp")
    y = lax.axis_index("rep")
    g = lax.axis_index("grp")
    rows, depth = hidden.shape
    rank = adapter_first_factor.shape[2]
    columns = down_projection_weight.shape[1] // tp
    half = depth // 2
    adapter = row_adapter_index.T

    def across(step):
        return [(i, i ^ step) for i in range(tp)]

    first = pack_columns(adapter_first_factor[0].T, tp, half, y, row_adapter_index)
    packed_first = first
    first = lax.all_to_all(first, "tp", split_axis=0, concat_axis=0, tiled=True)
    first = first.reshape(tp * rank, half)

    part = {}

    def multiply(js, out_dtype, after):
        outs = block_products(
            hidden, down_projection_weight, [t ^ j for j in js], columns, out_dtype, after
        )
        part.update(zip(js, outs))
        return outs[-1]

    odd = list(range(tp - 1, 0, -2))
    even = [j - 1 for j in odd]
    last = multiply(odd[:1], jnp.bfloat16, packed_first)

    tag_lanes = jnp.pad(adapter[0], (0, -rows % half if rows > half else half - rows))
    tags = tag_lanes.astype(jnp.bfloat16).reshape(-1, half)
    tags = jnp.pad(tags, ((0, TAG_ROWS - tags.shape[0]), (0, 0)))
    mine, other = pack_hidden(hidden, tags, half, y, last)
    from_rep = lax.ppermute(other, "rep", SWAP)
    from_grp = lax.ppermute(mine, "grp", SWAP)

    last = multiply(odd[1:3], jnp.bfloat16, mine)
    if odd[3:]:
        last = multiply(odd[3:], jnp.bfloat16, last)
    second = pack_columns(adapter_second_factor[0], tp, columns // 2, y, last)
    last = multiply(even, jnp.float32, second)
    second = lax.all_to_all(second, "tp", split_axis=0, concat_axis=0, tiled=True)
    second = second.reshape(tp * rank, columns // 2)
    second_other = lax.ppermute(second, "rep", SWAP)
    seconds = [
        second,
        second_other,
        lax.ppermute(second, "grp", SWAP),
        lax.ppermute(second_other, "grp", SWAP),
    ]

    from_both = lax.ppermute(from_rep, "grp", SWAP)
    away = latent_terms(first, [from_rep, from_both], rows, rank, g, last)
    here = latent_terms(first, [mine, from_grp], rows, rank, g, away[0])
    got = lax.ppermute(jnp.stack(away), "rep", SWAP)
    latent = here[0] + got[0] + lax.ppermute(here[1] + got[1], "grp", SWAP)
    step = 1
    while step < tp:
        latent = latent + lax.ppermute(latent, "tp", across(step))
        step *= 2
    latent = latent.astype(jnp.bfloat16).astype(jnp.float32)

    received = []
    step = 1
    while step < tp:
        for j in range(tp - step, 0, -2 * step):
            sent = lax.ppermute(part[j].astype(jnp.bfloat16), "tp", across(step))
            if j == step:
                received.append(sent)
            else:
                part[j ^ step] = part[j ^ step] + sent.astype(jnp.float32)
        step *= 2
    return finish(latent, adapter, seconds, part[0], received, y, g)


def solution(mesh):
    return jax.shard_map(
        local,
        mesh=mesh,
        in_specs=(
            P(("rep", "grp"), "tp"),
            P(("rep", "grp"), None),
            P("tp", None),
            P(("tp", "grp"), None, None),
            P(("tp", "grp"), None, None),
        ),
        out_specs=P(("rep", "grp"), "tp"),
        check_vma=False,
    )
```

time: 359 us -> 156 us (0.43)
  waiting for transfers between devices: 245 us -> 60.8 us
  Pallas kernels: 0 us -> 46.7 us
  matrix products: 35.6 us -> 0 us
  between operations: 13.5 us -> 0.3 us
  local copies, waits for them, and re-layouts: 17.2 us -> 9.78 us
  starting transfers between devices: 39.7 us -> 32.8 us
    all_to_all x2, waiting for transfers between devices: 235 us -> 3.78 us  [the longest x1 3.78 us: local(): lax.all_to_all(second, 'tp', split_axis=0, concat_axis=0, tiled=True)]
    ppermute x0 -> x18, waiting for transfers between devices: none -> 57 us  [the longest x3 24.4 us: local(): latent = latent + lax.ppermute(latent, 'tp', across(step))]
    pallas_call x0 -> x10, Pallas kernels: none -> 46.7 us  [the longest x4 32.6 us: block_products(): pl.pallas_call(kernel, out_shape=[jax.ShapeDtypeStruct((rows, block_colum...]
    dot_general x2 -> x0, matrix products: 35.6 us -> none  [the longest x1 26.9 us: local(): jnp.dot(hidden, down_projection_weight, preferred_element_type=jnp.float32)]
    all_to_all x2, starting transfers between devices: 39.5 us -> 13.1 us  [the longest x1 7.38 us: local(): first = lax.all_to_all(first, 'tp', split_axis=0, concat_axis=0, tiled=True)]
    ppermute x0 -> x18, starting transfers between devices: none -> 19.7 us  [the longest x7 11 us: local(): sent = lax.ppermute(part[j].astype(jnp.bfloat16), 'tp', across(step))]
    reduce_scatter x1 -> x0, waiting for transfers between devices: 10.6 us -> none  [local(): lax.psum_scatter(partial_value, 'tp', scatter_dimension=1, tiled=True)]
    scatter x1 -> x0, local copies, waits for them, and re-layouts: 8.4 us -> none  [local(): jnp.zeros((owners * capacity, local_hidden_units), jnp.bfloat16)]
  transfers between devices with their start and end apart: 3 -> 20, of which waited for: 3 -> 8; matrix products, arithmetic and copies ran while one was open for 12% -> 3% of each run, Pallas kernels for 0% -> 26%
where the time goes in v2:
time: 156 us
  waiting for transfers between devices  60.8 us (39%)
  Pallas kernels  46.7 us (30%)
  starting transfers between devices  32.8 us (21%)
  local copies, waits for them, and re-layouts  9.78 us (6%)
  other arithmetic  5.17 us (3%)
    pallas_call x4, Pallas kernels, block_products(): pl.pallas_call(kernel, out_shape=[jax.ShapeDtypeStruct((rows, block_colum...  32.6 us
    ppermute x3, waiting for transfers between devices, local(): latent = latent + lax.ppermute(latent, 'tp', across(step))  24.4 us
    ppermute x7, waiting for transfers between devices, local(): sent = lax.ppermute(part[j].astype(jnp.bfloat16), 'tp', across(step))  18.8 us
    ppermute x1, waiting for transfers between devices, local(): from_rep = lax.ppermute(other, 'rep', SWAP)  11.9 us
    ppermute x7, starting transfers between devices, local(): sent = lax.ppermute(part[j].astype(jnp.bfloat16), 'tp', across(step))  11 us
    unnamed x27, local copies, waits for them, and re-layouts  9.75 us
    all_to_all x1, starting transfers between devices, local(): first = lax.all_to_all(first, 'tp', split_axis=0, concat_axis=0, tiled=True)  7.38 us
    pallas_call x2, Pallas kernels, latent_terms(): pl.pallas_call(kernel, out_shape=[jax.ShapeDtypeStruct((rank, rows), jnp....  6.15 us
  transfers between devices with their start and end apart: 20, of which 8 were waited for; matrix products, arithmetic and copies ran while one was open for 3% of the time, Pallas kernels for 26%

profile of v2, /device:TPU:0, one launch (start us, length us, event | category | flops | bytes accessed | tf_op | source)
XLA Modules:
  0.0 155.6 jit_solution(5158685026145600697)
XLA Ops:
  0.0 0.8 copy.6.after_ref
  0.8 2.0 %copy-done.3 = bf16[1,28672,64]{1,2,0:T(8,128)(2,1)S(1)} copy-done((bf16[1,28672,64]{1,2,0:T(8,128)(2,1)S(1)}, bf16[1,28672,64]{1,2,0:T(8,128)(2,1)}, u32[]{:S(2)}) %copy-start.3) | copy-done | bytes 3670040
  2.9 2.9 %shard_map.55.after_ref = bf16[8,64,1792]{2,1,0:T(8,128)(2,1)S(1)} custom-call(s32[1]{0:T(128)} %bitcast.y_ref, bf16[64,28672]{1,0:T(8,128)(2,1)S(1)} %bitcast.29, s32[256,1]{1,0:T(8,128)S(1)} %copy.6.after_ref), custom_call_target="tpu_custom_call" | custom-call | bytes 3670016 | tf_op jit(solution)/shard_map/pallas_call | solution.py:77
  5.7 1.2 copy-done.1
  6.9 7.4 %all-to-all-start = ((bf16[8,64,1792]{2,1,0:T(8,128)(2,1)}), bf16[8,64,1792]{2,1,0:T(8,128)(2,1)}, u32[]{:S(2)}, u32[]{:S(2)}) async-start(bf16[8,64,1792]{2,1,0:T(8,128)(2,1)} %copy-done.1), calls=%async_computation | async-start | bytes 3670016 | tf_op jit(solution)/shard_map/all_to_all | solution.py:275
  14.4 1.5 copy-done.2
  15.9 5.9 %shard_map.56.after_ref = bf16[256,1024]{1,0:T(8,128)(2,1)} custom-call(s32[1]{0:T(128)} %bitcast.5.ids_ref, bf16[256,3584]{1,0:T(8,128)(2,1)S(1)} %copy-done, bf16[3584,8192]{1,0:T(8,128)(2,1)} %weight_ref.7, bf16[8,64,1792]{2,1,0:T(8,128)(2,1)S(1)} %copy-done.2), custom_call_target="tpu_custom_call" | custom-call | flops 1879048192 | bytes 7340032 | tf_op jit(solution)/shard_map/pallas_call | solution.py:31
  21.9 1.4 shard_map.57
  23.2 1.6 %collective-permute-start.1 = (bf16[272,1792]{1,0:T(8,128)(2,1)}, bf16[272,1792]{1,0:T(8,128)(2,1)}, u32[]{:S(2)}, u32[]{:S(2)}) collective-permute-start(bf16[272,1792]{1,0:T(8,128)(2,1)} %get-tuple-element.18), channel_id=1, source_target_pairs={{0,16},{16,0},{1,17},{17,1},{2,18},{18,2},{3,19},{19,3},{4,20},{20... | collective-permute-start | bytes 2924552 | tf_op jit(solution)/shard_map/ppermute | solution.py:295
  24.8 2.0 %collective-permute-start.15 = (bf16[256,1024]{1,0:T(8,128)(2,1)}, bf16[256,1024]{1,0:T(8,128)(2,1)}, u32[]{:S(2)}, u32[]{:S(2)}) collective-permute-start(bf16[256,1024]{1,0:T(8,128)(2,1)} %shard_map.56.after_ref), channel_id=1, source_target_pairs={{0,2},{2,0},{4,6},{6,4},{8,10},{10,8},{12,14},{14,12},{1,3},{3,1},... | collective-permute-start | bytes 1572872 | tf_op jit(solution)/shard_map/ppermute | solution.py:328
  26.8 0.1 pad_add_fusion.1.ids_ref
  26.9 7.8 %shard_map.58 = (bf16[256,1024]{1,0:T(8,128)(2,1)S(1)}, bf16[256,1024]{1,0:T(8,128)(2,1)S(1)}) custom-call(s32[2]{0:T(128)S(1)} %pad_add_fusion.1.ids_ref, bf16[256,3584]{1,0:T(8,128)(2,1)S(1)} %copy-done, bf16[3584,8192]{1,0:T(8,128)(2,1)} %weight_ref.7, bf16[272,1792]{1,0:T(8,128)(2,1)S(1)} %get-tuple-element.17.after_ref.refs_0_), custom_call_target="tpu_custom_call" | custom-call | flops 3758096384 | bytes 14680064 | tf_op jit(solution)/shard_map/pallas_call | solution.py:31
  34.7 11.9 %collective-permute-done.1.refs_0_ = bf16[272,1792]{1,0:T(8,128)(2,1)} collective-permute-done((bf16[272,1792]{1,0:T(8,128)(2,1)}, bf16[272,1792]{1,0:T(8,128)(2,1)}, u32[]{:S(2)}, u32[]{:S(2)}) %collective-permute-start.1) | collective-permute-done | bytes 974880 | tf_op jit(solution)/shard_map/ppermute | solution.py:295
  46.7 5.1 %shard_map.59.after_ref = bf16[256,1024]{1,0:T(8,128)(2,1)S(1)} custom-call(s32[1]{0:T(128)} %bitcast.11.ids_ref, bf16[256,3584]{1,0:T(8,128)(2,1)S(1)} %copy-done, bf16[3584,8192]{1,0:T(8,128)(2,1)} %weight_ref.7, bf16[256,1024]{1,0:T(8,128)(2,1)S(1)} %get-tuple-element.19.after_ref), custom_call_target="tpu_custom_call" | custom-call | flops 1879048192 | bytes 7340032 | tf_op jit(solution)/shard_map/pallas_call | solution.py:31
  51.8 0.1 pad_add_fusion.ids_ref
  51.9 1.2 copy-done.4
  53.1 1.0 shard_map.60.after_ref
  54.2 13.7 %shard_map.61 = (f32[256,1024]{1,0:T(8,128)S(1)}, f32[256,1024]{1,0:T(8,128)S(1)}, f32[256,1024]{1,0:T(8,128)S(1)}, f32[256,1024]{1,0:T(8,128)S(1)}) custom-call(s32[4]{0:T(128)S(1)} %pad_add_fusion.ids_ref, bf16[256,3584]{1,0:T(8,128)(2,1)} %hidden_ref.9, bf16[3584,8192]{1,0:T(8,128)(2,1)} %weight_ref.7, bf16[8,64,512]{2,1,0:T(8,128)(2,1)} %shard_map.60.after_ref), custom_call_target="tpu_custom_call" | custom-call | flops 7516192768 | bytes 29360128 | tf_op jit(solution)/shard_map/pallas_call | solution.py:31
  67.9 1.0 copy-done.5
  68.9 1.0 copy-done.7
  69.9 1.0 copy-done.8
  70.9 3.2 %shard_map.62 = (f32[64,256]{1,0:T(8,128)S(1)}, f32[64,256]{1,0:T(8,128)S(1)}) custom-call(s32[1]{0:T(128)} %bitcast.1.g_ref, bf16[512,1792]{1,0:T(8,128)(2,1)} %bitcast.4.first_ref, bf16[272,1792]{1,0:T(8,128)(2,1)} %collective-permute-done.1.refs_0_, bf16[272,1792]{1,0:T(8,128)(2,1)} %collective-permute-done.2.refs_1_, ...), custom_call_target="tpu_custom_call" | custom-call | flops 939524096 | bytes 3670016 | tf_op jit(solution)/shard_map/pallas_call | solution.py:180
  74.1 1.6 %collective-permute-start.3 = (f32[2,64,256]{2,1,0:T(8,128)S(1)}, f32[2,64,256]{2,1,0:T(8,128)S(1)}, u32[]{:S(2)}, u32[]{:S(2)}) collective-permute-start(f32[2,64,256]{2,1,0:T(8,128)S(1)} %pad_maximum_fusion), channel_id=1, source_target_pairs={{0,16},{16,0},{1,17},{17,1},{2,18},{18,2},{3,19},{19,3},{4,20},{20... | collective-permute-start | bytes 393224 | tf_op jit(solution)/shard_map/ppermute | solution.py:316
  75.7 5.7 %all-to-all-start.1 = ((bf16[8,64,512]{2,1,0:T(8,128)(2,1)}), bf16[8,64,512]{2,1,0:T(8,128)(2,1)S(1)}, u32[]{:S(2)}, u32[]{:S(2)}) async-start(bf16[8,64,512]{2,1,0:T(8,128)(2,1)} %shard_map.60.after_ref), calls=%async_computation.1 | async-start | bytes 1048576 | tf_op jit(solution)/shard_map/all_to_all | solution.py:303
  81.4 2.0 %collective-permute-start.12 = (bf16[256,1024]{1,0:T(8,128)(2,1)}, bf16[256,1024]{1,0:T(8,128)(2,1)}, u32[]{:S(2)}, u32[]{:S(2)}) collective-permute-start(bf16[256,1024]{1,0:T(8,128)(2,1)} %copy-done.10), channel_id=1, source_target_pairs={{0,2},{2,0},{4,6},{6,4},{8,10},{10,8},{12,14},{14,12},{1,3},{3,1},... | collective-permute-start | bytes 1572872 | tf_op jit(solution)/shard_map/ppermute | solution.py:328
  83.5 0.1 collective-permute-start.14
  83.5 3.0 %shard_map.63 = (f32[64,256]{1,0:T(8,128)S(1)}, f32[64,256]{1,0:T(8,128)S(1)}) custom-call(s32[1]{0:T(128)} %bitcast.1.g_ref, bf16[512,1792]{1,0:T(8,128)(2,1)} %bitcast.4.first_ref, bf16[272,1792]{1,0:T(8,128)(2,1)S(1)} %get-tuple-element.17.after_ref.refs_0_, bf16[272,1792]{1,0:T(8,128)(2,1)} %collective-permute-done.refs_1_, ...), custom_call_target="tpu_custom_call" | custom-call | flops 939524096 | bytes 3670016 | tf_op jit(solution)/shard_map/pallas_call | solution.py:180
  86.5 0.1 collective-permute-start.4
  86.6 2.0 %add_convert_fusion.1 = bf16[256,1024]{1,0:T(8,128)(2,1)} fusion(f32[256,1024]{1,0:T(8,128)S(1)} %copy-done.9, bf16[256,1024]{1,0:T(8,128)(2,1)} %collective-permute-done.15), kind=kLoop, calls=%fused_computation.1 | loop fusion | flops 786432 | bytes 2097152 | tf_op jit(solution)/shard_map/convert_element_type | solution.py:328
  88.6 1.9 %collective-permute-start.16 = (bf16[256,1024]{1,0:T(8,128)(2,1)}, bf16[256,1024]{1,0:T(8,128)(2,1)}, u32[]{:S(2)}, u32[]{:S(2)}) collective-permute-start(bf16[256,1024]{1,0:T(8,128)(2,1)} %add_convert_fusion.1), channel_id=1, source_target_pairs={{0,4},{2,6},{4,0},{6,2},{8,12},{10,14},{12,8},{14,10},{1,5},{3,7},... | collective-permute-start | bytes 1572872 | tf_op jit(solution)/shard_map/ppermute | solution.py:328
  90.5 1.5 collective-permute-start.5
  92.1 0.6 collective-permute-start.11
  92.6 3.8 %all-to-all-done.1 = bf16[8,64,512]{2,1,0:T(8,128)(2,1)S(1)} async-done(((bf16[8,64,512]{2,1,0:T(8,128)(2,1)}), bf16[8,64,512]{2,1,0:T(8,128)(2,1)S(1)}, u32[]{:S(2)}, u32[]{:S(2)}) %all-to-all-start.1) | async-done | bytes 524320 | tf_op jit(solution)/shard_map/all_to_all | solution.py:303
  96.4 18.3 %collective-permute-done.5 = f32[64,256]{1,0:T(8,128)S(1)} collective-permute-done((f32[64,256]{1,0:T(8,128)S(1)}, f32[64,256]{1,0:T(8,128)S(1)}, u32[]{:S(2)}, u32[]{:S(2)}) %collective-permute-start.5) | collective-permute-done | bytes 65568 | tf_op jit(solution)/shard_map/ppermute | solution.py:320
  114.7 0.5 collective-permute-start.8
  115.2 1.5 collective-permute-start.6
  116.8 1.5 add_convert_fusion.2
  118.3 1.7 %collective-permute-done.6 = f32[64,256]{1,0:T(8,128)S(1)} collective-permute-done((f32[64,256]{1,0:T(8,128)S(1)}, f32[64,256]{1,0:T(8,128)S(1)}, u32[]{:S(2)}, u32[]{:S(2)}) %collective-permute-start.6) | collective-permute-done | bytes 65568 | tf_op jit(solution)/shard_map/ppermute | solution.py:320
  120.0 1.5 collective-permute-start.13
  121.5 0.1 collective-permute-start.9
  121.5 1.8 %collective-permute-start.7 = (f32[64,256]{1,0:T(8,128)S(1)}, f32[64,256]{1,0:T(8,128)S(1)}, u32[]{:S(2)}, u32[]{:S(2)}) collective-permute-start(f32[64,256]{1,0:T(8,128)S(1)} %add.38), channel_id=1, source_target_pairs={{0,8},{2,10},{4,12},{6,14},{8,0},{10,2},{12,4},{14,6},{1,9},{3,11}... | collective-permute-start | bytes 196616 | tf_op jit(solution)/shard_map/ppermute | solution.py:320
  123.4 1.4 add_convert_fusion
  124.8 1.8 %collective-permute-done.8.refs_1_ = bf16[512,512]{1,0:T(8,128)(2,1)S(1)} collective-permute-done((bf16[512,512]{1,0:T(8,128)(2,1)S(1)}, bf16[512,512]{1,0:T(8,128)(2,1)S(1)}, u32[]{:S(2)}, u32[]{:S(2)}) %collective-permute-start.8) | collective-permute-done | bytes 524320 | tf_op jit(solution)/shard_map/ppermute | solution.py:305
  126.7 3.0 %collective-permute-start.17 = (bf16[256,1024]{1,0:T(8,128)(2,1)S(1)}, bf16[256,1024]{1,0:T(8,128)(2,1)S(1)}, u32[]{:S(2)}, u32[]{:S(2)}) collective-permute-start(bf16[256,1024]{1,0:T(8,128)(2,1)S(1)} %add_convert_fusion), channel_id=1, source_target_pairs={{0,8},{2,10},{4,12},{6,14},{8,0},{10,2},{12,4},{14,6},{1,9},{3,11}... | collective-permute-start | bytes 1572872 | tf_op jit(solution)/shard_map/ppermute | solution.py:328
  129.6 4.4 %collective-permute-done.7 = f32[64,256]{1,0:T(8,128)S(1)} collective-permute-done((f32[64,256]{1,0:T(8,128)S(1)}, f32[64,256]{1,0:T(8,128)S(1)}, u32[]{:S(2)}, u32[]{:S(2)}) %collective-permute-start.7) | collective-permute-done | bytes 65568 | tf_op jit(solution)/shard_map/ppermute | solution.py:320
  134.1 2.0 %collective-permute-done.13.refs_6_ = bf16[256,1024]{1,0:T(8,128)(2,1)S(1)} collective-permute-done((bf16[256,1024]{1,0:T(8,128)(2,1)S(1)}, bf16[256,1024]{1,0:T(8,128)(2,1)S(1)}, u32[]{:S(2)}, u32[]{:S(2)}) %collective-permute-start.13) | collective-permute-done | bytes 524320 | tf_op jit(solution)/shard_map/ppermute | solution.py:328
  136.1 16.8 %collective-permute-done.17.refs_7_ = bf16[256,1024]{1,0:T(8,128)(2,1)S(1)} collective-permute-done((bf16[256,1024]{1,0:T(8,128)(2,1)S(1)}, bf16[256,1024]{1,0:T(8,128)(2,1)S(1)}, u32[]{:S(2)}, u32[]{:S(2)}) %collective-permute-start.17) | collective-permute-done | bytes 524320 | tf_op jit(solution)/shard_map/ppermute | solution.py:328
  152.9 2.6 %shard_map.64 = bf16[256,1024]{1,0:T(8,128)(2,1)} custom-call(s32[1]{0:T(128)} %bitcast.y_ref, s32[1]{0:T(128)} %bitcast.1.g_ref, f32[64,256]{1,0:T(8,128)S(1)} %fusion.3.latent_ref, s32[1,256]{1,0:T(1,128)S(1)} %bitcast.36, bf16[512,512]{1,0:T(8,128)(2,1)S(1)} %bitcast.32, bf16[512,512]{1,0:T(8,128)(2,1)S(1)} %collective-permute-done.8.refs_1_, ...), custom_call_target="tpu_custom_call" | custom-call | flops 536870912 | bytes 5242880 | tf_op jit(solution)/shard_map/pallas_call | solution.py:243
  (44 shorter events, 0.2 us)
Async XLA Ops:
  0.8 2.0 %copy-start.3 = (bf16[1,28672,64]{1,2,0:T(8,128)(2,1)S(1)}, bf16[1,28672,64]{1,2,0:T(8,128)(2,1)}, u32[]{:S(2)}) copy-start(bf16[1,28672,64]{1,2,0:T(8,128)(2,1)} %param.8) | copy-start | bytes 11010052
  5.7 1.2 copy-start.1
  6.9 7.4 %copy-start.11 = (s32[256,1]{0,1:T(1,128)S(1)}, s32[256,1]{0,1:T(1,128)}, u32[]{:S(2)}) copy-start(s32[256,1]{0,1:T(1,128)} %param.6) | copy-start | bytes 3076
  6.9 7.5 %copy-start = (bf16[256,3584]{1,0:T(8,128)(2,1)S(1)}, bf16[256,3584]{1,0:T(8,128)(2,1)}, u32[]{:S(2)}) copy-start(bf16[256,3584]{1,0:T(8,128)(2,1)} %hidden_ref.9) | copy-start | bytes 5505028
  6.9 64.0 %all-to-all-start = ((bf16[8,64,1792]{2,1,0:T(8,128)(2,1)}), bf16[8,64,1792]{2,1,0:T(8,128)(2,1)}, u32[]{:S(2)}, u32[]{:S(2)}) async-start(bf16[8,64,1792]{2,1,0:T(8,128)(2,1)} %copy-done.1), calls=%async_computation | async-start | bytes 3670016 | tf_op jit(solution)/shard_map/all_to_all | solution.py:275
  14.4 1.5 copy-start.2
  23.2 23.4 %collective-permute-start.1 = (bf16[272,1792]{1,0:T(8,128)(2,1)}, bf16[272,1792]{1,0:T(8,128)(2,1)}, u32[]{:S(2)}, u32[]{:S(2)}) collective-permute-start(bf16[272,1792]{1,0:T(8,128)(2,1)} %get-tuple-element.18), channel_id=1, source_target_pairs={{0,16},{16,0},{1,17},{17,1},{2,18},{18,2},{3,19},{19,3},{4,20},{20... | collective-permute-start | bytes 2924552 | tf_op jit(solution)/shard_map/ppermute | solution.py:295
  24.8 61.8 %collective-permute-start.15 = (bf16[256,1024]{1,0:T(8,128)(2,1)}, bf16[256,1024]{1,0:T(8,128)(2,1)}, u32[]{:S(2)}, u32[]{:S(2)}) collective-permute-start(bf16[256,1024]{1,0:T(8,128)(2,1)} %shard_map.56.after_ref), channel_id=1, source_target_pairs={{0,2},{2,0},{4,6},{6,4},{8,10},{10,8},{12,14},{14,12},{1,3},{3,1},... | collective-permute-start | bytes 1572872 | tf_op jit(solution)/shard_map/ppermute | solution.py:328
  26.8 56.7 %collective-permute-start = (bf16[272,1792]{1,0:T(8,128)(2,1)S(1)}, bf16[272,1792]{1,0:T(8,128)(2,1)}, u32[]{:S(2)}, u32[]{:S(2)}) collective-permute-start(bf16[272,1792]{1,0:T(8,128)(2,1)S(1)} %get-tuple-element.17.after_ref.refs_0_), channel_id=1, source_target_pairs={{0,1},{1,0},{2,3},{3,2},{4,5},{5,4},{6,7},{7,6},{8,9},{9,8},{10,11... | collective-permute-start | bytes 2924552 | tf_op jit(solution)/shard_map/ppermute | solution.py:296
  34.7 17.1 %copy-start.10 = (bf16[256,1024]{1,0:T(8,128)(2,1)}, bf16[256,1024]{1,0:T(8,128)(2,1)S(1)}, u32[]{:S(2)}) copy-start(bf16[256,1024]{1,0:T(8,128)(2,1)S(1)} %get-tuple-element.19.after_ref) | copy-start | bytes 1572868
  34.7 17.1 %copy-start.12 = (bf16[256,1024]{1,0:T(8,128)(2,1)}, bf16[256,1024]{1,0:T(8,128)(2,1)S(1)}, u32[]{:S(2)}) copy-start(bf16[256,1024]{1,0:T(8,128)(2,1)S(1)} %get-tuple-element.27) | copy-start | bytes 1572868
  46.6 24.3 %collective-permute-start.2 = (bf16[272,1792]{1,0:T(8,128)(2,1)}, bf16[272,1792]{1,0:T(8,128)(2,1)}, u32[]{:S(2)}, u32[]{:S(2)}) collective-permute-start(bf16[272,1792]{1,0:T(8,128)(2,1)} %collective-permute-done.1.refs_0_), channel_id=1, source_target_pairs={{0,1},{1,0},{2,3},{3,2},{4,5},{5,4},{6,7},{7,6},{8,9},{9,8},{10,11... | collective-permute-start | bytes 2924552 | tf_op jit(solution)/shard_map/ppermute | solution.py:313
  51.9 1.2 copy-start.4
  67.9 1.0 copy-start.5
  68.9 1.0 copy-start.7
  69.9 1.0 copy-start.8
  74.1 12.4 %collective-permute-start.3 = (f32[2,64,256]{2,1,0:T(8,128)S(1)}, f32[2,64,256]{2,1,0:T(8,128)S(1)}, u32[]{:S(2)}, u32[]{:S(2)}) collective-permute-start(f32[2,64,256]{2,1,0:T(8,128)S(1)} %pad_maximum_fusion), channel_id=1, source_target_pairs={{0,16},{16,0},{1,17},{17,1},{2,18},{18,2},{3,19},{19,3},{4,20},{20... | collective-permute-start | bytes 393224 | tf_op jit(solution)/shard_map/ppermute | solution.py:316
  75.7 20.7 %all-to-all-start.1 = ((bf16[8,64,512]{2,1,0:T(8,128)(2,1)}), bf16[8,64,512]{2,1,0:T(8,128)(2,1)S(1)}, u32[]{:S(2)}, u32[]{:S(2)}) async-start(bf16[8,64,512]{2,1,0:T(8,128)(2,1)} %shard_map.60.after_ref), calls=%async_computation.1 | async-start | bytes 1048576 | tf_op jit(solution)/shard_map/all_to_all | solution.py:303
  81.4 33.8 %collective-permute-start.12 = (bf16[256,1024]{1,0:T(8,128)(2,1)}, bf16[256,1024]{1,0:T(8,128)(2,1)}, u32[]{:S(2)}, u32[]{:S(2)}) collective-permute-start(bf16[256,1024]{1,0:T(8,128)(2,1)} %copy-done.10), channel_id=1, source_target_pairs={{0,2},{2,0},{4,6},{6,4},{8,10},{10,8},{12,14},{14,12},{1,3},{3,1},... | collective-permute-start | bytes 1572872 | tf_op jit(solution)/shard_map/ppermute | solution.py:328
  83.5 3.2 %copy-start.9 = (f32[256,1024]{1,0:T(8,128)S(1)}, f32[256,1024]{1,0:T(8,128)}, u32[]{:S(2)}) copy-start(f32[256,1024]{1,0:T(8,128)} %copy-done.8) | copy-start | bytes 3145732
  83.5 38.0 %collective-permute-start.14 = (bf16[256,1024]{1,0:T(8,128)(2,1)}, bf16[256,1024]{1,0:T(8,128)(2,1)}, u32[]{:S(2)}, u32[]{:S(2)}) collective-permute-start(bf16[256,1024]{1,0:T(8,128)(2,1)} %copy-done.12), channel_id=1, source_target_pairs={{0,2},{2,0},{4,6},{6,4},{8,10},{10,8},{12,14},{14,12},{1,3},{3,1},... | collective-permute-start | bytes 1572872 | tf_op jit(solution)/shard_map/ppermute | solution.py:328
  86.5 4.0 %collective-permute-start.4 = (f32[64,256]{1,0:T(8,128)S(1)}, f32[64,256]{1,0:T(8,128)S(1)}, u32[]{:S(2)}, u32[]{:S(2)}) collective-permute-start(f32[64,256]{1,0:T(8,128)S(1)} %fusion), channel_id=1, source_target_pairs={{0,1},{1,0},{2,3},{3,2},{4,5},{5,4},{6,7},{7,6},{8,9},{9,8},{10,11... | collective-permute-start | bytes 196616 | tf_op jit(solution)/shard_map/ppermute | solution.py:317
  88.6 34.7 %copy-start.6 = (f32[256,1024]{1,0:T(8,128)S(1)}, f32[256,1024]{1,0:T(8,128)}, u32[]{:S(2)}) copy-start(f32[256,1024]{1,0:T(8,128)} %copy-done.5) | copy-start | bytes 3145732
  88.6 32.9 %collective-permute-start.16 = (bf16[256,1024]{1,0:T(8,128)(2,1)}, bf16[256,1024]{1,0:T(8,128)(2,1)}, u32[]{:S(2)}, u32[]{:S(2)}) collective-permute-start(bf16[256,1024]{1,0:T(8,128)(2,1)} %add_convert_fusion.1), channel_id=1, source_target_pairs={{0,4},{2,6},{4,0},{6,2},{8,12},{10,14},{12,8},{14,10},{1,5},{3,7},... | collective-permute-start | bytes 1572872 | tf_op jit(solution)/shard_map/ppermute | solution.py:328
  90.5 24.2 %collective-permute-start.5 = (f32[64,256]{1,0:T(8,128)S(1)}, f32[64,256]{1,0:T(8,128)S(1)}, u32[]{:S(2)}, u32[]{:S(2)}) collective-permute-start(f32[64,256]{1,0:T(8,128)S(1)} %fusion.2), channel_id=1, source_target_pairs={{0,2},{2,0},{4,6},{6,4},{8,10},{10,8},{12,14},{14,12},{1,3},{3,1},... | collective-permute-start | bytes 196616 | tf_op jit(solution)/shard_map/ppermute | solution.py:320
  92.1 42.0 %collective-permute-start.11 = (bf16[256,1024]{1,0:T(8,128)(2,1)S(1)}, bf16[256,1024]{1,0:T(8,128)(2,1)}, u32[]{:S(2)}, u32[]{:S(2)}) collective-permute-start(bf16[256,1024]{1,0:T(8,128)(2,1)S(1)} %shard_map.59.after_ref), channel_id=1, source_target_pairs={{0,2},{2,0},{4,6},{6,4},{8,10},{10,8},{12,14},{14,12},{1,3},{3,1},... | collective-permute-start | bytes 1572872 | tf_op jit(solution)/shard_map/ppermute | solution.py:328
  114.7 12.0 %collective-permute-start.8 = (bf16[512,512]{1,0:T(8,128)(2,1)S(1)}, bf16[512,512]{1,0:T(8,128)(2,1)S(1)}, u32[]{:S(2)}, u32[]{:S(2)}) collective-permute-start(bf16[512,512]{1,0:T(8,128)(2,1)S(1)} %bitcast.30), channel_id=1, source_target_pairs={{0,16},{16,0},{1,17},{17,1},{2,18},{18,2},{3,19},{19,3},{4,20},{20... | collective-permute-start | bytes 1572872 | tf_op jit(solution)/shard_map/ppermute | solution.py:305
  115.2 4.7 %collective-permute-start.6 = (f32[64,256]{1,0:T(8,128)S(1)}, f32[64,256]{1,0:T(8,128)S(1)}, u32[]{:S(2)}, u32[]{:S(2)}) collective-permute-start(f32[64,256]{1,0:T(8,128)S(1)} %add.37), channel_id=1, source_target_pairs={{0,4},{2,6},{4,0},{6,2},{8,12},{10,14},{12,8},{14,10},{1,5},{3,7},... | collective-permute-start | bytes 196616 | tf_op jit(solution)/shard_map/ppermute | solution.py:320
  120.0 16.2 %collective-permute-start.13 = (bf16[256,1024]{1,0:T(8,128)(2,1)S(1)}, bf16[256,1024]{1,0:T(8,128)(2,1)S(1)}, u32[]{:S(2)}, u32[]{:S(2)}) collective-permute-start(bf16[256,1024]{1,0:T(8,128)(2,1)S(1)} %add_convert_fusion.2), channel_id=1, source_target_pairs={{0,4},{2,6},{4,0},{6,2},{8,12},{10,14},{12,8},{14,10},{1,5},{3,7},... | collective-permute-start | bytes 1572872 | tf_op jit(solution)/shard_map/ppermute | solution.py:328
  121.5 14.7 %collective-permute-start.9 = (bf16[512,512]{1,0:T(8,128)(2,1)S(1)}, bf16[512,512]{1,0:T(8,128)(2,1)S(1)}, u32[]{:S(2)}, u32[]{:S(2)}) collective-permute-start(bf16[512,512]{1,0:T(8,128)(2,1)S(1)} %bitcast.31), channel_id=1, source_target_pairs={{0,1},{1,0},{2,3},{3,2},{4,5},{5,4},{6,7},{7,6},{8,9},{9,8},{10,11... | collective-permute-start | bytes 1572872 | tf_op jit(solution)/shard_map/ppermute | solution.py:309
  121.5 12.5 %collective-permute-start.7 = (f32[64,256]{1,0:T(8,128)S(1)}, f32[64,256]{1,0:T(8,128)S(1)}, u32[]{:S(2)}, u32[]{:S(2)}) collective-permute-start(f32[64,256]{1,0:T(8,128)S(1)} %add.38), channel_id=1, source_target_pairs={{0,8},{2,10},{4,12},{6,14},{8,0},{10,2},{12,4},{14,6},{1,9},{3,11}... | collective-permute-start | bytes 196616 | tf_op jit(solution)/shard_map/ppermute | solution.py:320
  126.7 26.3 %collective-permute-start.17 = (bf16[256,1024]{1,0:T(8,128)(2,1)S(1)}, bf16[256,1024]{1,0:T(8,128)(2,1)S(1)}, u32[]{:S(2)}, u32[]{:S(2)}) collective-permute-start(bf16[256,1024]{1,0:T(8,128)(2,1)S(1)} %add_convert_fusion), channel_id=1, source_target_pairs={{0,8},{2,10},{4,12},{6,14},{8,0},{10,2},{12,4},{14,6},{1,9},{3,11}... | collective-permute-start | bytes 1572872 | tf_op jit(solution)/shard_map/ppermute | solution.py:328
  134.1 18.9 %collective-permute-start.10 = (bf16[512,512]{1,0:T(8,128)(2,1)S(1)}, bf16[512,512]{1,0:T(8,128)(2,1)S(1)}, u32[]{:S(2)}, u32[]{:S(2)}) collective-permute-start(bf16[512,512]{1,0:T(8,128)(2,1)S(1)} %collective-permute-done.8.refs_1_), channel_id=1, source_target_pairs={{0,1},{1,0},{2,3},{3,2},{4,5},{5,4},{6,7},{7,6},{8,9},{9,8},{10,11... | collective-permute-start | bytes 1572872 | tf_op jit(solution)/shard_map/ppermute | solution.py:310

commit v3 on v2

v3 whole, which is shorter than its diff:
```python
import jax
import jax.numpy as jnp
from jax import lax
from jax.experimental import pallas as pl
from jax.experimental.pallas import tpu as pltpu
from jax.sharding import PartitionSpec as P

SWAP = ((0, 1), (1, 0))
ANY = pl.BlockSpec(memory_space=pl.ANY)
VMEM = pl.BlockSpec(memory_space=pltpu.VMEM)
SMEM = pl.BlockSpec(memory_space=pltpu.SMEM)
TAG_ROWS = 16
COST = pl.CostEstimate(flops=1, bytes_accessed=1, transcendentals=0)
PARAMS = pltpu.CompilerParams(vmem_limit_bytes=64 * 2**20)


class Order:
    def __init__(self, array):
        self.last = array


def relay(array, order):
    def kernel(array_ref, after_ref, out_ref):
        del array_ref, after_ref, out_ref

    out = pl.pallas_call(
        kernel,
        out_shape=jax.ShapeDtypeStruct(array.shape, array.dtype),
        in_specs=[ANY, ANY],
        out_specs=ANY,
        input_output_aliases={0: 0},
        compiler_params=PARAMS,
        cost_estimate=COST,
    )(array, order.last)
    order.last = out
    return out


def block_products(hidden, weight, sent_ids, kept_ids, columns, order):
    rows, depth = hidden.shape
    sent, kept = len(sent_ids), len(kept_ids)

    def kernel(ids_ref, hidden_ref, weight_ref, after_ref, *out_refs):
        product = jnp.dot(hidden_ref[...], weight_ref[...], preferred_element_type=jnp.float32)
        if sent:

            @pl.when(pl.program_id(0) < sent)
            def _():
                out_refs[0][0] = product.astype(jnp.bfloat16)

        if kept:

            @pl.when(pl.program_id(0) >= sent)
            def _():
                out_refs[-1][0] = product

    out_shape, out_specs = [], []
    if sent:
        out_shape.append(jax.ShapeDtypeStruct((sent, rows, columns), jnp.bfloat16))
        out_specs.append(
            pl.BlockSpec((1, rows, columns), lambda b, ids: (jnp.minimum(b, sent - 1), 0, 0))
        )
    if kept:
        out_shape.append(jax.ShapeDtypeStruct((kept, rows, columns), jnp.float32))
        out_specs.append(
            pl.BlockSpec((1, rows, columns), lambda b, ids: (jnp.maximum(b - sent, 0), 0, 0))
        )
    outs = pl.pallas_call(
        kernel,
        out_shape=out_shape,
        grid_spec=pltpu.PrefetchScalarGridSpec(
            num_scalar_prefetch=1,
            grid=(sent + kept,),
            in_specs=[
                pl.BlockSpec((rows, depth), lambda b, ids: (0, 0)),
                pl.BlockSpec((depth, columns), lambda b, ids: (0, ids[b])),
                ANY,
            ],
            out_specs=out_specs,
        ),
        compiler_params=PARAMS,
        cost_estimate=COST,
    )(jnp.stack(sent_ids + kept_ids), hidden, weight, order.last)
    order.last = outs[-1]
    return outs


def pack_factors(first, second, tp, y):
    rank = first.shape[0]
    widths = [first.shape[1] // (2 * tp), second.shape[1] // (2 * tp)]
    if widths[0] % 128 or widths[1] % 128:
        parts = [
            lax.dynamic_index_in_dim(
                source.reshape(rank, tp, 2, width), y, 2, keepdims=False
            ).transpose(1, 0, 2)
            for source, width in zip((first, second), widths)
        ]
        return jnp.concatenate(parts, axis=2)
    places = [pl.ds(0, widths[0]), pl.ds(widths[0], widths[1])]

    def kernel(y_ref, first_ref, second_ref, out_ref, buffer, in_sem, out_sem):
        def fetch(i, which):
            width = widths[which]
            start = pl.multiple_of((2 * i + y_ref[0]) * width, 128)
            return pltpu.make_async_copy(
                (first_ref, second_ref)[which].at[:, pl.ds(start, width)],
                buffer.at[i, :, places[which]],
                in_sem.at[i, which],
            )

        def store(i):
            return pltpu.make_async_copy(buffer.at[i], out_ref.at[i], out_sem.at[i])

        for i in range(tp):
            for which in range(2):
                fetch(i, which).start()
        for i in range(tp):
            for which in range(2):
                fetch(i, which).wait()
            store(i).start()
        for i in range(tp):
            store(i).wait()

    shape = (tp, rank, sum(widths))
    return pl.pallas_call(
        kernel,
        out_shape=jax.ShapeDtypeStruct(shape, first.dtype),
        in_specs=[SMEM, ANY, ANY],
        out_specs=ANY,
        scratch_shapes=[
            pltpu.VMEM(shape, first.dtype),
            pltpu.SemaphoreType.DMA((tp, 2)),
            pltpu.SemaphoreType.DMA((tp,)),
        ],
        compiler_params=PARAMS,
        cost_estimate=COST,
    )(y.reshape(1), first, second)


def pack_hidden(hidden, tags, half, y, order):
    rows = hidden.shape[0]
    if half % 128 or half < rows:
        return [
            jnp.concatenate(
                [lax.dynamic_slice(hidden, (0, which * half), (rows, half)), tags], axis=0
            )
            for which in (y, 1 - y)
        ]
    chunks = 4
    step = rows // chunks

    def kernel(y_ref, hidden_ref, tags_ref, after_ref, mine_ref, other_ref, buffer, in_sem, out_sem):
        def fetch(which, i):
            half_index = y_ref[0] if which == 0 else 1 - y_ref[0]
            return pltpu.make_async_copy(
                hidden_ref.at[
                    pl.ds(i * step, step), pl.ds(pl.multiple_of(half_index * half, 128), half)
                ],
                buffer.at[which, pl.ds(i * step, step)],
                in_sem.at[which, i],
            )

        def store(which):
            out_ref = (mine_ref, other_ref)[which]
            return pltpu.make_async_copy(buffer.at[which], out_ref, out_sem.at[which])

        for which in (1, 0):
            for i in range(chunks):
                fetch(which, i).start()
        for which in (1, 0):
            buffer[which, rows:] = tags_ref[...]
        for which in (1, 0):
            for i in range(chunks):
                fetch(which, i).wait()
            store(which).start()
        for which in (1, 0):
            store(which).wait()

    shape = jax.ShapeDtypeStruct((rows + TAG_ROWS, half), hidden.dtype)
    mine, other = pl.pallas_call(
        kernel,
        out_shape=[shape, shape],
        in_specs=[SMEM, ANY, VMEM, ANY],
        out_specs=[ANY, ANY],
        scratch_shapes=[
            pltpu.VMEM((2, rows + TAG_ROWS, half), hidden.dtype),
            pltpu.SemaphoreType.DMA((2, chunks)),
            pltpu.SemaphoreType.DMA((2,)),
        ],
        compiler_params=PARAMS,
        cost_estimate=COST,
    )(y.reshape(1), hidden, tags, order.last)
    order.last = mine
    return mine, other


def latent_terms(factors, half, blocks, rows, rank, g, with_second, order):
    count = factors.shape[0]
    tp = count // rank

    def term(factor, rows_held, adapter, core):
        full = lax.dot_general(
            factor, rows_held, (((1,), (1,)), ((), ())), preferred_element_type=jnp.float32
        )
        total = jnp.zeros((rank, rows), jnp.float32)
        for place in range(tp):
            total += jnp.where(
                adapter == place * 2 + core, full[place * rank : (place + 1) * rank], 0.0
            )
        return total

    if half % 128 or half < rows:
        outs = [
            term(
                factors[:, :half],
                block[:rows],
                block[rows:].reshape(-1)[:rows][None].astype(jnp.int32),
                g,
            )
            for block in blocks
        ]
        return [jnp.stack(outs)] + [factors[:, half:]] * with_second

    def kernel(g_ref, factors_ref, *refs):
        block_refs, out_refs = refs[: len(blocks)], refs[len(blocks) + 1 :]
        for i, block_ref in enumerate(block_refs):
            tag = block_ref[rows:, :rows].astype(jnp.float32)[0:1].astype(jnp.int32)
            out_refs[0][i] = term(factors_ref[:, :half], block_ref[:rows, :], tag, g_ref[0])
        if with_second:
            out_refs[-1][...] = factors_ref[:, half:]

    out_shape = [jax.ShapeDtypeStruct((len(blocks), rank, rows), jnp.float32)]
    if with_second:
        out_shape.append(jax.ShapeDtypeStruct((count, factors.shape[1] - half), factors.dtype))
    outs = pl.pallas_call(
        kernel,
        out_shape=out_shape,
        in_specs=[SMEM, VMEM] + [VMEM] * len(blocks) + [ANY],
        out_specs=[VMEM] * len(out_shape),
        compiler_params=PARAMS,
        cost_estimate=COST,
    )(g.reshape(1), factors, *blocks, order.last)
    order.last = outs[0]
    return outs


def block_specs(blocks):
    return [
        pl.BlockSpec((1, *array.shape[1:]), lambda b, i=i: (i, 0, 0)) for array, i in blocks
    ]


def add(pairs, order):
    blocks = [block for pair in pairs for block in pair]
    shape = blocks[0][0].shape[1:]

    def kernel(*refs):
        outs = refs[len(blocks) + 1 :]
        for i, out_ref in enumerate(outs):
            out_ref[...] = refs[2 * i][...] + refs[2 * i + 1][...]

    outs = pl.pallas_call(
        kernel,
        grid=(1,),
        out_shape=[jax.ShapeDtypeStruct((1, *shape), jnp.float32)] * len(pairs),
        in_specs=block_specs(blocks) + [ANY],
        out_specs=[pl.BlockSpec((1, *shape), lambda b: (0, 0, 0))] * len(pairs),
        compiler_params=PARAMS,
        cost_estimate=COST,
    )(*[array for array, _ in blocks], order.last)
    order.last = outs[0]
    return outs


def fold(blocks, dtype, order):
    shape = blocks[0][0].shape[1:]

    def kernel(*refs):
        total = refs[0][0]
        for ref in refs[1 : len(blocks)]:
            total += ref[0].astype(jnp.float32)
        refs[-1][0] = total.astype(dtype)

    out = pl.pallas_call(
        kernel,
        grid=(1,),
        out_shape=jax.ShapeDtypeStruct((1, *shape), dtype),
        in_specs=block_specs(blocks) + [ANY],
        out_specs=pl.BlockSpec((1, *shape), lambda b: (0, 0, 0)),
        compiler_params=PARAMS,
        cost_estimate=COST,
    )(*[array for array, _ in blocks], order.last)
    order.last = out
    return out


def finish(latents, adapter, seconds, blocks, y, g):
    rows, columns = blocks[0][0].shape[1:]
    rank = latents[0].shape[1]
    tp = seconds[0].shape[0] // rank
    half = columns // 2

    def spread(held, ids, core):
        zero = jnp.zeros_like(held)
        return jnp.concatenate(
            [jnp.where(ids == place * 2 + core, held, zero) for place in range(tp)], axis=0
        ).astype(jnp.bfloat16)

    def product(left, right):
        return lax.dot_general(
            left, right, (((0,), (0,)), ((), ())), preferred_element_type=jnp.float32
        )

    if half % 128:
        latent = (latents[0][0] + latents[1][0]).astype(jnp.bfloat16).astype(jnp.float32)
        near, far = spread(latent, adapter, g), spread(latent, adapter, 1 - g)
        mine = product(near, seconds[0]) + product(far, seconds[2])
        other = product(near, seconds[1]) + product(far, seconds[3])
        delta = jnp.where(
            y == 0,
            jnp.concatenate([mine, other], axis=1),
            jnp.concatenate([other, mine], axis=1),
        )
        total = delta.astype(jnp.bfloat16).astype(jnp.float32)
        for array, i in blocks:
            total = total + array[i].astype(jnp.float32)
        return total.astype(jnp.bfloat16)

    def kernel(y_ref, g_ref, a_ref, b_ref, adapter_ref, *refs):
        second_refs, block_refs, out_ref = refs[:4], refs[4:-1], refs[-1]
        latent = (a_ref[0] + b_ref[0]).astype(jnp.bfloat16).astype(jnp.float32)
        near = spread(latent, adapter_ref[...], g_ref[0])
        far = spread(latent, adapter_ref[...], 1 - g_ref[0])
        for which in range(2):
            index = y_ref[0] if which == 0 else 1 - y_ref[0]
            lanes = pl.ds(pl.multiple_of(index * half, 128), half)
            delta = product(near, second_refs[which][...])
            delta += product(far, second_refs[2 + which][...])
            total = block_refs[0][0, :, lanes]
            for block_ref in block_refs[1:]:
                total += block_ref[0, :, lanes].astype(jnp.float32)
            total += delta.astype(jnp.bfloat16).astype(jnp.float32)
            out_ref[:, lanes] = total.astype(jnp.bfloat16)

    whole = lambda array: pl.BlockSpec(array.shape, lambda b: (0,) * array.ndim)
    return pl.pallas_call(
        kernel,
        grid=(1,),
        out_shape=jax.ShapeDtypeStruct((rows, columns), jnp.bfloat16),
        in_specs=[SMEM, SMEM]
        + [whole(array) for array in (*latents, adapter, *seconds)]
        + block_specs(blocks),
        out_specs=pl.BlockSpec((rows, columns), lambda b: (0, 0)),
        compiler_params=PARAMS,
        cost_estimate=COST,
    )(y.reshape(1), g.reshape(1), *latents, adapter, *seconds, *[array for array, _ in blocks])


def local(
    hidden, row_adapter_index, down_projection_weight, adapter_first_factor, adapter_second_factor
):
    tp = lax.axis_size("tp")
    t = lax.axis_index("tp")
    y = lax.axis_index("rep")
    g = lax.axis_index("grp")
    rows, depth = hidden.shape
    rank = adapter_first_factor.shape[2]
    columns = down_projection_weight.shape[1] // tp
    half = depth // 2
    adapter = row_adapter_index.T

    def across(array, step):
        return lax.ppermute(array, "tp", [(i, i ^ step) for i in range(tp)])

    factors = pack_factors(adapter_first_factor[0].T, adapter_second_factor[0], tp, y)
    order = Order(factors)
    factors = lax.all_to_all(factors, "tp", split_axis=0, concat_axis=0, tiled=True)
    factors = factors.reshape(tp * rank, factors.shape[2])

    terms = {j: [] for j in range(0, tp, 2)}

    def multiply(sent, kept):
        outs = block_products(
            hidden,
            down_projection_weight,
            [t ^ j for j in sent],
            [t ^ j for j in kept],
            columns,
            order,
        )
        for i, j in enumerate(kept):
            terms[j].insert(0, (outs[-1], i))
        if sent:
            got = across(outs[0], 1)
            for i, j in enumerate(sent):
                terms[j ^ 1].append((got, i))

    def pass_on(step, j):
        terms[j ^ step].append((across(fold(terms[j], jnp.bfloat16, order), step), 0))

    odd = list(range(tp - 1, 0, -2))
    even = [j - 1 for j in odd]
    stages = []
    step = 2
    while step < tp:
        stages.append([(step, j) for j in range(tp - step, 0, -2 * step)])
        step *= 2
    multiply(odd[:1], [])

    tag_lanes = jnp.pad(adapter[0], (0, -rows % half if rows > half else half - rows))
    tags = tag_lanes.astype(jnp.bfloat16).reshape(-1, half)
    tags = jnp.pad(tags, ((0, TAG_ROWS - tags.shape[0]), (0, 0)))
    mine, other = pack_hidden(hidden, tags, half, y, order)
    from_rep = lax.ppermute(other, "rep", SWAP)
    from_grp = lax.ppermute(mine, "grp", SWAP)

    multiply(odd[1:3], [])
    multiply(odd[3:], even[:1])
    from_rep = relay(from_rep, order)
    from_both = lax.ppermute(from_rep, "grp", SWAP)
    pass_on(*stages[0][0])
    multiply([], even[1:])
    for item in stages[0][1:]:
        pass_on(*item)

    away = latent_terms(factors, half, [from_rep, from_both], rows, rank, g, False, order)[0]
    got = lax.ppermute(away, "rep", SWAP)
    near, second = latent_terms(
        factors, half, [mine, from_grp], rows, rank, g, True, order
    )
    second_other = lax.ppermute(second, "rep", SWAP)
    early = list(terms[0])
    for stage in stages[1:]:
        for item in stage:
            pass_on(*item)
    terms[0] = [(fold(early, jnp.float32, order), 0)] + terms[0][len(early) :]
    here, there = add([((near, i), (got, i)) for i in range(2)], order)
    latents = [here, lax.ppermute(there, "grp", SWAP)]
    step = 1
    while step < tp:
        latent = add([[(array, 0) for array in latents]], order)[0]
        latents = [latent, across(latent, step)]
        step *= 2
    second_other = relay(second_other, order)
    seconds = [
        second,
        second_other,
        lax.ppermute(second, "grp", SWAP),
        lax.ppermute(second_other, "grp", SWAP),
    ]
    return finish(latents, adapter, seconds, terms[0], y, g)


def solution(mesh):
    return jax.shard_map(
        local,
        mesh=mesh,
        in_specs=(
            P(("rep", "grp"), "tp"),
            P(("rep", "grp"), None),
            P("tp", None),
            P(("tp", "grp"), None, None),
            P(("tp", "grp"), None, None),
        ),
        out_specs=P(("rep", "grp"), "tp"),
        check_vma=False,
    )
```

time: 156 us -> 169 us (1.083)
  Pallas kernels: 46.7 us -> 72.5 us
  local copies, waits for them, and re-layouts: 9.78 us -> 0.64 us
  starting transfers between devices: 32.8 us -> 24.9 us
  waiting for transfers between devices: 60.8 us -> 67.2 us
  other arithmetic: 5.17 us -> 2.59 us
    pallas_call x10 -> x19, Pallas kernels: 46.7 us -> 72.5 us  [the longest x4 38.9 us: block_products(): pl.pallas_call(kernel, out_shape=out_shape, grid_spec=pltpu.PrefetchScala...]
    ppermute x12 -> x11, waiting for transfers between devices: 43.3 us -> 67.2 us  [the longest x9 57.6 us: across(): return lax.ppermute(array, 'tp', [(i, i ^ step) for i in range(tp)])]
    ppermute x1, waiting for transfers between devices: 11.9 us -> 0.01 us  [local(): from_rep = lax.ppermute(other, 'rep', SWAP)]
    unnamed x27 -> x0, local copies, waits for them, and re-layouts: 9.75 us -> none
    all_to_all x2 -> x1, starting transfers between devices: 13.1 us -> 7.26 us  [local(): lax.all_to_all(factors, 'tp', split_axis=0, concat_axis=0, tiled=True)]
    convert_element_type x4 -> x0, other arithmetic: 4.94 us -> none  [the longest x3 4.93 us: local(): sent = lax.ppermute(part[j].astype(jnp.bfloat16), 'tp', across(step))]
    all_to_all x2 -> x1, waiting for transfers between devices: 3.78 us -> 0.01 us  [local(): lax.all_to_all(factors, 'tp', split_axis=0, concat_axis=0, tiled=True)]
    ppermute x12 -> x11, starting transfers between devices: 17.5 us -> 15 us  [the longest x9 13.5 us: across(): return lax.ppermute(array, 'tp', [(i, i ^ step) for i in range(tp)])]
  transfers between devices with their start and end apart: 20 -> 18, of which waited for: 8 -> 6; matrix products, arithmetic and copies ran while one was open for 3% -> 2% of each run, Pallas kernels for 26% -> 39%
where the time goes in v3:
time: 169 us; the launch traced here: 168 us
  Pallas kernels  72.5 us (43%)
  waiting for transfers between devices  67.2 us (40%)
  starting transfers between devices  24.9 us (15%)
  other arithmetic  2.59 us (2%)
    ppermute x9, waiting for transfers between devices, across(): return lax.ppermute(array, 'tp', [(i, i ^ step) for i in range(tp)])  57.6 us
    pallas_call x4, Pallas kernels, block_products(): pl.pallas_call(kernel, out_shape=out_shape, grid_spec=pltpu.PrefetchScala...  38.9 us
    ppermute x9, starting transfers between devices, across(): return lax.ppermute(array, 'tp', [(i, i ^ step) for i in range(tp)])  13.5 us
    pallas_call x4, Pallas kernels, fold(): pl.pallas_call(kernel, grid=(1,), out_shape=jax.ShapeDtypeStruct((1, *sha...  9.59 us
    pallas_call x2, Pallas kernels, latent_terms(): pl.pallas_call(kernel, out_shape=out_shape, in_specs=[SMEM, VMEM] + [VMEM...  8.19 us
    ppermute x1, waiting for transfers between devices, local(): got = lax.ppermute(away, 'rep', SWAP)  8.01 us
    all_to_all x1, starting transfers between devices, local(): lax.all_to_all(factors, 'tp', split_axis=0, concat_axis=0, tiled=True)  7.26 us
    pallas_call x4, Pallas kernels, add(): pl.pallas_call(kernel, grid=(1,), out_shape=[jax.ShapeDtypeStruct((1, *sh...  6.09 us
  transfers between devices with their start and end apart: 18, of which 6 were waited for; matrix products, arithmetic and copies ran while one was open for 2% of the time, Pallas kernels for 39%

profile of v3, /device:TPU:0, one launch (start us, length us, event | category | flops | bytes accessed | tf_op | source)
XLA Modules:
  0.0 167.8 jit_solution(2728123008885904942)
XLA Ops:
  0.0 2.6 %shard_map.55.after_ref = bf16[8,64,2304]{2,1,0:T(8,128)(2,1)} custom-call(s32[1]{0:T(128)} %bitcast.y_ref, bf16[64,28672]{1,0:T(8,128)(2,1)} %bitcast.16, bf16[64,8192]{1,0:T(8,128)(2,1)} %bitcast.17), custom_call_target="tpu_custom_call" | custom-call | flops 1 | bytes 1 | tf_op jit(solution)/shard_map/pallas_call | solution.py:125
  2.7 7.3 %all-to-all-start = ((bf16[8,64,2304]{2,1,0:T(8,128)(2,1)}), bf16[8,64,2304]{2,1,0:T(8,128)(2,1)}, u32[]{:S(2)}, u32[]{:S(2)}) async-start(bf16[8,64,2304]{2,1,0:T(8,128)(2,1)} %shard_map.55.after_ref), calls=%async_computation | async-start | bytes 4718592 | tf_op jit(solution)/shard_map/all_to_all | solution.py:377
  9.9 6.5 %shard_map.56.after_ref = bf16[1,256,1024]{2,1,0:T(8,128)(2,1)} custom-call(s32[1]{0:T(128)} %bitcast.6.ids_ref, bf16[256,3584]{1,0:T(8,128)(2,1)} %hidden_ref.9, bf16[3584,8192]{1,0:T(8,128)(2,1)} %weight_ref.7, bf16[8,64,2304]{2,1,0:T(8,128)(2,1)} %shard_map.55.after_ref), custom_call_target="tpu_custom_call" | custom-call | flops 1 | bytes 1 | tf_op jit(solution)/shard_map/pallas_call | solution.py:68
  16.4 0.7 convert_reduce_fusion
  17.1 0.6 pad.10.tags_ref
  17.7 3.4 %shard_map.57 = (bf16[272,1792]{1,0:T(8,128)(2,1)}, bf16[272,1792]{1,0:T(8,128)(2,1)}) custom-call(s32[1]{0:T(128)} %bitcast.y_ref, bf16[256,3584]{1,0:T(8,128)(2,1)} %hidden_ref.9, bf16[16,1792]{1,0:T(8,128)(2,1)} %pad.10.tags_ref, bf16[1,256,1024]{2,1,0:T(8,128)(2,1)} %shard_map.56.after_ref), custom_call_target="tpu_custom_call" | custom-call | flops 1 | bytes 1 | tf_op jit(solution)/shard_map/pallas_call | solution.py:180
  21.2 1.6 collective-permute-start.1
  22.8 0.6 pad_add_fusion.1.ids_ref
  23.4 9.3 %shard_map.58.after_ref = bf16[2,256,1024]{2,1,0:T(8,128)(2,1)} custom-call(s32[2]{0:T(128)} %pad_add_fusion.1.ids_ref, bf16[256,3584]{1,0:T(8,128)(2,1)} %hidden_ref.9, bf16[3584,8192]{1,0:T(8,128)(2,1)} %weight_ref.7, bf16[272,1792]{1,0:T(8,128)(2,1)} %get-tuple-element.13.after_ref.refs_0_), custom_call_target="tpu_custom_call" | custom-call | flops 1 | bytes 1 | tf_op jit(solution)/shard_map/pallas_call | solution.py:68
  32.7 2.0 %collective-permute-start.4 = (bf16[2,256,1024]{2,1,0:T(8,128)(2,1)}, bf16[2,256,1024]{2,1,0:T(8,128)(2,1)}, u32[]{:S(2)}, u32[]{:S(2)}) collective-permute-start(bf16[2,256,1024]{2,1,0:T(8,128)(2,1)} %shard_map.58.after_ref), channel_id=1, source_target_pairs={{0,2},{2,0},{4,6},{6,4},{8,10},{10,8},{12,14},{14,12},{1,3},{3,1},... | collective-permute-start | bytes 3145736 | tf_op jit(solution)/shard_map/ppermute | solution.py:373
  34.7 0.7 pad_add_fusion.ids_ref
  35.4 9.7 %shard_map.59 = (bf16[1,256,1024]{2,1,0:T(8,128)(2,1)}, f32[1,256,1024]{2,1,0:T(8,128)}) custom-call(s32[2]{0:T(128)} %pad_add_fusion.ids_ref, bf16[256,3584]{1,0:T(8,128)(2,1)} %hidden_ref.9, bf16[3584,8192]{1,0:T(8,128)(2,1)} %weight_ref.7, bf16[2,256,1024]{2,1,0:T(8,128)(2,1)} %shard_map.58.after_ref), custom_call_target="tpu_custom_call" | custom-call | flops 1 | bytes 1 | tf_op jit(solution)/shard_map/pallas_call | solution.py:68
  45.1 0.0 collective-permute-start.2
  45.1 0.5 collective-permute-start
  45.6 1.2 collective-permute-start.3
  46.9 0.7 pad_add_fusion.2.ids_ref
  47.5 30.7 %collective-permute-done.3.refs_1_ = bf16[1,256,1024]{2,1,0:T(8,128)(2,1)} collective-permute-done((bf16[1,256,1024]{2,1,0:T(8,128)(2,1)}, bf16[1,256,1024]{2,1,0:T(8,128)(2,1)}, u32[]{:S(2)}, u32[]{:S(2)}) %collective-permute-start.3) | collective-permute-done | bytes 524320 | tf_op jit(solution)/shard_map/ppermute | solution.py:373
  78.2 2.2 %shard_map.61.after_ref = bf16[1,256,1024]{2,1,0:T(8,128)(2,1)} custom-call(f32[1,256,1024]{2,1,0:T(8,128)} %get-tuple-element.15.after_ref.refs_0_, bf16[1,256,1024]{2,1,0:T(8,128)(2,1)} %collective-permute-done.3.refs_1_, bf16[272,1792]{1,0:T(8,128)(2,1)} %shard_map.60.refs_2_.refs_0_), custom_call_target="tpu_custom_call" | custom-call | flops 1 | bytes 1 | tf_op jit(solution)/shard_map/pallas_call | solution.py:284
  80.5 4.7 %collective-permute-start.8 = (bf16[1,256,1024]{2,1,0:T(8,128)(2,1)}, bf16[1,256,1024]{2,1,0:T(8,128)(2,1)}, u32[]{:S(2)}, u32[]{:S(2)}) collective-permute-start(bf16[1,256,1024]{2,1,0:T(8,128)(2,1)} %shard_map.61.after_ref), channel_id=1, source_target_pairs={{0,4},{2,6},{4,0},{6,2},{8,12},{10,14},{12,8},{14,10},{1,5},{3,7},... | collective-permute-start | bytes 1572872 | tf_op jit(solution)/shard_map/ppermute | solution.py:373
  85.2 0.0 collective-permute-start.6
  85.2 13.3 %shard_map.62.refs_0_.refs_2_ = f32[3,256,1024]{2,1,0:T(8,128)} custom-call(s32[3]{0:T(128)} %pad_add_fusion.2.ids_ref, bf16[256,3584]{1,0:T(8,128)(2,1)} %hidden_ref.9, bf16[3584,8192]{1,0:T(8,128)(2,1)} %weight_ref.7, bf16[1,256,1024]{2,1,0:T(8,128)(2,1)} %shard_map.61.after_ref), custom_call_target="tpu_custom_call" | custom-call | flops 1 | bytes 1 | tf_op jit(solution)/shard_map/pallas_call | solution.py:68
  98.6 2.2 %shard_map.63.refs_2_ = bf16[1,256,1024]{2,1,0:T(8,128)(2,1)} custom-call(f32[3,256,1024]{2,1,0:T(8,128)} %shard_map.62.refs_0_.refs_2_, bf16[2,256,1024]{2,1,0:T(8,128)(2,1)} %collective-permute-done.4.refs_1_, f32[3,256,1024]{2,1,0:T(8,128)} %shard_map.62.refs_0_.refs_2_), custom_call_target="tpu_custom_call" | custom-call | flops 1 | bytes 1 | tf_op jit(solution)/shard_map/pallas_call | solution.py:284
  100.8 0.0 collective-permute-start.7
  100.8 0.0 collective-permute-done.2.refs_1_
  100.8 4.0 %shard_map.64.refs_2_ = f32[2,64,256]{2,1,0:T(8,128)} custom-call(s32[1]{0:T(128)} %bitcast.1.g_ref, bf16[512,2304]{1,0:T(8,128)(2,1)} %bitcast.5.factors_ref, bf16[272,1792]{1,0:T(8,128)(2,1)} %shard_map.60.refs_2_.refs_0_, bf16[272,1792]{1,0:T(8,128)(2,1)} %collective-permute-done.2.refs_1_, bf16[1,256,1024]{2,1,0:T(8,128)(2,1)} %shard_map.63.refs_2_), custom_call_target="tpu_custom_call" | custom-call | flops 1 | bytes 1 | tf_op jit(solution)/shard_map/pallas_call | solution.py:235
  104.8 0.0 collective-permute-done.refs_1_
  104.8 4.2 %shard_map.65 = (f32[2,64,256]{2,1,0:T(8,128)}, bf16[512,512]{1,0:T(8,128)(2,1)}) custom-call(s32[1]{0:T(128)} %bitcast.1.g_ref, bf16[512,2304]{1,0:T(8,128)(2,1)} %bitcast.5.factors_ref, bf16[272,1792]{1,0:T(8,128)(2,1)} %get-tuple-element.13.after_ref.refs_0_, bf16[272,1792]{1,0:T(8,128)(2,1)} %collective-permute-done.refs_1_, f32[2,64,256]{2,1,0:T(8,128)} %shard_map.64.refs_2_), custom_call_target="tpu_custom_call" | custom-call | flops 1 | bytes 1 | tf_op jit(solution)/shard_map/pallas_call | solution.py:235
  109.0 0.5 collective-permute-start.13
  109.5 1.5 collective-permute-start.5
  111.0 0.0 collective-permute-done.8.refs_2_
  111.0 2.5 %shard_map.66.refs_3_ = bf16[1,256,1024]{2,1,0:T(8,128)(2,1)} custom-call(f32[3,256,1024]{2,1,0:T(8,128)} %shard_map.62.refs_0_.refs_2_, bf16[2,256,1024]{2,1,0:T(8,128)(2,1)} %collective-permute-done.4.refs_1_, bf16[1,256,1024]{2,1,0:T(8,128)(2,1)} %collective-permute-done.8.refs_2_, f32[2,64,256]{2,1,0:T(8,128)} %get-tuple-element.16.refs_3_.refs_0_.refs_2_), custom_call_target="tpu_custom_call" | custom-call | flops 1 | bytes 1 | tf_op jit(solution)/shard_map/pallas_call | solution.py:284
  113.5 2.6 %shard_map.67.refs_4_ = f32[1,256,1024]{2,1,0:T(8,128)} custom-call(f32[3,256,1024]{2,1,0:T(8,128)} %shard_map.62.refs_0_.refs_2_, bf16[1,256,1024]{2,1,0:T(8,128)(2,1)} %collective-permute-done.6.refs_1_, bf16[1,256,1024]{2,1,0:T(8,128)(2,1)} %collective-permute-done.7.refs_2_, bf16[1,256,1024]{2,1,0:T(8,128)(2,1)} %shard_map.66.refs_3_), custom_call_target="tpu_custom_call" | custom-call | flops 1 | bytes 1 | tf_op jit(solution)/shard_map/pallas_call | solution.py:284
  116.2 8.0 %collective-permute-done.5.refs_1_.refs_3_ = f32[2,64,256]{2,1,0:T(8,128)} collective-permute-done((f32[2,64,256]{2,1,0:T(8,128)}, f32[2,64,256]{2,1,0:T(8,128)}, u32[]{:S(2)}, u32[]{:S(2)}) %collective-permute-start.5) | collective-permute-done | bytes 131104 | tf_op jit(solution)/shard_map/ppermute | solution.py:427
  124.2 1.6 shard_map.68
  125.8 1.6 collective-permute-done.9.refs_1_
  127.4 1.5 shard_map.69.refs_0_.refs_2_
  128.9 1.7 %collective-permute-start.10 = (f32[1,64,256]{2,1,0:T(8,128)}, f32[1,64,256]{2,1,0:T(8,128)}, u32[]{:S(2)}, u32[]{:S(2)}) collective-permute-start(f32[1,64,256]{2,1,0:T(8,128)} %shard_map.69.refs_0_.refs_2_), channel_id=1, source_target_pairs={{0,2},{2,0},{4,6},{6,4},{8,10},{10,8},{12,14},{14,12},{1,3},{3,1},... | collective-permute-start | bytes 196616 | tf_op jit(solution)/shard_map/ppermute | solution.py:373
  130.6 2.9 %collective-permute-done.10.refs_1_ = f32[1,64,256]{2,1,0:T(8,128)} collective-permute-done((f32[1,64,256]{2,1,0:T(8,128)}, f32[1,64,256]{2,1,0:T(8,128)}, u32[]{:S(2)}, u32[]{:S(2)}) %collective-permute-start.10) | collective-permute-done | bytes 65568 | tf_op jit(solution)/shard_map/ppermute | solution.py:373
  133.4 1.5 shard_map.70.refs_0_.refs_2_
  134.9 1.7 %collective-permute-start.11 = (f32[1,64,256]{2,1,0:T(8,128)}, f32[1,64,256]{2,1,0:T(8,128)}, u32[]{:S(2)}, u32[]{:S(2)}) collective-permute-start(f32[1,64,256]{2,1,0:T(8,128)} %shard_map.70.refs_0_.refs_2_), channel_id=1, source_target_pairs={{0,4},{2,6},{4,0},{6,2},{8,12},{10,14},{12,8},{14,10},{1,5},{3,7},... | collective-permute-start | bytes 196616 | tf_op jit(solution)/shard_map/ppermute | solution.py:373
  136.7 2.9 %collective-permute-done.11.refs_1_ = f32[1,64,256]{2,1,0:T(8,128)} collective-permute-done((f32[1,64,256]{2,1,0:T(8,128)}, f32[1,64,256]{2,1,0:T(8,128)}, u32[]{:S(2)}, u32[]{:S(2)}) %collective-permute-start.11) | collective-permute-done | bytes 65568 | tf_op jit(solution)/shard_map/ppermute | solution.py:373
  139.5 1.5 shard_map.71.after_ref.a_ref
  141.1 0.0 collective-permute-done.13.array_ref
  141.1 2.0 %collective-permute-start.12 = (f32[1,64,256]{2,1,0:T(8,128)}, f32[1,64,256]{2,1,0:T(8,128)}, u32[]{:S(2)}, u32[]{:S(2)}) collective-permute-start(f32[1,64,256]{2,1,0:T(8,128)} %shard_map.71.after_ref.a_ref), channel_id=1, source_target_pairs={{0,8},{2,10},{4,12},{6,14},{8,0},{10,2},{12,4},{14,6},{1,9},{3,11}... | collective-permute-start | bytes 196616 | tf_op jit(solution)/shard_map/ppermute | solution.py:373
  143.1 21.1 %collective-permute-done.12.b_ref = f32[1,64,256]{2,1,0:T(8,128)} collective-permute-done((f32[1,64,256]{2,1,0:T(8,128)}, f32[1,64,256]{2,1,0:T(8,128)}, u32[]{:S(2)}, u32[]{:S(2)}) %collective-permute-start.12) | collective-permute-done | bytes 65568 | tf_op jit(solution)/shard_map/ppermute | solution.py:373
  164.2 0.0 collective-permute-done.14.refs_2_
  164.2 0.0 collective-permute-done.15.refs_3_
  164.2 3.6 %shard_map.73 = bf16[256,1024]{1,0:T(8,128)(2,1)} custom-call(s32[1]{0:T(128)} %bitcast.y_ref, s32[1]{0:T(128)} %bitcast.1.g_ref, f32[1,64,256]{2,1,0:T(8,128)} %shard_map.71.after_ref.a_ref, f32[1,64,256]{2,1,0:T(8,128)} %collective-permute-done.12.b_ref, s32[1,256]{1,0:T(1,128)} %bitcast.18, bf16[512,512]{1,0:T(8,128)(2,1)} %get-tuple-element.20.refs_0_, ...), custom_call_target="tpu_custom_call" | custom-call | flops 1 | bytes 1 | tf_op jit(solution)/shard_map/pallas_call | solution.py:346
  (14 shorter events, 0.0 us)
Async XLA Ops:
  2.7 98.2 %all-to-all-start = ((bf16[8,64,2304]{2,1,0:T(8,128)(2,1)}), bf16[8,64,2304]{2,1,0:T(8,128)(2,1)}, u32[]{:S(2)}, u32[]{:S(2)}) async-start(bf16[8,64,2304]{2,1,0:T(8,128)(2,1)} %shard_map.55.after_ref), calls=%async_computation | async-start | bytes 4718592 | tf_op jit(solution)/shard_map/all_to_all | solution.py:377
  21.2 23.9 %collective-permute-start.1 = (bf16[272,1792]{1,0:T(8,128)(2,1)}, bf16[272,1792]{1,0:T(8,128)(2,1)}, u32[]{:S(2)}, u32[]{:S(2)}) collective-permute-start(bf16[272,1792]{1,0:T(8,128)(2,1)} %get-tuple-element.14), channel_id=1, source_target_pairs={{0,16},{16,0},{1,17},{17,1},{2,18},{18,2},{3,19},{19,3},{4,20},{20... | collective-permute-start | bytes 2924552 | tf_op jit(solution)/shard_map/ppermute | solution.py:414
  32.7 65.9 %collective-permute-start.4 = (bf16[2,256,1024]{2,1,0:T(8,128)(2,1)}, bf16[2,256,1024]{2,1,0:T(8,128)(2,1)}, u32[]{:S(2)}, u32[]{:S(2)}) collective-permute-start(bf16[2,256,1024]{2,1,0:T(8,128)(2,1)} %shard_map.58.after_ref), channel_id=1, source_target_pairs={{0,2},{2,0},{4,6},{6,4},{8,10},{10,8},{12,14},{14,12},{1,3},{3,1},... | collective-permute-start | bytes 3145736 | tf_op jit(solution)/shard_map/ppermute | solution.py:373
  45.1 55.7 %collective-permute-start.2 = (bf16[272,1792]{1,0:T(8,128)(2,1)}, bf16[272,1792]{1,0:T(8,128)(2,1)}, u32[]{:S(2)}, u32[]{:S(2)}) collective-permute-start(bf16[272,1792]{1,0:T(8,128)(2,1)} %shard_map.60.refs_2_.refs_0_), channel_id=1, source_target_pairs={{0,1},{1,0},{2,3},{3,2},{4,5},{5,4},{6,7},{7,6},{8,9},{9,8},{10,11... | collective-permute-start | bytes 2924552 | tf_op jit(solution)/shard_map/ppermute | solution.py:420
  45.1 59.7 %collective-permute-start = (bf16[272,1792]{1,0:T(8,128)(2,1)}, bf16[272,1792]{1,0:T(8,128)(2,1)}, u32[]{:S(2)}, u32[]{:S(2)}) collective-permute-start(bf16[272,1792]{1,0:T(8,128)(2,1)} %get-tuple-element.13.after_ref.refs_0_), channel_id=1, source_target_pairs={{0,1},{1,0},{2,3},{3,2},{4,5},{5,4},{6,7},{7,6},{8,9},{9,8},{10,11... | collective-permute-start | bytes 2924552 | tf_op jit(solution)/shard_map/ppermute | solution.py:415
  45.6 32.6 %collective-permute-start.3 = (bf16[1,256,1024]{2,1,0:T(8,128)(2,1)}, bf16[1,256,1024]{2,1,0:T(8,128)(2,1)}, u32[]{:S(2)}, u32[]{:S(2)}) collective-permute-start(bf16[1,256,1024]{2,1,0:T(8,128)(2,1)} %shard_map.56.after_ref), channel_id=1, source_target_pairs={{0,2},{2,0},{4,6},{6,4},{8,10},{10,8},{12,14},{14,12},{1,3},{3,1},... | collective-permute-start | bytes 1572872 | tf_op jit(solution)/shard_map/ppermute | solution.py:373
  80.5 30.6 %collective-permute-start.8 = (bf16[1,256,1024]{2,1,0:T(8,128)(2,1)}, bf16[1,256,1024]{2,1,0:T(8,128)(2,1)}, u32[]{:S(2)}, u32[]{:S(2)}) collective-permute-start(bf16[1,256,1024]{2,1,0:T(8,128)(2,1)} %shard_map.61.after_ref), channel_id=1, source_target_pairs={{0,4},{2,6},{4,0},{6,2},{8,12},{10,14},{12,8},{14,10},{1,5},{3,7},... | collective-permute-start | bytes 1572872 | tf_op jit(solution)/shard_map/ppermute | solution.py:373
  85.2 28.3 %collective-permute-start.6 = (bf16[1,256,1024]{2,1,0:T(8,128)(2,1)}, bf16[1,256,1024]{2,1,0:T(8,128)(2,1)}, u32[]{:S(2)}, u32[]{:S(2)}) collective-permute-start(bf16[1,256,1024]{2,1,0:T(8,128)(2,1)} %get-tuple-element.17), channel_id=1, source_target_pairs={{0,2},{2,0},{4,6},{6,4},{8,10},{10,8},{12,14},{14,12},{1,3},{3,1},... | collective-permute-start | bytes 1572872 | tf_op jit(solution)/shard_map/ppermute | solution.py:373
  100.8 12.7 %collective-permute-start.7 = (bf16[1,256,1024]{2,1,0:T(8,128)(2,1)}, bf16[1,256,1024]{2,1,0:T(8,128)(2,1)}, u32[]{:S(2)}, u32[]{:S(2)}) collective-permute-start(bf16[1,256,1024]{2,1,0:T(8,128)(2,1)} %shard_map.63.refs_2_), channel_id=1, source_target_pairs={{0,4},{2,6},{4,0},{6,2},{8,12},{10,14},{12,8},{14,10},{1,5},{3,7},... | collective-permute-start | bytes 1572872 | tf_op jit(solution)/shard_map/ppermute | solution.py:373
  109.0 32.1 %collective-permute-start.13 = (bf16[512,512]{1,0:T(8,128)(2,1)}, bf16[512,512]{1,0:T(8,128)(2,1)}, u32[]{:S(2)}, u32[]{:S(2)}) collective-permute-start(bf16[512,512]{1,0:T(8,128)(2,1)} %get-tuple-element.20.refs_0_), channel_id=1, source_target_pairs={{0,16},{16,0},{1,17},{17,1},{2,18},{18,2},{3,19},{19,3},{4,20},{20... | collective-permute-start | bytes 1572872 | tf_op jit(solution)/shard_map/ppermute | solution.py:431
  109.5 14.7 %collective-permute-start.5 = (f32[2,64,256]{2,1,0:T(8,128)}, f32[2,64,256]{2,1,0:T(8,128)}, u32[]{:S(2)}, u32[]{:S(2)}) collective-permute-start(f32[2,64,256]{2,1,0:T(8,128)} %shard_map.64.refs_2_), channel_id=1, source_target_pairs={{0,16},{16,0},{1,17},{17,1},{2,18},{18,2},{3,19},{19,3},{4,20},{20... | collective-permute-start | bytes 393224 | tf_op jit(solution)/shard_map/ppermute | solution.py:427
  125.8 1.6 collective-permute-start.9
  128.9 4.6 %collective-permute-start.10 = (f32[1,64,256]{2,1,0:T(8,128)}, f32[1,64,256]{2,1,0:T(8,128)}, u32[]{:S(2)}, u32[]{:S(2)}) collective-permute-start(f32[1,64,256]{2,1,0:T(8,128)} %shard_map.69.refs_0_.refs_2_), channel_id=1, source_target_pairs={{0,2},{2,0},{4,6},{6,4},{8,10},{10,8},{12,14},{14,12},{1,3},{3,1},... | collective-permute-start | bytes 196616 | tf_op jit(solution)/shard_map/ppermute | solution.py:373
  134.9 4.6 %collective-permute-start.11 = (f32[1,64,256]{2,1,0:T(8,128)}, f32[1,64,256]{2,1,0:T(8,128)}, u32[]{:S(2)}, u32[]{:S(2)}) collective-permute-start(f32[1,64,256]{2,1,0:T(8,128)} %shard_map.70.refs_0_.refs_2_), channel_id=1, source_target_pairs={{0,4},{2,6},{4,0},{6,2},{8,12},{10,14},{12,8},{14,10},{1,5},{3,7},... | collective-permute-start | bytes 196616 | tf_op jit(solution)/shard_map/ppermute | solution.py:373
  136.7 27.6 %collective-permute-start.16 = (bf16[1,256,1024]{2,1,0:T(8,128)(2,1)}, bf16[1,256,1024]{2,1,0:T(8,128)(2,1)}, u32[]{:S(2)}, u32[]{:S(2)}) collective-permute-start(bf16[1,256,1024]{2,1,0:T(8,128)(2,1)} %shard_map.66.refs_3_), channel_id=1, source_target_pairs={{0,8},{2,10},{4,12},{6,14},{8,0},{10,2},{12,4},{14,6},{1,9},{3,11}... | collective-permute-start | bytes 1572872 | tf_op jit(solution)/shard_map/ppermute | solution.py:373
  136.7 27.6 %collective-permute-start.14 = (bf16[512,512]{1,0:T(8,128)(2,1)}, bf16[512,512]{1,0:T(8,128)(2,1)}, u32[]{:S(2)}, u32[]{:S(2)}) collective-permute-start(bf16[512,512]{1,0:T(8,128)(2,1)} %get-tuple-element.20.refs_0_), channel_id=1, source_target_pairs={{0,1},{1,0},{2,3},{3,2},{4,5},{5,4},{6,7},{7,6},{8,9},{9,8},{10,11... | collective-permute-start | bytes 1572872 | tf_op jit(solution)/shard_map/ppermute | solution.py:448
  141.1 23.2 %collective-permute-start.15 = (bf16[512,512]{1,0:T(8,128)(2,1)}, bf16[512,512]{1,0:T(8,128)(2,1)}, u32[]{:S(2)}, u32[]{:S(2)}) collective-permute-start(bf16[512,512]{1,0:T(8,128)(2,1)} %shard_map.72.refs_1_), channel_id=1, source_target_pairs={{0,1},{1,0},{2,3},{3,2},{4,5},{5,4},{6,7},{7,6},{8,9},{9,8},{10,11... | collective-permute-start | bytes 1572872 | tf_op jit(solution)/shard_map/ppermute | solution.py:449
  141.1 23.1 %collective-permute-start.12 = (f32[1,64,256]{2,1,0:T(8,128)}, f32[1,64,256]{2,1,0:T(8,128)}, u32[]{:S(2)}, u32[]{:S(2)}) collective-permute-start(f32[1,64,256]{2,1,0:T(8,128)} %shard_map.71.after_ref.a_ref), channel_id=1, source_target_pairs={{0,8},{2,10},{4,12},{6,14},{8,0},{10,2},{12,4},{14,6},{1,9},{3,11}... | collective-permute-start | bytes 196616 | tf_op jit(solution)/shard_map/ppermute | solution.py:373

commit v4 on v3

v4 whole, which is shorter than its diff:
```python
import jax
import jax.numpy as jnp
from jax import lax
from jax.experimental import pallas as pl
from jax.experimental.pallas import tpu as pltpu
from jax.sharding import PartitionSpec as P

SWAP = ((0, 1), (1, 0))
ANY = pl.BlockSpec(memory_space=pl.ANY)
VMEM = pl.BlockSpec(memory_space=pltpu.VMEM)
SMEM = pl.BlockSpec(memory_space=pltpu.SMEM)
TAG_ROWS = 16
COST = pl.CostEstimate(flops=1, bytes_accessed=1, transcendentals=0)
PARAMS = pltpu.CompilerParams(vmem_limit_bytes=64 * 2**20)


class Order:
    def __init__(self, array):
        self.last = array


def block_products(hidden, weight, t, sent, kept, columns, order):
    rows, depth = hidden.shape

    def kernel(t_ref, hidden_ref, weight_ref, after_ref, *out_refs):
        product = jnp.dot(hidden_ref[...], weight_ref[...], preferred_element_type=jnp.float32)
        for i in range(len(sent)):

            @pl.when(pl.program_id(0) == i)
            def _():
                out_refs[i][0] = product.astype(jnp.bfloat16)

        if kept:

            @pl.when(pl.program_id(0) >= len(sent))
            def _():
                out_refs[-1][0] = product

    def block(b, t_ref):
        j = jnp.where(
            b < len(sent),
            (sent[0] if sent else 0) - 2 * b,
            (kept[0] if kept else 0) - 2 * (b - len(sent)),
        )
        return 0, t_ref[0] ^ j

    out_shape = [jax.ShapeDtypeStruct((1, rows, columns), jnp.bfloat16)] * len(sent)
    out_specs = [pl.BlockSpec((1, rows, columns), lambda b, _: (0, 0, 0))] * len(sent)
    if kept:
        out_shape.append(jax.ShapeDtypeStruct((len(kept), rows, columns), jnp.float32))
        out_specs.append(
            pl.BlockSpec((1, rows, columns), lambda b, _: (jnp.maximum(b - len(sent), 0), 0, 0))
        )
    outs = pl.pallas_call(
        kernel,
        name="products",
        out_shape=out_shape,
        grid_spec=pltpu.PrefetchScalarGridSpec(
            num_scalar_prefetch=1,
            grid=(len(sent) + len(kept),),
            in_specs=[
                pl.BlockSpec((rows, depth), lambda b, _: (0, 0)),
                pl.BlockSpec((depth, columns), block),
                ANY,
            ],
            out_specs=out_specs,
        ),
        compiler_params=PARAMS,
        cost_estimate=COST,
    )(t.reshape(1), hidden, weight, order.last)
    order.last = outs[-1]
    return outs


def pack_factors(first, second, tp, y):
    rank = first.shape[0]
    widths = [first.shape[1] // (2 * tp), second.shape[1] // (2 * tp)]
    if widths[0] % 128 or widths[1] % 128:
        parts = [
            lax.dynamic_index_in_dim(
                source.reshape(rank, tp, 2, width), y, 2, keepdims=False
            ).transpose(1, 0, 2)
            for source, width in zip((first, second), widths)
        ]
        return jnp.concatenate(parts, axis=2)
    places = [pl.ds(0, widths[0]), pl.ds(widths[0], widths[1])]

    def kernel(y_ref, first_ref, second_ref, out_ref, buffer, in_sem, out_sem):
        def fetch(i, which):
            width = widths[which]
            start = pl.multiple_of((2 * i + y_ref[0]) * width, 128)
            return pltpu.make_async_copy(
                (first_ref, second_ref)[which].at[:, pl.ds(start, width)],
                buffer.at[i, :, places[which]],
                in_sem.at[i, which],
            )

        def store(i):
            return pltpu.make_async_copy(buffer.at[i], out_ref.at[i], out_sem.at[i])

        for i in range(tp):
            for which in range(2):
                fetch(i, which).start()
        for i in range(tp):
            for which in range(2):
                fetch(i, which).wait()
            store(i).start()
        for i in range(tp):
            store(i).wait()

    shape = (tp, rank, sum(widths))
    return pl.pallas_call(
        kernel,
        name="pack_factors",
        out_shape=jax.ShapeDtypeStruct(shape, first.dtype),
        in_specs=[SMEM, ANY, ANY],
        out_specs=ANY,
        scratch_shapes=[
            pltpu.VMEM(shape, first.dtype),
            pltpu.SemaphoreType.DMA((tp, 2)),
            pltpu.SemaphoreType.DMA((tp,)),
        ],
        compiler_params=PARAMS,
        cost_estimate=COST,
    )(y.reshape(1), first, second)


def pack_hidden(hidden, adapter, half, y, order):
    rows = hidden.shape[0]
    if half % 128 or half < rows:
        tags = jnp.pad(adapter[0], (0, -rows % half)).astype(jnp.bfloat16).reshape(-1, half)
        tags = jnp.pad(tags, ((0, TAG_ROWS - tags.shape[0]), (0, 0)))
        return [
            jnp.concatenate(
                [lax.dynamic_slice(hidden, (0, which * half), (rows, half)), tags], axis=0
            )
            for which in (y, 1 - y)
        ]

    def kernel(y_ref, hidden_ref, adapter_ref, after_ref, mine_ref, other_ref, buffer, in_sem, out_sem):
        def fetch(which):
            half_index = y_ref[0] if which == 0 else 1 - y_ref[0]
            return pltpu.make_async_copy(
                hidden_ref.at[:, pl.ds(pl.multiple_of(half_index * half, 128), half)],
                buffer.at[which, pl.ds(0, rows)],
                in_sem.at[which],
            )

        def store(which):
            out_ref = (mine_ref, other_ref)[which]
            return pltpu.make_async_copy(buffer.at[which], out_ref, out_sem.at[which])

        for which in (1, 0):
            fetch(which).start()
        tags = adapter_ref[...].astype(jnp.float32).astype(hidden.dtype)
        for which in (1, 0):
            buffer[which, rows:, :rows] = jnp.broadcast_to(tags, (TAG_ROWS, rows))
        for which in (1, 0):
            fetch(which).wait()
            store(which).start()
        for which in (1, 0):
            store(which).wait()

    shape = jax.ShapeDtypeStruct((rows + TAG_ROWS, half), hidden.dtype)
    mine, other = pl.pallas_call(
        kernel,
        name="pack_hidden",
        out_shape=[shape, shape],
        in_specs=[SMEM, ANY, VMEM, ANY],
        out_specs=[ANY, ANY],
        scratch_shapes=[
            pltpu.VMEM((2, rows + TAG_ROWS, half), hidden.dtype),
            pltpu.SemaphoreType.DMA((2,)),
            pltpu.SemaphoreType.DMA((2,)),
        ],
        compiler_params=PARAMS,
        cost_estimate=COST,
    )(y.reshape(1), hidden, adapter, order.last)
    order.last = mine
    return mine, other


def latent_terms(factors, half, blocks, rows, rank, g, order):
    count = factors.shape[0]
    tp = count // rank
    pairs = len(blocks) // 2

    def term(factor, rows_held, adapter, core):
        full = lax.dot_general(
            factor, rows_held, (((1,), (1,)), ((), ())), preferred_element_type=jnp.float32
        )
        total = jnp.zeros((rank, rows), jnp.float32)
        for place in range(tp):
            total += jnp.where(
                adapter == place * 2 + core, full[place * rank : (place + 1) * rank], 0.0
            )
        return total

    if half % 128 or half < rows:
        outs = [
            term(
                factors[:, :half],
                block[:rows],
                block[rows:].reshape(-1)[:rows][None].astype(jnp.int32),
                g,
            )
            for block in blocks
        ]
        return jnp.stack(outs[:pairs]), jnp.stack(outs[pairs:]), factors[:, half:]

    def kernel(g_ref, factors_ref, *refs):
        block_refs, out_refs = refs[: len(blocks)], refs[len(blocks) + 1 :]
        for i, block_ref in enumerate(block_refs):
            tag = block_ref[rows:, :rows].astype(jnp.float32)[0:1].astype(jnp.int32)
            out_refs[i // pairs][i % pairs] = term(
                factors_ref[:, :half], block_ref[:rows, :], tag, g_ref[0]
            )
        out_refs[-1][...] = factors_ref[:, half:]

    outs = pl.pallas_call(
        kernel,
        name="latent_terms",
        out_shape=[jax.ShapeDtypeStruct((pairs, rank, rows), jnp.float32)] * 2
        + [jax.ShapeDtypeStruct((count, factors.shape[1] - half), factors.dtype)],
        in_specs=[SMEM, VMEM] + [VMEM] * len(blocks) + [ANY],
        out_specs=[VMEM] * 3,
        compiler_params=PARAMS,
        cost_estimate=COST,
    )(g.reshape(1), factors, *blocks, order.last)
    order.last = outs[0]
    return outs


def block_specs(blocks):
    return [
        pl.BlockSpec((1, *array.shape[1:]), lambda b, i=i: (i, 0, 0)) for array, i in blocks
    ]


def fold(sums, order, pair=()):
    blocks = [block for terms in sums for block in terms]
    shape = blocks[0][0].shape[1:]

    def kernel(*refs):
        at = 0
        outs = refs[len(blocks) + len(pair) + 1 :]
        for out_ref, terms in zip(outs, sums):
            total = refs[at][0]
            for ref in refs[at + 1 : at + len(terms)]:
                total += ref[0].astype(jnp.float32)
            out_ref[0] = total.astype(jnp.bfloat16)
            at += len(terms)
        if pair:
            count = pair[0].shape[0]
            outs[-1][:count] = refs[at][...]
            outs[-1][count:] = refs[at + 1][...]

    out_shape = [jax.ShapeDtypeStruct((1, *shape), jnp.bfloat16)] * len(sums)
    out_specs = [pl.BlockSpec((1, *shape), lambda b: (0, 0, 0))] * len(sums)
    if pair:
        count, width = pair[0].shape
        out_shape.append(jax.ShapeDtypeStruct((2 * count, width), pair[0].dtype))
        out_specs.append(pl.BlockSpec((2 * count, width), lambda b: (0, 0)))
    outs = pl.pallas_call(
        kernel,
        name="fold",
        grid=(1,),
        out_shape=out_shape,
        in_specs=block_specs(blocks)
        + [pl.BlockSpec(array.shape, lambda b: (0, 0)) for array in pair]
        + [ANY],
        out_specs=out_specs,
        compiler_params=PARAMS,
        cost_estimate=COST,
    )(*[array for array, _ in blocks], *pair, order.last)
    order.last = outs[0]
    return outs


def relay(array, after):
    def kernel(array_ref, after_ref, out_ref):
        del array_ref, after_ref, out_ref

    return pl.pallas_call(
        kernel,
        name="relay",
        out_shape=jax.ShapeDtypeStruct(array.shape, array.dtype),
        in_specs=[ANY, ANY],
        out_specs=ANY,
        input_output_aliases={0: 0},
        compiler_params=PARAMS,
        cost_estimate=COST,
    )(array, after)


def finish(latent, adapter, seconds, blocks, y, g):
    rows, columns = blocks[0][0].shape[1:]
    rank = latent.shape[0]
    tp = seconds[0].shape[0] // (2 * rank)
    half = columns // 2

    def spread(held, ids, core):
        held = held.astype(jnp.bfloat16).astype(jnp.float32)
        return jnp.concatenate(
            [
                jnp.where(ids == place * 2 + which, held, jnp.zeros_like(held))
                for which in (core, 1 - core)
                for place in range(tp)
            ],
            axis=0,
        ).astype(jnp.bfloat16)

    def product(left, right):
        return lax.dot_general(
            left, right, (((0,), (0,)), ((), ())), preferred_element_type=jnp.float32
        )

    if half % 128:
        wide = spread(latent, adapter, g)
        mine, other = product(wide, seconds[0]), product(wide, seconds[1])
        delta = jnp.where(
            y == 0,
            jnp.concatenate([mine, other], axis=1),
            jnp.concatenate([other, mine], axis=1),
        )
        total = delta.astype(jnp.bfloat16).astype(jnp.float32)
        for array, i in blocks:
            total = total + array[i].astype(jnp.float32)
        return total.astype(jnp.bfloat16)

    def kernel(y_ref, g_ref, latent_ref, adapter_ref, *refs):
        second_refs, block_refs, out_ref = refs[:2], refs[2:-1], refs[-1]
        wide = spread(latent_ref[...], adapter_ref[...], g_ref[0])
        for which in range(2):
            index = y_ref[0] if which == 0 else 1 - y_ref[0]
            lanes = pl.ds(pl.multiple_of(index * half, 128), half)
            delta = product(wide, second_refs[which][...])
            total = block_refs[0][0, :, lanes]
            for block_ref in block_refs[1:]:
                total += block_ref[0, :, lanes].astype(jnp.float32)
            total += delta.astype(jnp.bfloat16).astype(jnp.float32)
            out_ref[:, lanes] = total.astype(jnp.bfloat16)

    whole = lambda array: pl.BlockSpec(array.shape, lambda b: (0,) * array.ndim)
    return pl.pallas_call(
        kernel,
        name="finish",
        grid=(1,),
        out_shape=jax.ShapeDtypeStruct((rows, columns), jnp.bfloat16),
        in_specs=[SMEM, SMEM]
        + [whole(array) for array in (latent, adapter, *seconds)]
        + block_specs(blocks),
        out_specs=pl.BlockSpec((rows, columns), lambda b: (0, 0)),
        compiler_params=PARAMS,
        cost_estimate=COST,
    )(y.reshape(1), g.reshape(1), latent, adapter, *seconds, *[array for array, _ in blocks])


def local(
    hidden, row_adapter_index, down_projection_weight, adapter_first_factor, adapter_second_factor
):
    tp = lax.axis_size("tp")
    t = lax.axis_index("tp")
    y = lax.axis_index("rep")
    g = lax.axis_index("grp")
    rows, depth = hidden.shape
    rank = adapter_first_factor.shape[2]
    columns = down_projection_weight.shape[1] // tp
    half = depth // 2
    adapter = row_adapter_index.T

    def across(array, step):
        return lax.ppermute(array, "tp", [(i, i ^ step) for i in range(tp)])

    factors = pack_factors(adapter_first_factor[0].T, adapter_second_factor[0], tp, y)
    order = Order(factors)
    factors = lax.all_to_all(factors, "tp", split_axis=0, concat_axis=0, tiled=True)
    factors = factors.reshape(tp * rank, factors.shape[2])
    mine, other = pack_hidden(hidden, adapter, half, y, order)
    from_rep = lax.ppermute(other, "rep", SWAP)
    from_grp = lax.ppermute(mine, "grp", SWAP)
    from_both = lax.ppermute(other, ("rep", "grp"), [(i, 3 - i) for i in range(4)])

    terms = {j: [] for j in range(0, tp, 2)}

    def multiply(sent, kept):
        outs = block_products(hidden, down_projection_weight, t, sent, kept, columns, order)
        for i, j in enumerate(kept):
            terms[j].insert(0, (outs[-1], i))
        for j, out in zip(sent, outs):
            terms[j ^ 1].append((across(out, 1), 0))

    def pass_on(items, pair=()):
        outs = fold([terms[j] for _, j in items], order, pair)
        for (step, j), out in zip(items, outs):
            terms[j ^ step].append((across(out, step), 0))
        return outs[-1]

    odd = list(range(tp - 1, 0, -2))
    stages = []
    step = 2
    while step < tp:
        stages.append([(step, j) for j in range(tp - step, 0, -2 * step)])
        step *= 2

    multiply(odd[:1], [])
    multiply(odd[1:2], [odd[0] - 1])
    multiply(odd[2:3], [odd[1] - 1])
    multiply(odd[3:], [j - 1 for j in odd[2:]])
    pass_on(stages[0][:1])

    blocks = [mine, from_grp, from_rep, from_both]
    near, away, second = latent_terms(factors, half, blocks, rows, rank, g, order)
    got = lax.ppermute(away, "rep", SWAP)
    rest = [stages[0][1:], *stages[1:]]
    if tp <= 8:
        rest = [[item for items in reversed(rest) for item in items]]
    for items in rest[:-1]:
        pass_on(items)
    second = pass_on(rest[-1], (second, lax.ppermute(second, "grp", SWAP)))
    second = relay(second, got)
    seconds = [second, lax.ppermute(second, "rep", SWAP)]

    def exchange(near, got):
        held = near + got
        latent = held[0] + lax.ppermute(held[1], "grp", SWAP)
        step = 1
        while step < tp:
            latent = latent + across(latent, step)
            step *= 2
        return latent

    latent = lax.cond(t < tp, exchange, lambda near, got: near[0], relay(near, order.last), got)
    return finish(latent, adapter, seconds, terms[0], y, g)


def solution(mesh):
    return jax.shard_map(
        local,
        mesh=mesh,
        in_specs=(
            P(("rep", "grp"), "tp"),
            P(("rep", "grp"), None),
            P("tp", None),
            P(("tp", "grp"), None, None),
            P(("tp", "grp"), None, None),
        ),
        out_specs=P(("rep", "grp"), "tp"),
        check_vma=False,
    )
```

time: 169 us -> 119 us (0.70)
  waiting for transfers between devices: 67.2 us -> 31.9 us
  Pallas kernels: 72.5 us -> 58.2 us
  starting transfers between devices: 24.9 us -> 26.6 us
    ppermute x9 -> x10, waiting for transfers between devices: 57.6 us -> 26.1 us  [across(): return lax.ppermute(array, 'tp', [(i, i ^ step) for i in range(tp)])]
    pallas_call x19 -> x12, Pallas kernels: 72.5 us -> 58.2 us  [the longest x4 36.7 us: block_products(): pl.pallas_call(kernel, name='products', out_shape=out_shape, grid_spec=pl...]
    ppermute x1, waiting for transfers between devices: 8.01 us -> 0.01 us  [local(): got = lax.ppermute(away, 'rep', SWAP)]
    all_to_all x1, waiting for transfers between devices: 0.01 us -> 4.55 us  [local(): lax.all_to_all(factors, 'tp', split_axis=0, concat_axis=0, tiled=True)]
    another operation x4 -> x0, other arithmetic: 2.59 us -> none  [the longest x3 1.9 us: block_products(): jnp.stack(sent_ids + kept_ids)]
    ppermute x5 -> x4, starting transfers between devices: 0.49 us -> 2.4 us  [the longest x1 1.58 us: local(): seconds = [second, lax.ppermute(second, 'rep', SWAP)]]
    ppermute x9 -> x10, starting transfers between devices: 13.5 us -> 14.2 us  [across(): return lax.ppermute(array, 'tp', [(i, i ^ step) for i in range(tp)])]
  transfers between devices with their start and end apart: 18 -> 18, of which waited for: 6 -> 7; matrix products, arithmetic and copies ran while one was open for 2% -> 1% of each run, Pallas kernels for 39% -> 44%
where the time goes in v4:
time: 119 us; the launch traced here: 118 us
  Pallas kernels  58.2 us (49%)
  waiting for transfers between devices  31.9 us (27%)
  starting transfers between devices  26.6 us (22%)
  other arithmetic  1.64 us (1%)
    pallas_call x4, Pallas kernels, block_products(): pl.pallas_call(kernel, name='products', out_shape=out_shape, grid_spec=pl...  36.7 us
    ppermute x10, waiting for transfers between devices, across(): return lax.ppermute(array, 'tp', [(i, i ^ step) for i in range(tp)])  26.1 us
    ppermute x10, starting transfers between devices, across(): return lax.ppermute(array, 'tp', [(i, i ^ step) for i in range(tp)])  14.2 us
    all_to_all x1, starting transfers between devices, local(): lax.all_to_all(factors, 'tp', split_axis=0, concat_axis=0, tiled=True)  7.26 us
    pallas_call x2, Pallas kernels, fold(): pl.pallas_call(kernel, name='fold', grid=(1,), out_shape=out_shape, in_sp...  5.94 us
    pallas_call x1, Pallas kernels, latent_terms(): pl.pallas_call(kernel, name='latent_terms', out_shape=[jax.ShapeDtypeStru...  5.79 us
    all_to_all x1, waiting for transfers between devices, local(): lax.all_to_all(factors, 'tp', split_axis=0, concat_axis=0, tiled=True)  4.55 us
    pallas_call x1, Pallas kernels, finish(): pl.pallas_call(kernel, name='finish', grid=(1,), out_shape=jax.ShapeDtype...  3.92 us
  transfers between devices with their start and end apart: 18, of which 7 were waited for; matrix products, arithmetic and copies ran while one was open for 1% of the time, Pallas kernels for 44%

profile of v4, /device:TPU:0, one launch (start us, length us, event | category | flops | bytes accessed | tf_op | source)
XLA Modules:
  0.0 118.4 jit_solution(17778169824561715246)
XLA Ops:
  0.0 2.7 %pack_factors.1.after_ref = bf16[8,64,2304]{2,1,0:T(8,128)(2,1)} custom-call(s32[1]{0:T(128)} %bitcast.3.y_ref, bf16[64,28672]{1,0:T(8,128)(2,1)} %bitcast.17, bf16[64,8192]{1,0:T(8,128)(2,1)} %bitcast.18), custom_call_target="tpu_custom_call" | custom-call | flops 1 | bytes 1 | tf_op jit(solution)/shard_map/pack_factors/pallas_call | solution.py:112
  2.7 7.3 %all-to-all-start = ((bf16[8,64,2304]{2,1,0:T(8,128)(2,1)}), bf16[8,64,2304]{2,1,0:T(8,128)(2,1)}, u32[]{:S(2)}, u32[]{:S(2)}) async-start(bf16[8,64,2304]{2,1,0:T(8,128)(2,1)} %pack_factors.1.after_ref), calls=%async_computation | async-start | bytes 4718592 | tf_op jit(solution)/shard_map/all_to_all | solution.py:377
  10.0 3.1 %pack_hidden.1 = (bf16[272,1792]{1,0:T(8,128)(2,1)}, bf16[272,1792]{1,0:T(8,128)(2,1)}) custom-call(s32[1]{0:T(128)} %bitcast.3.y_ref, bf16[256,3584]{1,0:T(8,128)(2,1)} %hidden_ref.9, s32[1,256]{1,0:T(1,128)} %bitcast.19, bf16[8,64,2304]{2,1,0:T(8,128)(2,1)} %pack_factors.1.after_ref), custom_call_target="tpu_custom_call" | custom-call | flops 1 | bytes 1 | tf_op jit(solution)/shard_map/pack_hidden/pallas_call | solution.py:165
  13.1 0.7 collective-permute-start.6
  13.8 0.9 collective-permute-start.5
  14.8 0.3 collective-permute-start.4
  15.0 6.5 %products.4.after_ref = bf16[1,256,1024]{2,1,0:T(8,128)(2,1)} custom-call(s32[1]{0:T(128)} %bitcast.10.t_ref, bf16[256,3584]{1,0:T(8,128)(2,1)} %hidden_ref.9, bf16[3584,8192]{1,0:T(8,128)(2,1)} %weight_ref.7, bf16[272,1792]{1,0:T(8,128)(2,1)} %get-tuple-element.29.after_ref.refs_0_), custom_call_target="tpu_custom_call" | custom-call | flops 1 | bytes 1 | tf_op jit(solution)/shard_map/products/pallas_call | solution.py:54
  21.5 2.0 %collective-permute-start.7 = (bf16[1,256,1024]{2,1,0:T(8,128)(2,1)}, bf16[1,256,1024]{2,1,0:T(8,128)(2,1)}, u32[]{:S(2)}, u32[]{:S(2)}) collective-permute-start(bf16[1,256,1024]{2,1,0:T(8,128)(2,1)} %products.4.after_ref), channel_id=1, source_target_pairs={{0,2},{2,0},{4,6},{6,4},{8,10},{10,8},{12,14},{14,12},{1,3},{3,1},... | collective-permute-start | bytes 1572872 | tf_op jit(solution)/shard_map/ppermute | solution.py:373
  23.5 9.1 %products.5 = (bf16[1,256,1024]{2,1,0:T(8,128)(2,1)}, f32[1,256,1024]{2,1,0:T(8,128)}) custom-call(s32[1]{0:T(128)} %bitcast.10.t_ref, bf16[256,3584]{1,0:T(8,128)(2,1)} %hidden_ref.9, bf16[3584,8192]{1,0:T(8,128)(2,1)} %weight_ref.7, bf16[1,256,1024]{2,1,0:T(8,128)(2,1)} %products.4.after_ref), custom_call_target="tpu_custom_call" | custom-call | flops 1 | bytes 1 | tf_op jit(solution)/shard_map/products/pallas_call | solution.py:54
  32.7 0.0 collective-permute-start.8
  32.7 9.0 %products.6 = (bf16[1,256,1024]{2,1,0:T(8,128)(2,1)}, f32[1,256,1024]{2,1,0:T(8,128)}) custom-call(s32[1]{0:T(128)} %bitcast.10.t_ref, bf16[256,3584]{1,0:T(8,128)(2,1)} %hidden_ref.9, bf16[3584,8192]{1,0:T(8,128)(2,1)} %weight_ref.7, f32[1,256,1024]{2,1,0:T(8,128)} %get-tuple-element.31.after_ref.refs_0_), custom_call_target="tpu_custom_call" | custom-call | flops 1 | bytes 1 | tf_op jit(solution)/shard_map/products/pallas_call | solution.py:54
  41.7 12.1 %products.7 = (bf16[1,256,1024]{2,1,0:T(8,128)(2,1)}, f32[2,256,1024]{2,1,0:T(8,128)}) custom-call(s32[1]{0:T(128)} %bitcast.10.t_ref, bf16[256,3584]{1,0:T(8,128)(2,1)} %hidden_ref.9, bf16[3584,8192]{1,0:T(8,128)(2,1)} %weight_ref.7, f32[1,256,1024]{2,1,0:T(8,128)} %get-tuple-element.32.after_ref.refs_0_), custom_call_target="tpu_custom_call" | custom-call | flops 1 | bytes 1 | tf_op jit(solution)/shard_map/products/pallas_call | solution.py:54
  53.8 0.0 collective-permute-done.7.refs_1_
  53.8 2.0 %collective-permute-start.10 = (bf16[1,256,1024]{2,1,0:T(8,128)(2,1)}, bf16[1,256,1024]{2,1,0:T(8,128)(2,1)}, u32[]{:S(2)}, u32[]{:S(2)}) collective-permute-start(bf16[1,256,1024]{2,1,0:T(8,128)(2,1)} %get-tuple-element.36), channel_id=1, source_target_pairs={{0,2},{2,0},{4,6},{6,4},{8,10},{10,8},{12,14},{14,12},{1,3},{3,1},... | collective-permute-start | bytes 1572872 | tf_op jit(solution)/shard_map/ppermute | solution.py:373
  55.8 2.2 %fold.2.refs_4_ = bf16[1,256,1024]{2,1,0:T(8,128)(2,1)} custom-call(f32[1,256,1024]{2,1,0:T(8,128)} %get-tuple-element.31.after_ref.refs_0_, bf16[1,256,1024]{2,1,0:T(8,128)(2,1)} %collective-permute-done.7.refs_1_, f32[2,256,1024]{2,1,0:T(8,128)} %get-tuple-element.33.refs_2_.refs_3_), custom_call_target="tpu_custom_call" | custom-call | flops 1 | bytes 1 | tf_op jit(solution)/shard_map/fold/pallas_call | solution.py:264
  58.1 0.0 collective-permute-done.6.refs_3_
  58.1 1.5 %collective-permute-start.9 = (bf16[1,256,1024]{2,1,0:T(8,128)(2,1)}, bf16[1,256,1024]{2,1,0:T(8,128)(2,1)}, u32[]{:S(2)}, u32[]{:S(2)}) collective-permute-start(bf16[1,256,1024]{2,1,0:T(8,128)(2,1)} %fold.2.refs_4_), channel_id=1, source_target_pairs={{0,4},{2,6},{4,0},{6,2},{8,12},{10,14},{12,8},{14,10},{1,5},{3,7},... | collective-permute-start | bytes 1572872 | tf_op jit(solution)/shard_map/ppermute | solution.py:373
  59.5 0.0 collective-permute-done.5.refs_2_
  59.5 0.0 collective-permute-done.4.refs_1_
  59.5 4.6 %all-to-all-done = bf16[8,64,2304]{2,1,0:T(8,128)(2,1)} async-done(((bf16[8,64,2304]{2,1,0:T(8,128)(2,1)}), bf16[8,64,2304]{2,1,0:T(8,128)(2,1)}, u32[]{:S(2)}, u32[]{:S(2)}) %all-to-all-start) | async-done | bytes 2359328 | tf_op jit(solution)/shard_map/all_to_all | solution.py:377
  64.1 5.8 %latent_terms.1 = (f32[2,64,256]{2,1,0:T(8,128)}, f32[2,64,256]{2,1,0:T(8,128)}, bf16[512,512]{1,0:T(8,128)(2,1)}) custom-call(s32[1]{0:T(128)} %bitcast.4.g_ref, bf16[512,2304]{1,0:T(8,128)(2,1)} %bitcast.8.factors_ref, bf16[272,1792]{1,0:T(8,128)(2,1)} %get-tuple-element.29.after_ref.refs_0_, bf16[272,1792]{1,0:T(8,128)(2,1)} %collective-permute-done.4.refs_1_, ...), custom_call_target="tpu_custom_call" | custom-call | flops 1 | bytes 1 | tf_op jit(solution)/shard_map/latent_terms/pallas_call | solution.py:220
  69.9 0.0 collective-permute-start.11
  69.9 1.5 %collective-permute-start.12 = (f32[2,64,256]{2,1,0:T(8,128)}, f32[2,64,256]{2,1,0:T(8,128)}, u32[]{:S(2)}, u32[]{:S(2)}) collective-permute-start(f32[2,64,256]{2,1,0:T(8,128)} %get-tuple-element.39), channel_id=1, source_target_pairs={{0,16},{16,0},{1,17},{17,1},{2,18},{18,2},{3,19},{19,3},{4,20},{20... | collective-permute-start | bytes 393224 | tf_op jit(solution)/shard_map/ppermute | solution.py:414
  71.4 0.0 collective-permute-done.8.refs_1_
  71.4 0.9 collective-permute-done.10.refs_4_
  72.3 2.9 %collective-permute-done.9.refs_2_ = bf16[1,256,1024]{2,1,0:T(8,128)(2,1)} collective-permute-done((bf16[1,256,1024]{2,1,0:T(8,128)(2,1)}, bf16[1,256,1024]{2,1,0:T(8,128)(2,1)}, u32[]{:S(2)}, u32[]{:S(2)}) %collective-permute-start.9) | collective-permute-done | bytes 524320 | tf_op jit(solution)/shard_map/ppermute | solution.py:373
  75.2 0.0 collective-permute-done.11.refs_6_
  75.2 3.7 %fold.3 = (bf16[1,256,1024]{2,1,0:T(8,128)(2,1)}, bf16[1,256,1024]{2,1,0:T(8,128)(2,1)}, bf16[1024,512]{1,0:T(8,128)(2,1)}) custom-call(f32[1,256,1024]{2,1,0:T(8,128)} %get-tuple-element.32.after_ref.refs_0_, bf16[1,256,1024]{2,1,0:T(8,128)(2,1)} %collective-permute-done.8.refs_1_, bf16[1,256,1024]{2,1,0:T(8,128)(2,1)} %collective-permute-done.9.refs_2_, ...), custom_call_target="tpu_custom_call" | custom-call | flops 1 | bytes 1 | tf_op jit(solution)/shard_map/fold/pallas_call | solution.py:264
  78.9 0.0 collective-permute-done.12.after_ref
  78.9 1.6 %collective-permute-start.13 = (bf16[1024,512]{1,0:T(8,128)(2,1)}, bf16[1024,512]{1,0:T(8,128)(2,1)}, u32[]{:S(2)}, u32[]{:S(2)}) collective-permute-start(bf16[1024,512]{1,0:T(8,128)(2,1)} %relay.3.refs_0_), channel_id=1, source_target_pairs={{0,16},{16,0},{1,17},{17,1},{2,18},{18,2},{3,19},{19,3},{4,20},{20... | collective-permute-start | bytes 3145736 | tf_op jit(solution)/shard_map/ppermute | solution.py:422
  80.5 1.5 %collective-permute-start.14 = (bf16[1,256,1024]{2,1,0:T(8,128)(2,1)}, bf16[1,256,1024]{2,1,0:T(8,128)(2,1)}, u32[]{:S(2)}, u32[]{:S(2)}) collective-permute-start(bf16[1,256,1024]{2,1,0:T(8,128)(2,1)} %get-tuple-element.41), channel_id=1, source_target_pairs={{0,2},{2,0},{4,6},{6,4},{8,10},{10,8},{12,14},{14,12},{1,3},{3,1},... | collective-permute-start | bytes 1572872 | tf_op jit(solution)/shard_map/ppermute | solution.py:373
  82.0 0.0 collective-permute-start.16
  82.0 3.4 %collective-permute-start.15 = (bf16[1,256,1024]{2,1,0:T(8,128)(2,1)}, bf16[1,256,1024]{2,1,0:T(8,128)(2,1)}, u32[]{:S(2)}, u32[]{:S(2)}) collective-permute-start(bf16[1,256,1024]{2,1,0:T(8,128)(2,1)} %get-tuple-element.38.after_ref), channel_id=1, source_target_pairs={{0,8},{2,10},{4,12},{6,14},{8,0},{10,2},{12,4},{14,6},{1,9},{3,11}... | collective-permute-start | bytes 1572872 | tf_op jit(solution)/shard_map/ppermute | solution.py:373
  85.4 29.1 %conditional.1 = (f32[64,256]{1,0:T(8,128)}) conditional(s32[]{:T(128)} %convert_element_type.3, f32[2,64,256]{2,1,0:T(8,128)} %relay.2, (f32[2,64,256]{2,1,0:T(8,128)}, f32[2,64,256]{2,1,0:T(8,128)}) %tuple.11), branch_computations={%region_0.0_spmd, %region_1.0_spmd} | conditional | flops 98304 | bytes 2359464 | solution.py:433
  85.4 1.0 add.10
  86.4 0.1 collective-permute-start
  86.5 1.2 %collective-permute-done = f32[64,256]{1,0:T(8,128)S(1)} collective-permute-done((f32[64,256]{1,0:T(8,128)S(1)}, f32[64,256]{1,0:T(8,128)S(1)}, u32[]{:S(2)}, u32[]{:S(2)}) %collective-permute-start) | collective-permute-done | bytes 65568 | tf_op jit(solution)/shard_map/cond/branch_1_fun/ppermute | solution.py:426
  87.7 2.1 %collective-permute-start.1 = (f32[64,256]{1,0:T(8,128)S(1)}, f32[64,256]{1,0:T(8,128)S(1)}, u32[]{:S(2)}, u32[]{:S(2)}) collective-permute-start(f32[64,256]{1,0:T(8,128)S(1)} %fusion), channel_id=1, source_target_pairs={{0,2},{2,0},{4,6},{6,4},{8,10},{10,8},{12,14},{14,12},{1,3},{3,1},... | collective-permute-start | bytes 196616 | tf_op jit(solution)/shard_map/cond/branch_1_fun/ppermute | solution.py:373
  89.8 5.9 %collective-permute-done.1 = f32[64,256]{1,0:T(8,128)S(1)} collective-permute-done((f32[64,256]{1,0:T(8,128)S(1)}, f32[64,256]{1,0:T(8,128)S(1)}, u32[]{:S(2)}, u32[]{:S(2)}) %collective-permute-start.1) | collective-permute-done | bytes 65568 | tf_op jit(solution)/shard_map/cond/branch_1_fun/ppermute | solution.py:373
  95.7 0.1 collective-permute-start.2
  95.8 12.3 %collective-permute-done.2 = f32[64,256]{1,0:T(8,128)S(1)} collective-permute-done((f32[64,256]{1,0:T(8,128)S(1)}, f32[64,256]{1,0:T(8,128)S(1)}, u32[]{:S(2)}, u32[]{:S(2)}) %collective-permute-start.2) | collective-permute-done | bytes 65568 | tf_op jit(solution)/shard_map/cond/branch_1_fun/ppermute | solution.py:373
  108.1 1.7 %collective-permute-start.3 = (f32[64,256]{1,0:T(8,128)S(1)}, f32[64,256]{1,0:T(8,128)S(1)}, u32[]{:S(2)}, u32[]{:S(2)}) collective-permute-start(f32[64,256]{1,0:T(8,128)S(1)} %add.13), channel_id=1, source_target_pairs={{0,8},{2,10},{4,12},{6,14},{8,0},{10,2},{12,4},{14,6},{1,9},{3,11}... | collective-permute-start | bytes 196616 | tf_op jit(solution)/shard_map/cond/branch_1_fun/ppermute | solution.py:373
  109.8 4.1 %collective-permute-done.3 = f32[64,256]{1,0:T(8,128)S(1)} collective-permute-done((f32[64,256]{1,0:T(8,128)S(1)}, f32[64,256]{1,0:T(8,128)S(1)}, u32[]{:S(2)}, u32[]{:S(2)}) %collective-permute-start.3) | collective-permute-done | bytes 65568 | tf_op jit(solution)/shard_map/cond/branch_1_fun/ppermute | solution.py:373
  113.9 0.6 add.14
  114.5 0.0 collective-permute-done.14.refs_3_
  114.5 0.0 collective-permute-done.16.refs_5_
  114.5 0.0 collective-permute-done.15.refs_4_
  114.5 3.9 %finish.1 = bf16[256,1024]{1,0:T(8,128)(2,1)} custom-call(s32[1]{0:T(128)} %bitcast.3.y_ref, s32[1]{0:T(128)} %bitcast.4.g_ref, f32[64,256]{1,0:T(8,128)} %get-tuple-element.43.latent_ref, s32[1,256]{1,0:T(1,128)} %bitcast.20, bf16[1024,512]{1,0:T(8,128)(2,1)} %relay.3.refs_0_, bf16[1024,512]{1,0:T(8,128)(2,1)} %collective-permute-done.13.refs_1_, ...), custom_call_target="tpu_custom_call" | custom-call | flops 1 | bytes 1 | tf_op jit(solution)/shard_map/finish/pallas_call | solution.py:345
  (7 shorter events, 0.0 us)
Async XLA Ops:
  2.7 61.4 %all-to-all-start = ((bf16[8,64,2304]{2,1,0:T(8,128)(2,1)}), bf16[8,64,2304]{2,1,0:T(8,128)(2,1)}, u32[]{:S(2)}, u32[]{:S(2)}) async-start(bf16[8,64,2304]{2,1,0:T(8,128)(2,1)} %pack_factors.1.after_ref), calls=%async_computation | async-start | bytes 4718592 | tf_op jit(solution)/shard_map/all_to_all | solution.py:377
  13.1 45.0 %collective-permute-start.6 = (bf16[272,1792]{1,0:T(8,128)(2,1)}, bf16[272,1792]{1,0:T(8,128)(2,1)}, u32[]{:S(2)}, u32[]{:S(2)}) collective-permute-start(bf16[272,1792]{1,0:T(8,128)(2,1)} %get-tuple-element.30), channel_id=1, source_target_pairs={{0,17},{1,16},{16,1},{17,0},{2,19},{3,18},{18,3},{19,2},{4,21},{5,... | collective-permute-start | bytes 2924552 | tf_op jit(solution)/shard_map/ppermute | solution.py:382
  13.8 45.7 %collective-permute-start.5 = (bf16[272,1792]{1,0:T(8,128)(2,1)}, bf16[272,1792]{1,0:T(8,128)(2,1)}, u32[]{:S(2)}, u32[]{:S(2)}) collective-permute-start(bf16[272,1792]{1,0:T(8,128)(2,1)} %get-tuple-element.30), channel_id=1, source_target_pairs={{0,16},{16,0},{1,17},{17,1},{2,18},{18,2},{3,19},{19,3},{4,20},{20... | collective-permute-start | bytes 2924552 | tf_op jit(solution)/shard_map/ppermute | solution.py:380
  14.8 44.8 %collective-permute-start.4 = (bf16[272,1792]{1,0:T(8,128)(2,1)}, bf16[272,1792]{1,0:T(8,128)(2,1)}, u32[]{:S(2)}, u32[]{:S(2)}) collective-permute-start(bf16[272,1792]{1,0:T(8,128)(2,1)} %get-tuple-element.29.after_ref.refs_0_), channel_id=1, source_target_pairs={{0,1},{1,0},{2,3},{3,2},{4,5},{5,4},{6,7},{7,6},{8,9},{9,8},{10,11... | collective-permute-start | bytes 2924552 | tf_op jit(solution)/shard_map/ppermute | solution.py:381
  21.5 32.3 %collective-permute-start.7 = (bf16[1,256,1024]{2,1,0:T(8,128)(2,1)}, bf16[1,256,1024]{2,1,0:T(8,128)(2,1)}, u32[]{:S(2)}, u32[]{:S(2)}) collective-permute-start(bf16[1,256,1024]{2,1,0:T(8,128)(2,1)} %products.4.after_ref), channel_id=1, source_target_pairs={{0,2},{2,0},{4,6},{6,4},{8,10},{10,8},{12,14},{14,12},{1,3},{3,1},... | collective-permute-start | bytes 1572872 | tf_op jit(solution)/shard_map/ppermute | solution.py:373
  32.7 38.7 %collective-permute-start.8 = (bf16[1,256,1024]{2,1,0:T(8,128)(2,1)}, bf16[1,256,1024]{2,1,0:T(8,128)(2,1)}, u32[]{:S(2)}, u32[]{:S(2)}) collective-permute-start(bf16[1,256,1024]{2,1,0:T(8,128)(2,1)} %get-tuple-element.35), channel_id=1, source_target_pairs={{0,2},{2,0},{4,6},{6,4},{8,10},{10,8},{12,14},{14,12},{1,3},{3,1},... | collective-permute-start | bytes 1572872 | tf_op jit(solution)/shard_map/ppermute | solution.py:373
  53.8 18.5 %collective-permute-start.10 = (bf16[1,256,1024]{2,1,0:T(8,128)(2,1)}, bf16[1,256,1024]{2,1,0:T(8,128)(2,1)}, u32[]{:S(2)}, u32[]{:S(2)}) collective-permute-start(bf16[1,256,1024]{2,1,0:T(8,128)(2,1)} %get-tuple-element.36), channel_id=1, source_target_pairs={{0,2},{2,0},{4,6},{6,4},{8,10},{10,8},{12,14},{14,12},{1,3},{3,1},... | collective-permute-start | bytes 1572872 | tf_op jit(solution)/shard_map/ppermute | solution.py:373
  58.1 17.2 %collective-permute-start.9 = (bf16[1,256,1024]{2,1,0:T(8,128)(2,1)}, bf16[1,256,1024]{2,1,0:T(8,128)(2,1)}, u32[]{:S(2)}, u32[]{:S(2)}) collective-permute-start(bf16[1,256,1024]{2,1,0:T(8,128)(2,1)} %fold.2.refs_4_), channel_id=1, source_target_pairs={{0,4},{2,6},{4,0},{6,2},{8,12},{10,14},{12,8},{14,10},{1,5},{3,7},... | collective-permute-start | bytes 1572872 | tf_op jit(solution)/shard_map/ppermute | solution.py:373
  69.9 5.3 %collective-permute-start.11 = (bf16[512,512]{1,0:T(8,128)(2,1)}, bf16[512,512]{1,0:T(8,128)(2,1)}, u32[]{:S(2)}, u32[]{:S(2)}) collective-permute-start(bf16[512,512]{1,0:T(8,128)(2,1)} %get-tuple-element.37.refs_5_), channel_id=1, source_target_pairs={{0,1},{1,0},{2,3},{3,2},{4,5},{5,4},{6,7},{7,6},{8,9},{9,8},{10,11... | collective-permute-start | bytes 1572872 | tf_op jit(solution)/shard_map/ppermute | solution.py:420
  69.9 9.0 %collective-permute-start.12 = (f32[2,64,256]{2,1,0:T(8,128)}, f32[2,64,256]{2,1,0:T(8,128)}, u32[]{:S(2)}, u32[]{:S(2)}) collective-permute-start(f32[2,64,256]{2,1,0:T(8,128)} %get-tuple-element.39), channel_id=1, source_target_pairs={{0,16},{16,0},{1,17},{17,1},{2,18},{18,2},{3,19},{19,3},{4,20},{20... | collective-permute-start | bytes 393224 | tf_op jit(solution)/shard_map/ppermute | solution.py:414
  78.9 35.6 %collective-permute-start.13 = (bf16[1024,512]{1,0:T(8,128)(2,1)}, bf16[1024,512]{1,0:T(8,128)(2,1)}, u32[]{:S(2)}, u32[]{:S(2)}) collective-permute-start(bf16[1024,512]{1,0:T(8,128)(2,1)} %relay.3.refs_0_), channel_id=1, source_target_pairs={{0,16},{16,0},{1,17},{17,1},{2,18},{18,2},{3,19},{19,3},{4,20},{20... | collective-permute-start | bytes 3145736 | tf_op jit(solution)/shard_map/ppermute | solution.py:422
  80.5 34.0 %collective-permute-start.14 = (bf16[1,256,1024]{2,1,0:T(8,128)(2,1)}, bf16[1,256,1024]{2,1,0:T(8,128)(2,1)}, u32[]{:S(2)}, u32[]{:S(2)}) collective-permute-start(bf16[1,256,1024]{2,1,0:T(8,128)(2,1)} %get-tuple-element.41), channel_id=1, source_target_pairs={{0,2},{2,0},{4,6},{6,4},{8,10},{10,8},{12,14},{14,12},{1,3},{3,1},... | collective-permute-start | bytes 1572872 | tf_op jit(solution)/shard_map/ppermute | solution.py:373
  82.0 32.5 %collective-permute-start.16 = (bf16[1,256,1024]{2,1,0:T(8,128)(2,1)}, bf16[1,256,1024]{2,1,0:T(8,128)(2,1)}, u32[]{:S(2)}, u32[]{:S(2)}) collective-permute-start(bf16[1,256,1024]{2,1,0:T(8,128)(2,1)} %get-tuple-element.42), channel_id=1, source_target_pairs={{0,4},{2,6},{4,0},{6,2},{8,12},{10,14},{12,8},{14,10},{1,5},{3,7},... | collective-permute-start | bytes 1572872 | tf_op jit(solution)/shard_map/ppermute | solution.py:373
  82.0 32.5 %collective-permute-start.15 = (bf16[1,256,1024]{2,1,0:T(8,128)(2,1)}, bf16[1,256,1024]{2,1,0:T(8,128)(2,1)}, u32[]{:S(2)}, u32[]{:S(2)}) collective-permute-start(bf16[1,256,1024]{2,1,0:T(8,128)(2,1)} %get-tuple-element.38.after_ref), channel_id=1, source_target_pairs={{0,8},{2,10},{4,12},{6,14},{8,0},{10,2},{12,4},{14,6},{1,9},{3,11}... | collective-permute-start | bytes 1572872 | tf_op jit(solution)/shard_map/ppermute | solution.py:373
  86.4 1.3 %collective-permute-start = (f32[64,256]{1,0:T(8,128)S(1)}, f32[64,256]{1,0:T(8,128)S(1)}, u32[]{:S(2)}, u32[]{:S(2)}) collective-permute-start(f32[64,256]{1,0:T(8,128)S(1)} %slice_bitcast_fusion.1), channel_id=1, source_target_pairs={{0,1},{1,0},{2,3},{3,2},{4,5},{5,4},{6,7},{7,6},{8,9},{9,8},{10,11... | collective-permute-start | bytes 196616 | tf_op jit(solution)/shard_map/cond/branch_1_fun/ppermute | solution.py:426
  87.7 8.0 %collective-permute-start.1 = (f32[64,256]{1,0:T(8,128)S(1)}, f32[64,256]{1,0:T(8,128)S(1)}, u32[]{:S(2)}, u32[]{:S(2)}) collective-permute-start(f32[64,256]{1,0:T(8,128)S(1)} %fusion), channel_id=1, source_target_pairs={{0,2},{2,0},{4,6},{6,4},{8,10},{10,8},{12,14},{14,12},{1,3},{3,1},... | collective-permute-start | bytes 196616 | tf_op jit(solution)/shard_map/cond/branch_1_fun/ppermute | solution.py:373
  95.7 12.4 %collective-permute-start.2 = (f32[64,256]{1,0:T(8,128)S(1)}, f32[64,256]{1,0:T(8,128)S(1)}, u32[]{:S(2)}, u32[]{:S(2)}) collective-permute-start(f32[64,256]{1,0:T(8,128)S(1)} %add.12), channel_id=1, source_target_pairs={{0,4},{2,6},{4,0},{6,2},{8,12},{10,14},{12,8},{14,10},{1,5},{3,7},... | collective-permute-start | bytes 196616 | tf_op jit(solution)/shard_map/cond/branch_1_fun/ppermute | solution.py:373
  108.1 5.8 %collective-permute-start.3 = (f32[64,256]{1,0:T(8,128)S(1)}, f32[64,256]{1,0:T(8,128)S(1)}, u32[]{:S(2)}, u32[]{:S(2)}) collective-permute-start(f32[64,256]{1,0:T(8,128)S(1)} %add.13), channel_id=1, source_target_pairs={{0,8},{2,10},{4,12},{6,14},{8,0},{10,2},{12,4},{14,6},{1,9},{3,11}... | collective-permute-start | bytes 196616 | tf_op jit(solution)/shard_map/cond/branch_1_fun/ppermute | solution.py:373

commit v5 on v4

--- a/solution.py
+++ b/solution.py
@@ -277,20 +277,20 @@
     return outs
 
 
-def relay(array, after):
-    def kernel(array_ref, after_ref, out_ref):
-        del array_ref, after_ref, out_ref
+def relay(array, *after):
+    def kernel(*refs):
+        del refs
 
     return pl.pallas_call(
         kernel,
         name="relay",
         out_shape=jax.ShapeDtypeStruct(array.shape, array.dtype),
-        in_specs=[ANY, ANY],
+        in_specs=[ANY] * (1 + len(after)),
         out_specs=ANY,
         input_output_aliases={0: 0},
         compiler_params=PARAMS,
         cost_estimate=COST,
-    )(array, after)
+    )(array, *after)
 
 
 def finish(latent, adapter, seconds, blocks, y, g):
@@ -431,7 +431,8 @@
         return latent
 
     latent = lax.cond(t < tp, exchange, lambda near, got: near[0], relay(near, order.last), got)
-    return finish(latent, adapter, seconds, terms[0], y, g)
+    *blocks, (late, i) = terms[0]
+    return finish(latent, adapter, seconds, [*blocks, (relay(late, latent), i)], y, g)
 
 
 def solution(mesh):

time: 119 us -> 117 us (0.983)
  waiting for transfers between devices: 31.9 us -> 27.2 us
  starting transfers between devices: 26.6 us -> 29.5 us
    ppermute x10, waiting for transfers between devices: 26.1 us -> 21.4 us  [across(): return lax.ppermute(array, 'tp', [(i, i ^ step) for i in range(tp)])]
    ppermute x10, starting transfers between devices: 14.2 us -> 17.2 us  [across(): return lax.ppermute(array, 'tp', [(i, i ^ step) for i in range(tp)])]
where the time goes in v5:
time: 117 us
  Pallas kernels  58.2 us (50%)
  starting transfers between devices  29.5 us (25%)
  waiting for transfers between devices  27.2 us (23%)
  other arithmetic  1.64 us (1%)
    pallas_call x4, Pallas kernels, block_products(): pl.pallas_call(kernel, name='products', out_shape=out_shape, grid_spec=pl...  36.7 us
    ppermute x10, waiting for transfers between devices, across(): return lax.ppermute(array, 'tp', [(i, i ^ step) for i in range(tp)])  21.4 us
    ppermute x10, starting transfers between devices, across(): return lax.ppermute(array, 'tp', [(i, i ^ step) for i in range(tp)])  17.2 us
    all_to_all x1, starting transfers between devices, local(): lax.all_to_all(factors, 'tp', split_axis=0, concat_axis=0, tiled=True)  7.26 us
    pallas_call x2, Pallas kernels, fold(): pl.pallas_call(kernel, name='fold', grid=(1,), out_shape=out_shape, in_sp...  5.94 us
    pallas_call x1, Pallas kernels, latent_terms(): pl.pallas_call(kernel, name='latent_terms', out_shape=[jax.ShapeDtypeStru...  5.79 us
    all_to_all x1, waiting for transfers between devices, local(): lax.all_to_all(factors, 'tp', split_axis=0, concat_axis=0, tiled=True)  4.55 us
    pallas_call x1, Pallas kernels, finish(): pl.pallas_call(kernel, name='finish', grid=(1,), out_shape=jax.ShapeDtype...  3.91 us
  transfers between devices with their start and end apart: 18, of which 7 were waited for; matrix products, arithmetic and copies ran while one was open for 1% of the time, Pallas kernels for 44%

profile of v5, /device:TPU:0, one launch (start us, length us, event | category | flops | bytes accessed | tf_op | source)
XLA Modules:
  0.0 116.7 jit_solution(73082514001013913)
XLA Ops:
  0.0 2.7 %pack_factors.1.after_ref = bf16[8,64,2304]{2,1,0:T(8,128)(2,1)} custom-call(s32[1]{0:T(128)} %bitcast.3.y_ref, bf16[64,28672]{1,0:T(8,128)(2,1)} %bitcast.17, bf16[64,8192]{1,0:T(8,128)(2,1)} %bitcast.18), custom_call_target="tpu_custom_call" | custom-call | flops 1 | bytes 1 | tf_op jit(solution)/shard_map/pack_factors/pallas_call | solution.py:112
  2.7 7.3 %all-to-all-start = ((bf16[8,64,2304]{2,1,0:T(8,128)(2,1)}), bf16[8,64,2304]{2,1,0:T(8,128)(2,1)}, u32[]{:S(2)}, u32[]{:S(2)}) async-start(bf16[8,64,2304]{2,1,0:T(8,128)(2,1)} %pack_factors.1.after_ref), calls=%async_computation | async-start | bytes 4718592 | tf_op jit(solution)/shard_map/all_to_all | solution.py:377
  10.0 3.1 %pack_hidden.1 = (bf16[272,1792]{1,0:T(8,128)(2,1)}, bf16[272,1792]{1,0:T(8,128)(2,1)}) custom-call(s32[1]{0:T(128)} %bitcast.3.y_ref, bf16[256,3584]{1,0:T(8,128)(2,1)} %hidden_ref.9, s32[1,256]{1,0:T(1,128)} %bitcast.19, bf16[8,64,2304]{2,1,0:T(8,128)(2,1)} %pack_factors.1.after_ref), custom_call_target="tpu_custom_call" | custom-call | flops 1 | bytes 1 | tf_op jit(solution)/shard_map/pack_hidden/pallas_call | solution.py:165
  13.1 0.7 collective-permute-start.6
  13.8 0.9 collective-permute-start.5
  14.8 0.3 collective-permute-start.4
  15.0 6.5 %products.4.after_ref = bf16[1,256,1024]{2,1,0:T(8,128)(2,1)} custom-call(s32[1]{0:T(128)} %bitcast.10.t_ref, bf16[256,3584]{1,0:T(8,128)(2,1)} %hidden_ref.9, bf16[3584,8192]{1,0:T(8,128)(2,1)} %weight_ref.7, bf16[272,1792]{1,0:T(8,128)(2,1)} %get-tuple-element.29.after_ref.refs_0_), custom_call_target="tpu_custom_call" | custom-call | flops 1 | bytes 1 | tf_op jit(solution)/shard_map/products/pallas_call | solution.py:54
  21.5 2.0 %collective-permute-start.7 = (bf16[1,256,1024]{2,1,0:T(8,128)(2,1)}, bf16[1,256,1024]{2,1,0:T(8,128)(2,1)}, u32[]{:S(2)}, u32[]{:S(2)}) collective-permute-start(bf16[1,256,1024]{2,1,0:T(8,128)(2,1)} %products.4.after_ref), channel_id=1, source_target_pairs={{0,2},{2,0},{4,6},{6,4},{8,10},{10,8},{12,14},{14,12},{1,3},{3,1},... | collective-permute-start | bytes 1572872 | tf_op jit(solution)/shard_map/ppermute | solution.py:373
  23.5 9.1 %products.5 = (bf16[1,256,1024]{2,1,0:T(8,128)(2,1)}, f32[1,256,1024]{2,1,0:T(8,128)}) custom-call(s32[1]{0:T(128)} %bitcast.10.t_ref, bf16[256,3584]{1,0:T(8,128)(2,1)} %hidden_ref.9, bf16[3584,8192]{1,0:T(8,128)(2,1)} %weight_ref.7, bf16[1,256,1024]{2,1,0:T(8,128)(2,1)} %products.4.after_ref), custom_call_target="tpu_custom_call" | custom-call | flops 1 | bytes 1 | tf_op jit(solution)/shard_map/products/pallas_call | solution.py:54
  32.7 0.0 collective-permute-start.8
  32.7 9.0 %products.6 = (bf16[1,256,1024]{2,1,0:T(8,128)(2,1)}, f32[1,256,1024]{2,1,0:T(8,128)}) custom-call(s32[1]{0:T(128)} %bitcast.10.t_ref, bf16[256,3584]{1,0:T(8,128)(2,1)} %hidden_ref.9, bf16[3584,8192]{1,0:T(8,128)(2,1)} %weight_ref.7, f32[1,256,1024]{2,1,0:T(8,128)} %get-tuple-element.31.after_ref.refs_0_), custom_call_target="tpu_custom_call" | custom-call | flops 1 | bytes 1 | tf_op jit(solution)/shard_map/products/pallas_call | solution.py:54
  41.7 12.1 %products.7 = (bf16[1,256,1024]{2,1,0:T(8,128)(2,1)}, f32[2,256,1024]{2,1,0:T(8,128)}) custom-call(s32[1]{0:T(128)} %bitcast.10.t_ref, bf16[256,3584]{1,0:T(8,128)(2,1)} %hidden_ref.9, bf16[3584,8192]{1,0:T(8,128)(2,1)} %weight_ref.7, f32[1,256,1024]{2,1,0:T(8,128)} %get-tuple-element.32.after_ref.refs_0_), custom_call_target="tpu_custom_call" | custom-call | flops 1 | bytes 1 | tf_op jit(solution)/shard_map/products/pallas_call | solution.py:54
  53.8 0.0 collective-permute-done.7.refs_1_
  53.8 2.0 %collective-permute-start.10 = (bf16[1,256,1024]{2,1,0:T(8,128)(2,1)}, bf16[1,256,1024]{2,1,0:T(8,128)(2,1)}, u32[]{:S(2)}, u32[]{:S(2)}) collective-permute-start(bf16[1,256,1024]{2,1,0:T(8,128)(2,1)} %get-tuple-element.36), channel_id=1, source_target_pairs={{0,2},{2,0},{4,6},{6,4},{8,10},{10,8},{12,14},{14,12},{1,3},{3,1},... | collective-permute-start | bytes 1572872 | tf_op jit(solution)/shard_map/ppermute | solution.py:373
  55.8 2.2 %fold.2.refs_4_ = bf16[1,256,1024]{2,1,0:T(8,128)(2,1)} custom-call(f32[1,256,1024]{2,1,0:T(8,128)} %get-tuple-element.31.after_ref.refs_0_, bf16[1,256,1024]{2,1,0:T(8,128)(2,1)} %collective-permute-done.7.refs_1_, f32[2,256,1024]{2,1,0:T(8,128)} %get-tuple-element.33.refs_2_.refs_3_), custom_call_target="tpu_custom_call" | custom-call | flops 1 | bytes 1 | tf_op jit(solution)/shard_map/fold/pallas_call | solution.py:264
  58.1 0.0 collective-permute-done.6.refs_3_
  58.1 1.5 %collective-permute-start.9 = (bf16[1,256,1024]{2,1,0:T(8,128)(2,1)}, bf16[1,256,1024]{2,1,0:T(8,128)(2,1)}, u32[]{:S(2)}, u32[]{:S(2)}) collective-permute-start(bf16[1,256,1024]{2,1,0:T(8,128)(2,1)} %fold.2.refs_4_), channel_id=1, source_target_pairs={{0,4},{2,6},{4,0},{6,2},{8,12},{10,14},{12,8},{14,10},{1,5},{3,7},... | collective-permute-start | bytes 1572872 | tf_op jit(solution)/shard_map/ppermute | solution.py:373
  59.5 0.0 collective-permute-done.5.refs_2_
  59.5 0.0 collective-permute-done.4.refs_1_
  59.5 4.6 %all-to-all-done = bf16[8,64,2304]{2,1,0:T(8,128)(2,1)} async-done(((bf16[8,64,2304]{2,1,0:T(8,128)(2,1)}), bf16[8,64,2304]{2,1,0:T(8,128)(2,1)}, u32[]{:S(2)}, u32[]{:S(2)}) %all-to-all-start) | async-done | bytes 2359328 | tf_op jit(solution)/shard_map/all_to_all | solution.py:377
  64.1 5.8 %latent_terms.1 = (f32[2,64,256]{2,1,0:T(8,128)}, f32[2,64,256]{2,1,0:T(8,128)}, bf16[512,512]{1,0:T(8,128)(2,1)}) custom-call(s32[1]{0:T(128)} %bitcast.4.g_ref, bf16[512,2304]{1,0:T(8,128)(2,1)} %bitcast.8.factors_ref, bf16[272,1792]{1,0:T(8,128)(2,1)} %get-tuple-element.29.after_ref.refs_0_, bf16[272,1792]{1,0:T(8,128)(2,1)} %collective-permute-done.4.refs_1_, ...), custom_call_target="tpu_custom_call" | custom-call | flops 1 | bytes 1 | tf_op jit(solution)/shard_map/latent_terms/pallas_call | solution.py:220
  69.9 0.0 collective-permute-start.11
  69.9 1.5 %collective-permute-start.12 = (f32[2,64,256]{2,1,0:T(8,128)}, f32[2,64,256]{2,1,0:T(8,128)}, u32[]{:S(2)}, u32[]{:S(2)}) collective-permute-start(f32[2,64,256]{2,1,0:T(8,128)} %get-tuple-element.39), channel_id=1, source_target_pairs={{0,16},{16,0},{1,17},{17,1},{2,18},{18,2},{3,19},{19,3},{4,20},{20... | collective-permute-start | bytes 393224 | tf_op jit(solution)/shard_map/ppermute | solution.py:414
  71.4 0.0 collective-permute-done.8.refs_1_
  71.4 0.9 collective-permute-done.10.refs_4_
  72.3 2.9 %collective-permute-done.9.refs_2_ = bf16[1,256,1024]{2,1,0:T(8,128)(2,1)} collective-permute-done((bf16[1,256,1024]{2,1,0:T(8,128)(2,1)}, bf16[1,256,1024]{2,1,0:T(8,128)(2,1)}, u32[]{:S(2)}, u32[]{:S(2)}) %collective-permute-start.9) | collective-permute-done | bytes 524320 | tf_op jit(solution)/shard_map/ppermute | solution.py:373
  75.2 0.0 collective-permute-done.11.refs_6_
  75.2 3.7 %fold.3 = (bf16[1,256,1024]{2,1,0:T(8,128)(2,1)}, bf16[1,256,1024]{2,1,0:T(8,128)(2,1)}, bf16[1024,512]{1,0:T(8,128)(2,1)}) custom-call(f32[1,256,1024]{2,1,0:T(8,128)} %get-tuple-element.32.after_ref.refs_0_, bf16[1,256,1024]{2,1,0:T(8,128)(2,1)} %collective-permute-done.8.refs_1_, bf16[1,256,1024]{2,1,0:T(8,128)(2,1)} %collective-permute-done.9.refs_2_, ...), custom_call_target="tpu_custom_call" | custom-call | flops 1 | bytes 1 | tf_op jit(solution)/shard_map/fold/pallas_call | solution.py:264
  78.9 0.0 collective-permute-done.12.refs_1_
  78.9 1.6 %collective-permute-start.13 = (bf16[1024,512]{1,0:T(8,128)(2,1)}, bf16[1024,512]{1,0:T(8,128)(2,1)}, u32[]{:S(2)}, u32[]{:S(2)}) collective-permute-start(bf16[1024,512]{1,0:T(8,128)(2,1)} %relay.4.refs_0_), channel_id=1, source_target_pairs={{0,16},{16,0},{1,17},{17,1},{2,18},{18,2},{3,19},{19,3},{4,20},{20... | collective-permute-start | bytes 3145736 | tf_op jit(solution)/shard_map/ppermute | solution.py:422
  80.5 0.0 collective-permute-start.16
  80.5 1.5 %collective-permute-start.14 = (bf16[1,256,1024]{2,1,0:T(8,128)(2,1)}, bf16[1,256,1024]{2,1,0:T(8,128)(2,1)}, u32[]{:S(2)}, u32[]{:S(2)}) collective-permute-start(bf16[1,256,1024]{2,1,0:T(8,128)(2,1)} %get-tuple-element.41), channel_id=1, source_target_pairs={{0,2},{2,0},{4,6},{6,4},{8,10},{10,8},{12,14},{14,12},{1,3},{3,1},... | collective-permute-start | bytes 1572872 | tf_op jit(solution)/shard_map/ppermute | solution.py:373
  82.0 3.4 %collective-permute-start.15 = (bf16[1,256,1024]{2,1,0:T(8,128)(2,1)}, bf16[1,256,1024]{2,1,0:T(8,128)(2,1)}, u32[]{:S(2)}, u32[]{:S(2)}) collective-permute-start(bf16[1,256,1024]{2,1,0:T(8,128)(2,1)} %get-tuple-element.38.refs_1_), channel_id=1, source_target_pairs={{0,8},{2,10},{4,12},{6,14},{8,0},{10,2},{12,4},{14,6},{1,9},{3,11}... | collective-permute-start | bytes 1572872 | tf_op jit(solution)/shard_map/ppermute | solution.py:373
  85.4 27.4 %conditional.1 = (f32[64,256]{1,0:T(8,128)}) conditional(s32[]{:T(128)} %convert_element_type.3, f32[2,64,256]{2,1,0:T(8,128)} %relay.3, (f32[2,64,256]{2,1,0:T(8,128)}, f32[2,64,256]{2,1,0:T(8,128)}) %tuple.11), branch_computations={%region_0.0_spmd, %region_1.0_spmd} | conditional | flops 98304 | bytes 2359464 | solution.py:433
  85.4 1.0 add.10
  86.4 0.1 collective-permute-start
  86.5 1.2 %collective-permute-done = f32[64,256]{1,0:T(8,128)S(1)} collective-permute-done((f32[64,256]{1,0:T(8,128)S(1)}, f32[64,256]{1,0:T(8,128)S(1)}, u32[]{:S(2)}, u32[]{:S(2)}) %collective-permute-start) | collective-permute-done | bytes 65568 | tf_op jit(solution)/shard_map/cond/branch_1_fun/ppermute | solution.py:426
  87.7 2.1 %collective-permute-start.1 = (f32[64,256]{1,0:T(8,128)S(1)}, f32[64,256]{1,0:T(8,128)S(1)}, u32[]{:S(2)}, u32[]{:S(2)}) collective-permute-start(f32[64,256]{1,0:T(8,128)S(1)} %fusion), channel_id=1, source_target_pairs={{0,2},{2,0},{4,6},{6,4},{8,10},{10,8},{12,14},{14,12},{1,3},{3,1},... | collective-permute-start | bytes 196616 | tf_op jit(solution)/shard_map/cond/branch_1_fun/ppermute | solution.py:373
  89.8 5.9 %collective-permute-done.1 = f32[64,256]{1,0:T(8,128)S(1)} collective-permute-done((f32[64,256]{1,0:T(8,128)S(1)}, f32[64,256]{1,0:T(8,128)S(1)}, u32[]{:S(2)}, u32[]{:S(2)}) %collective-permute-start.1) | collective-permute-done | bytes 65568 | tf_op jit(solution)/shard_map/cond/branch_1_fun/ppermute | solution.py:373
  95.7 1.8 %collective-permute-start.2 = (f32[64,256]{1,0:T(8,128)S(1)}, f32[64,256]{1,0:T(8,128)S(1)}, u32[]{:S(2)}, u32[]{:S(2)}) collective-permute-start(f32[64,256]{1,0:T(8,128)S(1)} %add.12), channel_id=1, source_target_pairs={{0,4},{2,6},{4,0},{6,2},{8,12},{10,14},{12,8},{14,10},{1,5},{3,7},... | collective-permute-start | bytes 196616 | tf_op jit(solution)/shard_map/cond/branch_1_fun/ppermute | solution.py:373
  97.5 9.4 %collective-permute-done.2 = f32[64,256]{1,0:T(8,128)S(1)} collective-permute-done((f32[64,256]{1,0:T(8,128)S(1)}, f32[64,256]{1,0:T(8,128)S(1)}, u32[]{:S(2)}, u32[]{:S(2)}) %collective-permute-start.2) | collective-permute-done | bytes 65568 | tf_op jit(solution)/shard_map/cond/branch_1_fun/ppermute | solution.py:373
  106.9 2.9 %collective-permute-start.3 = (f32[64,256]{1,0:T(8,128)S(1)}, f32[64,256]{1,0:T(8,128)S(1)}, u32[]{:S(2)}, u32[]{:S(2)}) collective-permute-start(f32[64,256]{1,0:T(8,128)S(1)} %add.13), channel_id=1, source_target_pairs={{0,8},{2,10},{4,12},{6,14},{8,0},{10,2},{12,4},{14,6},{1,9},{3,11}... | collective-permute-start | bytes 196616 | tf_op jit(solution)/shard_map/cond/branch_1_fun/ppermute | solution.py:373
  109.8 2.3 %collective-permute-done.3 = f32[64,256]{1,0:T(8,128)S(1)} collective-permute-done((f32[64,256]{1,0:T(8,128)S(1)}, f32[64,256]{1,0:T(8,128)S(1)}, u32[]{:S(2)}, u32[]{:S(2)}) %collective-permute-start.3) | collective-permute-done | bytes 65568 | tf_op jit(solution)/shard_map/cond/branch_1_fun/ppermute | solution.py:373
  112.1 0.6 add.14
  112.8 0.0 collective-permute-done.16.refs_0_
  112.8 0.0 collective-permute-done.14.refs_3_
  112.8 0.0 collective-permute-done.15.refs_4_
  112.8 3.9 %finish.1 = bf16[256,1024]{1,0:T(8,128)(2,1)} custom-call(s32[1]{0:T(128)} %bitcast.3.y_ref, s32[1]{0:T(128)} %bitcast.4.g_ref, f32[64,256]{1,0:T(8,128)} %get-tuple-element.43.refs_1_.latent_ref, s32[1,256]{1,0:T(1,128)} %bitcast.20, bf16[1024,512]{1,0:T(8,128)(2,1)} %relay.4.refs_0_, bf16[1024,512]{1,0:T(8,128)(2,1)} %collective-permute-done.13.refs_1_, ...), custom_call_target="tpu_custom_call" | custom-call | flops 1 | bytes 1 | tf_op jit(solution)/shard_map/finish/pallas_call | solution.py:345
  (8 shorter events, 0.0 us)
Async XLA Ops:
  2.7 61.4 %all-to-all-start = ((bf16[8,64,2304]{2,1,0:T(8,128)(2,1)}), bf16[8,64,2304]{2,1,0:T(8,128)(2,1)}, u32[]{:S(2)}, u32[]{:S(2)}) async-start(bf16[8,64,2304]{2,1,0:T(8,128)(2,1)} %pack_factors.1.after_ref), calls=%async_computation | async-start | bytes 4718592 | tf_op jit(solution)/shard_map/all_to_all | solution.py:377
  13.1 45.0 %collective-permute-start.6 = (bf16[272,1792]{1,0:T(8,128)(2,1)}, bf16[272,1792]{1,0:T(8,128)(2,1)}, u32[]{:S(2)}, u32[]{:S(2)}) collective-permute-start(bf16[272,1792]{1,0:T(8,128)(2,1)} %get-tuple-element.30), channel_id=1, source_target_pairs={{0,17},{1,16},{16,1},{17,0},{2,19},{3,18},{18,3},{19,2},{4,21},{5,... | collective-permute-start | bytes 2924552 | tf_op jit(solution)/shard_map/ppermute | solution.py:382
  13.8 45.7 %collective-permute-start.5 = (bf16[272,1792]{1,0:T(8,128)(2,1)}, bf16[272,1792]{1,0:T(8,128)(2,1)}, u32[]{:S(2)}, u32[]{:S(2)}) collective-permute-start(bf16[272,1792]{1,0:T(8,128)(2,1)} %get-tuple-element.30), channel_id=1, source_target_pairs={{0,16},{16,0},{1,17},{17,1},{2,18},{18,2},{3,19},{19,3},{4,20},{20... | collective-permute-start | bytes 2924552 | tf_op jit(solution)/shard_map/ppermute | solution.py:380
  14.8 44.8 %collective-permute-start.4 = (bf16[272,1792]{1,0:T(8,128)(2,1)}, bf16[272,1792]{1,0:T(8,128)(2,1)}, u32[]{:S(2)}, u32[]{:S(2)}) collective-permute-start(bf16[272,1792]{1,0:T(8,128)(2,1)} %get-tuple-element.29.after_ref.refs_0_), channel_id=1, source_target_pairs={{0,1},{1,0},{2,3},{3,2},{4,5},{5,4},{6,7},{7,6},{8,9},{9,8},{10,11... | collective-permute-start | bytes 2924552 | tf_op jit(solution)/shard_map/ppermute | solution.py:381
  21.5 32.3 %collective-permute-start.7 = (bf16[1,256,1024]{2,1,0:T(8,128)(2,1)}, bf16[1,256,1024]{2,1,0:T(8,128)(2,1)}, u32[]{:S(2)}, u32[]{:S(2)}) collective-permute-start(bf16[1,256,1024]{2,1,0:T(8,128)(2,1)} %products.4.after_ref), channel_id=1, source_target_pairs={{0,2},{2,0},{4,6},{6,4},{8,10},{10,8},{12,14},{14,12},{1,3},{3,1},... | collective-permute-start | bytes 1572872 | tf_op jit(solution)/shard_map/ppermute | solution.py:373
  32.7 38.7 %collective-permute-start.8 = (bf16[1,256,1024]{2,1,0:T(8,128)(2,1)}, bf16[1,256,1024]{2,1,0:T(8,128)(2,1)}, u32[]{:S(2)}, u32[]{:S(2)}) collective-permute-start(bf16[1,256,1024]{2,1,0:T(8,128)(2,1)} %get-tuple-element.35), channel_id=1, source_target_pairs={{0,2},{2,0},{4,6},{6,4},{8,10},{10,8},{12,14},{14,12},{1,3},{3,1},... | collective-permute-start | bytes 1572872 | tf_op jit(solution)/shard_map/ppermute | solution.py:373
  53.8 18.5 %collective-permute-start.10 = (bf16[1,256,1024]{2,1,0:T(8,128)(2,1)}, bf16[1,256,1024]{2,1,0:T(8,128)(2,1)}, u32[]{:S(2)}, u32[]{:S(2)}) collective-permute-start(bf16[1,256,1024]{2,1,0:T(8,128)(2,1)} %get-tuple-element.36), channel_id=1, source_target_pairs={{0,2},{2,0},{4,6},{6,4},{8,10},{10,8},{12,14},{14,12},{1,3},{3,1},... | collective-permute-start | bytes 1572872 | tf_op jit(solution)/shard_map/ppermute | solution.py:373
  58.1 17.2 %collective-permute-start.9 = (bf16[1,256,1024]{2,1,0:T(8,128)(2,1)}, bf16[1,256,1024]{2,1,0:T(8,128)(2,1)}, u32[]{:S(2)}, u32[]{:S(2)}) collective-permute-start(bf16[1,256,1024]{2,1,0:T(8,128)(2,1)} %fold.2.refs_4_), channel_id=1, source_target_pairs={{0,4},{2,6},{4,0},{6,2},{8,12},{10,14},{12,8},{14,10},{1,5},{3,7},... | collective-permute-start | bytes 1572872 | tf_op jit(solution)/shard_map/ppermute | solution.py:373
  69.9 5.3 %collective-permute-start.11 = (bf16[512,512]{1,0:T(8,128)(2,1)}, bf16[512,512]{1,0:T(8,128)(2,1)}, u32[]{:S(2)}, u32[]{:S(2)}) collective-permute-start(bf16[512,512]{1,0:T(8,128)(2,1)} %get-tuple-element.37.refs_5_), channel_id=1, source_target_pairs={{0,1},{1,0},{2,3},{3,2},{4,5},{5,4},{6,7},{7,6},{8,9},{9,8},{10,11... | collective-permute-start | bytes 1572872 | tf_op jit(solution)/shard_map/ppermute | solution.py:420
  69.9 9.0 %collective-permute-start.12 = (f32[2,64,256]{2,1,0:T(8,128)}, f32[2,64,256]{2,1,0:T(8,128)}, u32[]{:S(2)}, u32[]{:S(2)}) collective-permute-start(f32[2,64,256]{2,1,0:T(8,128)} %get-tuple-element.39), channel_id=1, source_target_pairs={{0,16},{16,0},{1,17},{17,1},{2,18},{18,2},{3,19},{19,3},{4,20},{20... | collective-permute-start | bytes 393224 | tf_op jit(solution)/shard_map/ppermute | solution.py:414
  78.9 33.9 %collective-permute-start.13 = (bf16[1024,512]{1,0:T(8,128)(2,1)}, bf16[1024,512]{1,0:T(8,128)(2,1)}, u32[]{:S(2)}, u32[]{:S(2)}) collective-permute-start(bf16[1024,512]{1,0:T(8,128)(2,1)} %relay.4.refs_0_), channel_id=1, source_target_pairs={{0,16},{16,0},{1,17},{17,1},{2,18},{18,2},{3,19},{19,3},{4,20},{20... | collective-permute-start | bytes 3145736 | tf_op jit(solution)/shard_map/ppermute | solution.py:422
  80.5 32.3 %collective-permute-start.16 = (bf16[1,256,1024]{2,1,0:T(8,128)(2,1)}, bf16[1,256,1024]{2,1,0:T(8,128)(2,1)}, u32[]{:S(2)}, u32[]{:S(2)}) collective-permute-start(bf16[1,256,1024]{2,1,0:T(8,128)(2,1)} %get-tuple-element.42), channel_id=1, source_target_pairs={{0,4},{2,6},{4,0},{6,2},{8,12},{10,14},{12,8},{14,10},{1,5},{3,7},... | collective-permute-start | bytes 1572872 | tf_op jit(solution)/shard_map/ppermute | solution.py:373
  80.5 32.3 %collective-permute-start.14 = (bf16[1,256,1024]{2,1,0:T(8,128)(2,1)}, bf16[1,256,1024]{2,1,0:T(8,128)(2,1)}, u32[]{:S(2)}, u32[]{:S(2)}) collective-permute-start(bf16[1,256,1024]{2,1,0:T(8,128)(2,1)} %get-tuple-element.41), channel_id=1, source_target_pairs={{0,2},{2,0},{4,6},{6,4},{8,10},{10,8},{12,14},{14,12},{1,3},{3,1},... | collective-permute-start | bytes 1572872 | tf_op jit(solution)/shard_map/ppermute | solution.py:373
  82.0 30.8 %collective-permute-start.15 = (bf16[1,256,1024]{2,1,0:T(8,128)(2,1)}, bf16[1,256,1024]{2,1,0:T(8,128)(2,1)}, u32[]{:S(2)}, u32[]{:S(2)}) collective-permute-start(bf16[1,256,1024]{2,1,0:T(8,128)(2,1)} %get-tuple-element.38.refs_1_), channel_id=1, source_target_pairs={{0,8},{2,10},{4,12},{6,14},{8,0},{10,2},{12,4},{14,6},{1,9},{3,11}... | collective-permute-start | bytes 1572872 | tf_op jit(solution)/shard_map/ppermute | solution.py:373
  86.4 1.3 %collective-permute-start = (f32[64,256]{1,0:T(8,128)S(1)}, f32[64,256]{1,0:T(8,128)S(1)}, u32[]{:S(2)}, u32[]{:S(2)}) collective-permute-start(f32[64,256]{1,0:T(8,128)S(1)} %slice_bitcast_fusion.1), channel_id=1, source_target_pairs={{0,1},{1,0},{2,3},{3,2},{4,5},{5,4},{6,7},{7,6},{8,9},{9,8},{10,11... | collective-permute-start | bytes 196616 | tf_op jit(solution)/shard_map/cond/branch_1_fun/ppermute | solution.py:426
  87.7 8.0 %collective-permute-start.1 = (f32[64,256]{1,0:T(8,128)S(1)}, f32[64,256]{1,0:T(8,128)S(1)}, u32[]{:S(2)}, u32[]{:S(2)}) collective-permute-start(f32[64,256]{1,0:T(8,128)S(1)} %fusion), channel_id=1, source_target_pairs={{0,2},{2,0},{4,6},{6,4},{8,10},{10,8},{12,14},{14,12},{1,3},{3,1},... | collective-permute-start | bytes 196616 | tf_op jit(solution)/shard_map/cond/branch_1_fun/ppermute | solution.py:373
  95.7 11.2 %collective-permute-start.2 = (f32[64,256]{1,0:T(8,128)S(1)}, f32[64,256]{1,0:T(8,128)S(1)}, u32[]{:S(2)}, u32[]{:S(2)}) collective-permute-start(f32[64,256]{1,0:T(8,128)S(1)} %add.12), channel_id=1, source_target_pairs={{0,4},{2,6},{4,0},{6,2},{8,12},{10,14},{12,8},{14,10},{1,5},{3,7},... | collective-permute-start | bytes 196616 | tf_op jit(solution)/shard_map/cond/branch_1_fun/ppermute | solution.py:373
  106.9 5.2 %collective-permute-start.3 = (f32[64,256]{1,0:T(8,128)S(1)}, f32[64,256]{1,0:T(8,128)S(1)}, u32[]{:S(2)}, u32[]{:S(2)}) collective-permute-start(f32[64,256]{1,0:T(8,128)S(1)} %add.13), channel_id=1, source_target_pairs={{0,8},{2,10},{4,12},{6,14},{8,0},{10,2},{12,4},{14,6},{1,9},{3,11}... | collective-permute-start | bytes 196616 | tf_op jit(solution)/shard_map/cond/branch_1_fun/ppermute | solution.py:373

commit v6 on v5

--- a/solution.py
+++ b/solution.py
@@ -296,17 +296,13 @@
 def finish(latent, adapter, seconds, blocks, y, g):
     rows, columns = blocks[0][0].shape[1:]
     rank = latent.shape[0]
-    tp = seconds[0].shape[0] // (2 * rank)
+    tp = seconds[0].shape[0] // rank
     half = columns // 2
 
     def spread(held, ids, core):
         held = held.astype(jnp.bfloat16).astype(jnp.float32)
         return jnp.concatenate(
-            [
-                jnp.where(ids == place * 2 + which, held, jnp.zeros_like(held))
-                for which in (core, 1 - core)
-                for place in range(tp)
-            ],
+            [jnp.where(ids == place * 2 + core, held, jnp.zeros_like(held)) for place in range(tp)],
             axis=0,
         ).astype(jnp.bfloat16)
 
@@ -316,8 +312,9 @@
         )
 
     if half % 128:
-        wide = spread(latent, adapter, g)
-        mine, other = product(wide, seconds[0]), product(wide, seconds[1])
+        near, far = spread(latent, adapter, g), spread(latent, adapter, 1 - g)
+        mine = product(near, seconds[0]) + product(far, seconds[1])
+        other = product(near, seconds[2]) + product(far, seconds[3])
         delta = jnp.where(
             y == 0,
             jnp.concatenate([mine, other], axis=1),
@@ -329,12 +326,14 @@
         return total.astype(jnp.bfloat16)
 
     def kernel(y_ref, g_ref, latent_ref, adapter_ref, *refs):
-        second_refs, block_refs, out_ref = refs[:2], refs[2:-1], refs[-1]
-        wide = spread(latent_ref[...], adapter_ref[...], g_ref[0])
+        second_refs, block_refs, out_ref = refs[:4], refs[4:-1], refs[-1]
+        near = spread(latent_ref[...], adapter_ref[...], g_ref[0])
+        far = spread(latent_ref[...], adapter_ref[...], 1 - g_ref[0])
         for which in range(2):
             index = y_ref[0] if which == 0 else 1 - y_ref[0]
             lanes = pl.ds(pl.multiple_of(index * half, 128), half)
-            delta = product(wide, second_refs[which][...])
+            delta = product(near, second_refs[2 * which][...])
+            delta += product(far, second_refs[2 * which + 1][...])
             total = block_refs[0][0, :, lanes]
             for block_ref in block_refs[1:]:
                 total += block_ref[0, :, lanes].astype(jnp.float32)
@@ -414,25 +413,39 @@
     got = lax.ppermute(away, "rep", SWAP)
     rest = [stages[0][1:], *stages[1:]]
     if tp <= 8:
-        rest = [[item for items in reversed(rest) for item in items]]
-    for items in rest[:-1]:
+        rest = [[item] for items in reversed(rest) for item in items]
+    for items in rest:
         pass_on(items)
-    second = pass_on(rest[-1], (second, lax.ppermute(second, "grp", SWAP)))
-    second = relay(second, got)
-    seconds = [second, lax.ppermute(second, "rep", SWAP)]
-
-    def exchange(near, got):
+
+    def inner(near, got):
         held = near + got
         latent = held[0] + lax.ppermute(held[1], "grp", SWAP)
         step = 1
-        while step < tp:
+        while 4 * step < tp:
             latent = latent + across(latent, step)
             step *= 2
         return latent
 
-    latent = lax.cond(t < tp, exchange, lambda near, got: near[0], relay(near, order.last), got)
-    *blocks, (late, i) = terms[0]
-    return finish(latent, adapter, seconds, [*blocks, (relay(late, latent), i)], y, g)
+    def outer(latent):
+        step = tp // 4
+        sent = latent.astype(jnp.bfloat16)
+        for i in range(1, 4):
+            latent = latent + across(sent, i * step).astype(jnp.float32)
+        return latent
+
+    def swap(*arrays):
+        return [lax.ppermute(array, "grp", SWAP) for array in arrays]
+
+    latent = lax.cond(t < tp, inner, lambda near, got: near[0], relay(near, order.last), got)
+    kept, (r, i), (late, k), *others = terms[0]
+    r = relay(r, latent)
+    second = relay(second, got)
+    second_other = relay(lax.ppermute(second, "rep", SWAP), r)
+    twins = lax.cond(t < tp, swap, lambda *arrays: list(arrays), second, second_other)
+    latent = lax.cond(t < tp, outer, lambda latent: latent, relay(latent, twins[1]))
+    seconds = [second, twins[0], second_other, twins[1]]
+    blocks = [kept, (r, i), (relay(late, latent), k), *others]
+    return finish(latent, adapter, seconds, blocks, y, g)
 
 
 def solution(mesh):

time: 117 us -> 114 us (0.974)
  waiting for transfers between devices: 27.2 us -> 22.3 us
  other arithmetic: 1.64 us -> 3.98 us
  starting transfers between devices: 29.5 us -> 28.2 us
    ppermute x10 -> x11, waiting for transfers between devices: 21.4 us -> 11.8 us  [across(): return lax.ppermute(array, 'tp', [(i, i ^ step) for i in range(tp)])]
    ppermute x3 -> x4, waiting for transfers between devices: 1.25 us -> 3.73 us  [the longest x2 2.49 us: swap(): return [lax.ppermute(array, 'grp', SWAP) for array in arrays]]
    ppermute x1, waiting for transfers between devices: 0.01 us -> 2.31 us  [local(): got = lax.ppermute(away, 'rep', SWAP)]
    ppermute x10 -> x11, starting transfers between devices: 17.2 us -> 15.3 us  [across(): return lax.ppermute(array, 'tp', [(i, i ^ step) for i in range(tp)])]
    add x5 -> x4, other arithmetic: 1.64 us -> 3.13 us  [the longest x1 1.49 us: outer(): latent = latent + across(sent, i * step).astype(jnp.float32)]
    pallas_call x2 -> x3, Pallas kernels: 5.94 us -> 6.97 us  [fold(): pl.pallas_call(kernel, name='fold', grid=(1,), out_shape=out_shape, in_sp...]
  transfers between devices with their start and end apart: 18 -> 20, of which waited for: 7 -> 9; matrix products, arithmetic and copies ran while one was open for 1% -> 4% of each run, Pallas kernels for 44% -> 46%
where the time goes in v6:
time: 114 us
  Pallas kernels  59.2 us (52%)
  starting transfers between devices  28.2 us (25%)
  waiting for transfers between devices  22.3 us (20%)
  other arithmetic  3.98 us (3%)
    pallas_call x4, Pallas kernels, block_products(): pl.pallas_call(kernel, name='products', out_shape=out_shape, grid_spec=pl...  36.8 us
    ppermute x11, starting transfers between devices, across(): return lax.ppermute(array, 'tp', [(i, i ^ step) for i in range(tp)])  15.3 us
    ppermute x11, waiting for transfers between devices, across(): return lax.ppermute(array, 'tp', [(i, i ^ step) for i in range(tp)])  11.8 us
    all_to_all x1, starting transfers between devices, local(): lax.all_to_all(factors, 'tp', split_axis=0, concat_axis=0, tiled=True)  7.26 us
    pallas_call x3, Pallas kernels, fold(): pl.pallas_call(kernel, name='fold', grid=(1,), out_shape=out_shape, in_sp...  6.97 us
    pallas_call x1, Pallas kernels, latent_terms(): pl.pallas_call(kernel, name='latent_terms', out_shape=[jax.ShapeDtypeStru...  5.74 us
    all_to_all x1, waiting for transfers between devices, local(): lax.all_to_all(factors, 'tp', split_axis=0, concat_axis=0, tiled=True)  4.49 us
    pallas_call x1, Pallas kernels, finish(): pl.pallas_call(kernel, name='finish', grid=(1,), out_shape=jax.ShapeDtype...  3.92 us
  transfers between devices with their start and end apart: 20, of which 9 were waited for; matrix products, arithmetic and copies ran while one was open for 4% of the time, Pallas kernels for 46%

profile of v6, /device:TPU:0, one launch (start us, length us, event | category | flops | bytes accessed | tf_op | source)
XLA Modules:
  0.0 113.8 jit_solution(13061765384039494597)
XLA Ops:
  0.0 2.7 %pack_factors.1.after_ref = bf16[8,64,2304]{2,1,0:T(8,128)(2,1)} custom-call(s32[1]{0:T(128)} %bitcast.3.y_ref, bf16[64,28672]{1,0:T(8,128)(2,1)} %bitcast.17, bf16[64,8192]{1,0:T(8,128)(2,1)} %bitcast.18), custom_call_target="tpu_custom_call" | custom-call | flops 1 | bytes 1 | tf_op jit(solution)/shard_map/pack_factors/pallas_call | solution.py:112
  2.7 7.3 %all-to-all-start = ((bf16[8,64,2304]{2,1,0:T(8,128)(2,1)}), bf16[8,64,2304]{2,1,0:T(8,128)(2,1)}, u32[]{:S(2)}, u32[]{:S(2)}) async-start(bf16[8,64,2304]{2,1,0:T(8,128)(2,1)} %pack_factors.1.after_ref), calls=%async_computation | async-start | bytes 4718592 | tf_op jit(solution)/shard_map/all_to_all | solution.py:376
  10.0 3.1 %pack_hidden.1 = (bf16[272,1792]{1,0:T(8,128)(2,1)}, bf16[272,1792]{1,0:T(8,128)(2,1)}) custom-call(s32[1]{0:T(128)} %bitcast.3.y_ref, bf16[256,3584]{1,0:T(8,128)(2,1)} %hidden_ref.9, s32[1,256]{1,0:T(1,128)} %bitcast.19, bf16[8,64,2304]{2,1,0:T(8,128)(2,1)} %pack_factors.1.after_ref), custom_call_target="tpu_custom_call" | custom-call | flops 1 | bytes 1 | tf_op jit(solution)/shard_map/pack_hidden/pallas_call | solution.py:165
  13.1 0.7 collective-permute-start.9
  13.8 0.9 collective-permute-start.8
  14.8 0.3 collective-permute-start.7
  15.0 6.5 %products.4.after_ref = bf16[1,256,1024]{2,1,0:T(8,128)(2,1)} custom-call(s32[1]{0:T(128)} %bitcast.10.t_ref, bf16[256,3584]{1,0:T(8,128)(2,1)} %hidden_ref.9, bf16[3584,8192]{1,0:T(8,128)(2,1)} %weight_ref.7, bf16[272,1792]{1,0:T(8,128)(2,1)} %get-tuple-element.43.after_ref.refs_0_), custom_call_target="tpu_custom_call" | custom-call | flops 1 | bytes 1 | tf_op jit(solution)/shard_map/products/pallas_call | solution.py:54
  21.5 2.0 %collective-permute-start.10 = (bf16[1,256,1024]{2,1,0:T(8,128)(2,1)}, bf16[1,256,1024]{2,1,0:T(8,128)(2,1)}, u32[]{:S(2)}, u32[]{:S(2)}) collective-permute-start(bf16[1,256,1024]{2,1,0:T(8,128)(2,1)} %products.4.after_ref), channel_id=1, source_target_pairs={{0,2},{2,0},{4,6},{6,4},{8,10},{10,8},{12,14},{14,12},{1,3},{3,1},... | collective-permute-start | bytes 1572872 | tf_op jit(solution)/shard_map/ppermute | solution.py:372
  23.5 9.1 %products.5 = (bf16[1,256,1024]{2,1,0:T(8,128)(2,1)}, f32[1,256,1024]{2,1,0:T(8,128)}) custom-call(s32[1]{0:T(128)} %bitcast.10.t_ref, bf16[256,3584]{1,0:T(8,128)(2,1)} %hidden_ref.9, bf16[3584,8192]{1,0:T(8,128)(2,1)} %weight_ref.7, bf16[1,256,1024]{2,1,0:T(8,128)(2,1)} %products.4.after_ref), custom_call_target="tpu_custom_call" | custom-call | flops 1 | bytes 1 | tf_op jit(solution)/shard_map/products/pallas_call | solution.py:54
  32.7 0.0 collective-permute-start.12
  32.7 9.0 %products.6 = (bf16[1,256,1024]{2,1,0:T(8,128)(2,1)}, f32[1,256,1024]{2,1,0:T(8,128)}) custom-call(s32[1]{0:T(128)} %bitcast.10.t_ref, bf16[256,3584]{1,0:T(8,128)(2,1)} %hidden_ref.9, bf16[3584,8192]{1,0:T(8,128)(2,1)} %weight_ref.7, f32[1,256,1024]{2,1,0:T(8,128)} %get-tuple-element.45.after_ref.refs_0_), custom_call_target="tpu_custom_call" | custom-call | flops 1 | bytes 1 | tf_op jit(solution)/shard_map/products/pallas_call | solution.py:54
  41.8 12.1 %products.7 = (bf16[1,256,1024]{2,1,0:T(8,128)(2,1)}, f32[2,256,1024]{2,1,0:T(8,128)}) custom-call(s32[1]{0:T(128)} %bitcast.10.t_ref, bf16[256,3584]{1,0:T(8,128)(2,1)} %hidden_ref.9, bf16[3584,8192]{1,0:T(8,128)(2,1)} %weight_ref.7, f32[1,256,1024]{2,1,0:T(8,128)} %get-tuple-element.46.after_ref.refs_0_), custom_call_target="tpu_custom_call" | custom-call | flops 1 | bytes 1 | tf_op jit(solution)/shard_map/products/pallas_call | solution.py:54
  53.9 2.2 %fold.3.refs_4_ = bf16[1,256,1024]{2,1,0:T(8,128)(2,1)} custom-call(f32[1,256,1024]{2,1,0:T(8,128)} %get-tuple-element.45.after_ref.refs_0_, bf16[1,256,1024]{2,1,0:T(8,128)(2,1)} %collective-permute-done.10.refs_1_, f32[2,256,1024]{2,1,0:T(8,128)} %get-tuple-element.47.refs_2_.refs_0_.refs_4_), custom_call_target="tpu_custom_call" | custom-call | flops 1 | bytes 1 | tf_op jit(solution)/shard_map/fold/pallas_call | solution.py:264
  56.1 2.0 %collective-permute-start.13 = (bf16[1,256,1024]{2,1,0:T(8,128)(2,1)}, bf16[1,256,1024]{2,1,0:T(8,128)(2,1)}, u32[]{:S(2)}, u32[]{:S(2)}) collective-permute-start(bf16[1,256,1024]{2,1,0:T(8,128)(2,1)} %fold.3.refs_4_), channel_id=1, source_target_pairs={{0,4},{2,6},{4,0},{6,2},{8,12},{10,14},{12,8},{14,10},{1,5},{3,7},... | collective-permute-start | bytes 1572872 | tf_op jit(solution)/shard_map/ppermute | solution.py:372
  58.1 1.5 %collective-permute-start.11 = (bf16[1,256,1024]{2,1,0:T(8,128)(2,1)}, bf16[1,256,1024]{2,1,0:T(8,128)(2,1)}, u32[]{:S(2)}, u32[]{:S(2)}) collective-permute-start(bf16[1,256,1024]{2,1,0:T(8,128)(2,1)} %get-tuple-element.49), channel_id=1, source_target_pairs={{0,2},{2,0},{4,6},{6,4},{8,10},{10,8},{12,14},{14,12},{1,3},{3,1},... | collective-permute-start | bytes 1572872 | tf_op jit(solution)/shard_map/ppermute | solution.py:372
  59.6 0.0 collective-permute-done.8.refs_2_
  59.6 0.0 collective-permute-done.7.refs_1_
  59.6 4.5 %all-to-all-done = bf16[8,64,2304]{2,1,0:T(8,128)(2,1)} async-done(((bf16[8,64,2304]{2,1,0:T(8,128)(2,1)}), bf16[8,64,2304]{2,1,0:T(8,128)(2,1)}, u32[]{:S(2)}, u32[]{:S(2)}) %all-to-all-start) | async-done | bytes 2359328 | tf_op jit(solution)/shard_map/all_to_all | solution.py:376
  64.1 5.7 %latent_terms.1 = (f32[2,64,256]{2,1,0:T(8,128)}, f32[2,64,256]{2,1,0:T(8,128)}, bf16[512,512]{1,0:T(8,128)(2,1)}) custom-call(s32[1]{0:T(128)} %bitcast.4.g_ref, bf16[512,2304]{1,0:T(8,128)(2,1)} %bitcast.8.factors_ref, bf16[272,1792]{1,0:T(8,128)(2,1)} %get-tuple-element.43.after_ref.refs_0_, bf16[272,1792]{1,0:T(8,128)(2,1)} %collective-permute-done.7.refs_1_, ...), custom_call_target="tpu_custom_call" | custom-call | flops 1 | bytes 1 | tf_op jit(solution)/shard_map/latent_terms/pallas_call | solution.py:220
  69.8 1.5 %collective-permute-start.14 = (f32[2,64,256]{2,1,0:T(8,128)}, f32[2,64,256]{2,1,0:T(8,128)}, u32[]{:S(2)}, u32[]{:S(2)}) collective-permute-start(f32[2,64,256]{2,1,0:T(8,128)} %get-tuple-element.51), channel_id=1, source_target_pairs={{0,16},{16,0},{1,17},{17,1},{2,18},{18,2},{3,19},{19,3},{4,20},{20... | collective-permute-start | bytes 393224 | tf_op jit(solution)/shard_map/ppermute | solution.py:413
  71.3 1.5 %collective-permute-start.16 = (bf16[1,256,1024]{2,1,0:T(8,128)(2,1)}, bf16[1,256,1024]{2,1,0:T(8,128)(2,1)}, u32[]{:S(2)}, u32[]{:S(2)}) collective-permute-start(bf16[1,256,1024]{2,1,0:T(8,128)(2,1)} %get-tuple-element.53), channel_id=1, source_target_pairs={{0,2},{2,0},{4,6},{6,4},{8,10},{10,8},{12,14},{14,12},{1,3},{3,1},... | collective-permute-start | bytes 1572872 | tf_op jit(solution)/shard_map/ppermute | solution.py:372
  72.8 2.3 %collective-permute-done.14.refs_1_ = f32[2,64,256]{2,1,0:T(8,128)} collective-permute-done((f32[2,64,256]{2,1,0:T(8,128)}, f32[2,64,256]{2,1,0:T(8,128)}, u32[]{:S(2)}, u32[]{:S(2)}) %collective-permute-start.14) | collective-permute-done | bytes 131104 | tf_op jit(solution)/shard_map/ppermute | solution.py:413
  75.1 1.5 %collective-permute-start.15 = (bf16[512,512]{1,0:T(8,128)(2,1)}, bf16[512,512]{1,0:T(8,128)(2,1)}, u32[]{:S(2)}, u32[]{:S(2)}) collective-permute-start(bf16[512,512]{1,0:T(8,128)(2,1)} %relay.7.refs_0_), channel_id=1, source_target_pairs={{0,16},{16,0},{1,17},{17,1},{2,18},{18,2},{3,19},{19,3},{4,20},{20... | collective-permute-start | bytes 1572872 | tf_op jit(solution)/shard_map/ppermute | solution.py:443
  76.6 2.5 %fold.4.refs_2_ = bf16[1,256,1024]{2,1,0:T(8,128)(2,1)} custom-call(f32[1,256,1024]{2,1,0:T(8,128)} %get-tuple-element.46.after_ref.refs_0_, bf16[1,256,1024]{2,1,0:T(8,128)(2,1)} %collective-permute-done.12.refs_1_, bf16[1,256,1024]{2,1,0:T(8,128)(2,1)} %collective-permute-done.13.refs_2_, f32[2,64,256]{2,1,0:T(8,128)} %get-tuple-element.48.refs_3_.refs_0_), custom_call_target="tpu_custom_call" | custom-call | flops 1 | bytes 1 | tf_op jit(solution)/shard_map/fold/pallas_call | solution.py:264
  79.1 2.3 %fold.5.refs_1_ = bf16[1,256,1024]{2,1,0:T(8,128)(2,1)} custom-call(f32[2,256,1024]{2,1,0:T(8,128)} %get-tuple-element.47.refs_2_.refs_0_.refs_4_, bf16[1,256,1024]{2,1,0:T(8,128)(2,1)} %collective-permute-done.11.refs_1_, bf16[1,256,1024]{2,1,0:T(8,128)(2,1)} %fold.4.refs_2_), custom_call_target="tpu_custom_call" | custom-call | flops 1 | bytes 1 | tf_op jit(solution)/shard_map/fold/pallas_call | solution.py:264
  81.4 3.2 %collective-permute-start.18 = (bf16[1,256,1024]{2,1,0:T(8,128)(2,1)}, bf16[1,256,1024]{2,1,0:T(8,128)(2,1)}, u32[]{:S(2)}, u32[]{:S(2)}) collective-permute-start(bf16[1,256,1024]{2,1,0:T(8,128)(2,1)} %fold.5.refs_1_), channel_id=1, source_target_pairs={{0,4},{2,6},{4,0},{6,2},{8,12},{10,14},{12,8},{14,10},{1,5},{3,7},... | collective-permute-start | bytes 1572872 | tf_op jit(solution)/shard_map/ppermute | solution.py:372
  84.6 7.3 %conditional.3 = (f32[64,256]{1,0:T(8,128)}) conditional(s32[]{:T(128)} %convert_element_type.17, f32[2,64,256]{2,1,0:T(8,128)} %relay.6, (f32[2,64,256]{2,1,0:T(8,128)}, f32[2,64,256]{2,1,0:T(8,128)}) %tuple.24), branch_computations={%region_0.0_spmd, %region_1.0_spmd} | conditional | flops 65536 | bytes 1441880 | solution.py:439
  84.6 1.0 add.12
  85.6 0.1 collective-permute-start.2
  85.7 1.2 %collective-permute-done.2 = f32[64,256]{1,0:T(8,128)S(1)} collective-permute-done((f32[64,256]{1,0:T(8,128)S(1)}, f32[64,256]{1,0:T(8,128)S(1)}, u32[]{:S(2)}, u32[]{:S(2)}) %collective-permute-start.2) | collective-permute-done | bytes 65568 | tf_op jit(solution)/shard_map/cond/branch_1_fun/ppermute | solution.py:422
  86.9 0.8 collective-permute-start.3
  87.7 3.6 %collective-permute-done.3 = f32[64,256]{1,0:T(8,128)S(1)} collective-permute-done((f32[64,256]{1,0:T(8,128)S(1)}, f32[64,256]{1,0:T(8,128)S(1)}, u32[]{:S(2)}, u32[]{:S(2)}) %collective-permute-start.3) | collective-permute-done | bytes 65568 | tf_op jit(solution)/shard_map/cond/branch_1_fun/ppermute | solution.py:372
  91.2 0.6 add.14
  91.9 3.1 %conditional.4 = (bf16[512,512]{1,0:T(8,128)(2,1)}, bf16[512,512]{1,0:T(8,128)(2,1)}) conditional(s32[]{:T(128)} %convert_element_type.17, (bf16[512,512]{1,0:T(8,128)(2,1)}, bf16[512,512]{1,0:T(8,128)(2,1)}) %tuple.25, (bf16[512,512]{1,0:T(8,128)(2,1)}, bf16[512,512]{1,0:T(8,128)(2,1)}) %tuple.25), branch_computations={%region_2.0_spmd, %region_3.0_spmd} | conditional | bytes 4194400 | solution.py:444
  91.9 0.1 collective-permute-start
  92.0 0.5 collective-permute-start.1
  92.5 1.7 %collective-permute-done = bf16[512,512]{1,0:T(8,128)(2,1)} collective-permute-done((bf16[512,512]{1,0:T(8,128)(2,1)}, bf16[512,512]{1,0:T(8,128)(2,1)}, u32[]{:S(2)}, u32[]{:S(2)}) %collective-permute-start) | collective-permute-done | bytes 524320 | tf_op jit(solution)/shard_map/cond/branch_1_fun/ppermute | solution.py:437
  94.2 0.7 collective-permute-done.1
  95.0 14.9 %conditional.5 = (f32[64,256]{1,0:T(8,128)}) conditional(s32[]{:T(128)} %convert_element_type.17, f32[64,256]{1,0:T(8,128)} %relay.10, f32[64,256]{1,0:T(8,128)} %relay.10), branch_computations={%region_4.0_spmd, %region_5.0_spmd} | conditional | flops 114688 | bytes 721024 | solution.py:445
  95.0 0.8 convert_element_type.3
  95.8 1.2 %collective-permute-start.6 = (bf16[64,256]{1,0:T(8,128)(2,1)S(1)}, bf16[64,256]{1,0:T(8,128)(2,1)S(1)}, u32[]{:S(2)}, u32[]{:S(2)}) collective-permute-start(bf16[64,256]{1,0:T(8,128)(2,1)S(1)} %convert_element_type.3), channel_id=1, source_target_pairs={{0,12},{2,14},{4,8},{6,10},{8,4},{10,6},{12,0},{14,2},{1,13},{3,15... | collective-permute-start | bytes 98312 | tf_op jit(solution)/shard_map/cond/branch_1_fun/ppermute | solution.py:372
  97.0 0.3 collective-permute-start.5
  97.3 2.9 %collective-permute-start.4 = (bf16[64,256]{1,0:T(8,128)(2,1)S(1)}, bf16[64,256]{1,0:T(8,128)(2,1)S(1)}, u32[]{:S(2)}, u32[]{:S(2)}) collective-permute-start(bf16[64,256]{1,0:T(8,128)(2,1)S(1)} %convert_element_type.3), channel_id=1, source_target_pairs={{0,4},{2,6},{4,0},{6,2},{8,12},{10,14},{12,8},{14,10},{1,5},{3,7},... | collective-permute-start | bytes 98312 | tf_op jit(solution)/shard_map/cond/branch_1_fun/ppermute | solution.py:372
  100.2 5.5 %collective-permute-done.6 = bf16[64,256]{1,0:T(8,128)(2,1)S(1)} collective-permute-done((bf16[64,256]{1,0:T(8,128)(2,1)S(1)}, bf16[64,256]{1,0:T(8,128)(2,1)S(1)}, u32[]{:S(2)}, u32[]{:S(2)}) %collective-permute-start.6) | collective-permute-done | bytes 32800 | tf_op jit(solution)/shard_map/cond/branch_1_fun/ppermute | solution.py:372
  105.7 1.1 collective-permute-done.5
  106.8 1.7 %collective-permute-done.4 = bf16[64,256]{1,0:T(8,128)(2,1)S(1)} collective-permute-done((bf16[64,256]{1,0:T(8,128)(2,1)S(1)}, bf16[64,256]{1,0:T(8,128)(2,1)S(1)}, u32[]{:S(2)}, u32[]{:S(2)}) %collective-permute-start.4) | collective-permute-done | bytes 32800 | tf_op jit(solution)/shard_map/cond/branch_1_fun/ppermute | solution.py:372
  108.4 1.5 %convert_add_fusion = f32[64,256]{1,0:T(8,128)} fusion(bf16[64,256]{1,0:T(8,128)(2,1)S(1)} %collective-permute-done.6, bf16[64,256]{1,0:T(8,128)(2,1)S(1)} %collective-permute-done.5, f32[64,256]{1,0:T(8,128)} %param.5, bf16[64,256]{1,0:T(8,128)(2,1)S(1)} %collective-permute-done.4), kind=kLoop, calls=%fused_computation.4 | loop fusion | flops 98304 | bytes 229376 | tf_op jit(solution)/shard_map/cond/branch_1_fun/add | solution.py:433
  109.9 3.9 %finish.1 = bf16[256,1024]{1,0:T(8,128)(2,1)} custom-call(s32[1]{0:T(128)} %bitcast.3.y_ref, s32[1]{0:T(128)} %bitcast.4.g_ref, f32[64,256]{1,0:T(8,128)} %get-tuple-element.61.refs_1_.latent_ref, s32[1,256]{1,0:T(1,128)} %bitcast.20, bf16[512,512]{1,0:T(8,128)(2,1)} %relay.7.refs_0_, bf16[512,512]{1,0:T(8,128)(2,1)} %get-tuple-element.55.refs_1_, ...), custom_call_target="tpu_custom_call" | custom-call | flops 1 | bytes 1 | tf_op jit(solution)/shard_map/finish/pallas_call | solution.py:344
  (18 shorter events, 0.0 us)
Async XLA Ops:
  2.7 61.4 %all-to-all-start = ((bf16[8,64,2304]{2,1,0:T(8,128)(2,1)}), bf16[8,64,2304]{2,1,0:T(8,128)(2,1)}, u32[]{:S(2)}, u32[]{:S(2)}) async-start(bf16[8,64,2304]{2,1,0:T(8,128)(2,1)} %pack_factors.1.after_ref), calls=%async_computation | async-start | bytes 4718592 | tf_op jit(solution)/shard_map/all_to_all | solution.py:376
  13.1 45.0 %collective-permute-start.9 = (bf16[272,1792]{1,0:T(8,128)(2,1)}, bf16[272,1792]{1,0:T(8,128)(2,1)}, u32[]{:S(2)}, u32[]{:S(2)}) collective-permute-start(bf16[272,1792]{1,0:T(8,128)(2,1)} %get-tuple-element.44), channel_id=1, source_target_pairs={{0,17},{1,16},{16,1},{17,0},{2,19},{3,18},{18,3},{19,2},{4,21},{5,... | collective-permute-start | bytes 2924552 | tf_op jit(solution)/shard_map/ppermute | solution.py:381
  13.8 45.7 %collective-permute-start.8 = (bf16[272,1792]{1,0:T(8,128)(2,1)}, bf16[272,1792]{1,0:T(8,128)(2,1)}, u32[]{:S(2)}, u32[]{:S(2)}) collective-permute-start(bf16[272,1792]{1,0:T(8,128)(2,1)} %get-tuple-element.44), channel_id=1, source_target_pairs={{0,16},{16,0},{1,17},{17,1},{2,18},{18,2},{3,19},{19,3},{4,20},{20... | collective-permute-start | bytes 2924552 | tf_op jit(solution)/shard_map/ppermute | solution.py:379
  14.8 44.8 %collective-permute-start.7 = (bf16[272,1792]{1,0:T(8,128)(2,1)}, bf16[272,1792]{1,0:T(8,128)(2,1)}, u32[]{:S(2)}, u32[]{:S(2)}) collective-permute-start(bf16[272,1792]{1,0:T(8,128)(2,1)} %get-tuple-element.43.after_ref.refs_0_), channel_id=1, source_target_pairs={{0,1},{1,0},{2,3},{3,2},{4,5},{5,4},{6,7},{7,6},{8,9},{9,8},{10,11... | collective-permute-start | bytes 2924552 | tf_op jit(solution)/shard_map/ppermute | solution.py:380
  21.5 32.3 %collective-permute-start.10 = (bf16[1,256,1024]{2,1,0:T(8,128)(2,1)}, bf16[1,256,1024]{2,1,0:T(8,128)(2,1)}, u32[]{:S(2)}, u32[]{:S(2)}) collective-permute-start(bf16[1,256,1024]{2,1,0:T(8,128)(2,1)} %products.4.after_ref), channel_id=1, source_target_pairs={{0,2},{2,0},{4,6},{6,4},{8,10},{10,8},{12,14},{14,12},{1,3},{3,1},... | collective-permute-start | bytes 1572872 | tf_op jit(solution)/shard_map/ppermute | solution.py:372
  32.7 43.9 %collective-permute-start.12 = (bf16[1,256,1024]{2,1,0:T(8,128)(2,1)}, bf16[1,256,1024]{2,1,0:T(8,128)(2,1)}, u32[]{:S(2)}, u32[]{:S(2)}) collective-permute-start(bf16[1,256,1024]{2,1,0:T(8,128)(2,1)} %get-tuple-element.50), channel_id=1, source_target_pairs={{0,2},{2,0},{4,6},{6,4},{8,10},{10,8},{12,14},{14,12},{1,3},{3,1},... | collective-permute-start | bytes 1572872 | tf_op jit(solution)/shard_map/ppermute | solution.py:372
  56.1 20.5 %collective-permute-start.13 = (bf16[1,256,1024]{2,1,0:T(8,128)(2,1)}, bf16[1,256,1024]{2,1,0:T(8,128)(2,1)}, u32[]{:S(2)}, u32[]{:S(2)}) collective-permute-start(bf16[1,256,1024]{2,1,0:T(8,128)(2,1)} %fold.3.refs_4_), channel_id=1, source_target_pairs={{0,4},{2,6},{4,0},{6,2},{8,12},{10,14},{12,8},{14,10},{1,5},{3,7},... | collective-permute-start | bytes 1572872 | tf_op jit(solution)/shard_map/ppermute | solution.py:372
  58.1 21.0 %collective-permute-start.11 = (bf16[1,256,1024]{2,1,0:T(8,128)(2,1)}, bf16[1,256,1024]{2,1,0:T(8,128)(2,1)}, u32[]{:S(2)}, u32[]{:S(2)}) collective-permute-start(bf16[1,256,1024]{2,1,0:T(8,128)(2,1)} %get-tuple-element.49), channel_id=1, source_target_pairs={{0,2},{2,0},{4,6},{6,4},{8,10},{10,8},{12,14},{14,12},{1,3},{3,1},... | collective-permute-start | bytes 1572872 | tf_op jit(solution)/shard_map/ppermute | solution.py:372
  69.8 5.3 %collective-permute-start.14 = (f32[2,64,256]{2,1,0:T(8,128)}, f32[2,64,256]{2,1,0:T(8,128)}, u32[]{:S(2)}, u32[]{:S(2)}) collective-permute-start(f32[2,64,256]{2,1,0:T(8,128)} %get-tuple-element.51), channel_id=1, source_target_pairs={{0,16},{16,0},{1,17},{17,1},{2,18},{18,2},{3,19},{19,3},{4,20},{20... | collective-permute-start | bytes 393224 | tf_op jit(solution)/shard_map/ppermute | solution.py:413
  71.3 20.6 %collective-permute-start.16 = (bf16[1,256,1024]{2,1,0:T(8,128)(2,1)}, bf16[1,256,1024]{2,1,0:T(8,128)(2,1)}, u32[]{:S(2)}, u32[]{:S(2)}) collective-permute-start(bf16[1,256,1024]{2,1,0:T(8,128)(2,1)} %get-tuple-element.53), channel_id=1, source_target_pairs={{0,2},{2,0},{4,6},{6,4},{8,10},{10,8},{12,14},{14,12},{1,3},{3,1},... | collective-permute-start | bytes 1572872 | tf_op jit(solution)/shard_map/ppermute | solution.py:372
  75.1 16.8 %collective-permute-start.15 = (bf16[512,512]{1,0:T(8,128)(2,1)}, bf16[512,512]{1,0:T(8,128)(2,1)}, u32[]{:S(2)}, u32[]{:S(2)}) collective-permute-start(bf16[512,512]{1,0:T(8,128)(2,1)} %relay.7.refs_0_), channel_id=1, source_target_pairs={{0,16},{16,0},{1,17},{17,1},{2,18},{18,2},{3,19},{19,3},{4,20},{20... | collective-permute-start | bytes 1572872 | tf_op jit(solution)/shard_map/ppermute | solution.py:443
  79.1 30.8 %collective-permute-start.17 = (bf16[1,256,1024]{2,1,0:T(8,128)(2,1)}, bf16[1,256,1024]{2,1,0:T(8,128)(2,1)}, u32[]{:S(2)}, u32[]{:S(2)}) collective-permute-start(bf16[1,256,1024]{2,1,0:T(8,128)(2,1)} %fold.4.refs_2_), channel_id=1, source_target_pairs={{0,8},{2,10},{4,12},{6,14},{8,0},{10,2},{12,4},{14,6},{1,9},{3,11}... | collective-permute-start | bytes 1572872 | tf_op jit(solution)/shard_map/ppermute | solution.py:372
  81.4 28.6 %collective-permute-start.18 = (bf16[1,256,1024]{2,1,0:T(8,128)(2,1)}, bf16[1,256,1024]{2,1,0:T(8,128)(2,1)}, u32[]{:S(2)}, u32[]{:S(2)}) collective-permute-start(bf16[1,256,1024]{2,1,0:T(8,128)(2,1)} %fold.5.refs_1_), channel_id=1, source_target_pairs={{0,4},{2,6},{4,0},{6,2},{8,12},{10,14},{12,8},{14,10},{1,5},{3,7},... | collective-permute-start | bytes 1572872 | tf_op jit(solution)/shard_map/ppermute | solution.py:372
  85.6 1.3 %collective-permute-start.2 = (f32[64,256]{1,0:T(8,128)S(1)}, f32[64,256]{1,0:T(8,128)S(1)}, u32[]{:S(2)}, u32[]{:S(2)}) collective-permute-start(f32[64,256]{1,0:T(8,128)S(1)} %slice_bitcast_fusion.1), channel_id=1, source_target_pairs={{0,1},{1,0},{2,3},{3,2},{4,5},{5,4},{6,7},{7,6},{8,9},{9,8},{10,11... | collective-permute-start | bytes 196616 | tf_op jit(solution)/shard_map/cond/branch_1_fun/ppermute | solution.py:422
  86.9 4.3 %collective-permute-start.3 = (f32[64,256]{1,0:T(8,128)S(1)}, f32[64,256]{1,0:T(8,128)S(1)}, u32[]{:S(2)}, u32[]{:S(2)}) collective-permute-start(f32[64,256]{1,0:T(8,128)S(1)} %fusion), channel_id=1, source_target_pairs={{0,2},{2,0},{4,6},{6,4},{8,10},{10,8},{12,14},{14,12},{1,3},{3,1},... | collective-permute-start | bytes 196616 | tf_op jit(solution)/shard_map/cond/branch_1_fun/ppermute | solution.py:372
  91.9 2.3 %collective-permute-start = (bf16[512,512]{1,0:T(8,128)(2,1)}, bf16[512,512]{1,0:T(8,128)(2,1)}, u32[]{:S(2)}, u32[]{:S(2)}) collective-permute-start(bf16[512,512]{1,0:T(8,128)(2,1)} %get-tuple-element.28), channel_id=1, source_target_pairs={{0,1},{1,0},{2,3},{3,2},{4,5},{5,4},{6,7},{7,6},{8,9},{9,8},{10,11... | collective-permute-start | bytes 1572872 | tf_op jit(solution)/shard_map/cond/branch_1_fun/ppermute | solution.py:437
  92.0 3.0 %collective-permute-start.1 = (bf16[512,512]{1,0:T(8,128)(2,1)}, bf16[512,512]{1,0:T(8,128)(2,1)}, u32[]{:S(2)}, u32[]{:S(2)}) collective-permute-start(bf16[512,512]{1,0:T(8,128)(2,1)} %get-tuple-element.29), channel_id=1, source_target_pairs={{0,1},{1,0},{2,3},{3,2},{4,5},{5,4},{6,7},{7,6},{8,9},{9,8},{10,11... | collective-permute-start | bytes 1572872 | tf_op jit(solution)/shard_map/cond/branch_1_fun/ppermute | solution.py:437
  95.8 9.9 %collective-permute-start.6 = (bf16[64,256]{1,0:T(8,128)(2,1)S(1)}, bf16[64,256]{1,0:T(8,128)(2,1)S(1)}, u32[]{:S(2)}, u32[]{:S(2)}) collective-permute-start(bf16[64,256]{1,0:T(8,128)(2,1)S(1)} %convert_element_type.3), channel_id=1, source_target_pairs={{0,12},{2,14},{4,8},{6,10},{8,4},{10,6},{12,0},{14,2},{1,13},{3,15... | collective-permute-start | bytes 98312 | tf_op jit(solution)/shard_map/cond/branch_1_fun/ppermute | solution.py:372
  97.0 9.8 %collective-permute-start.5 = (bf16[64,256]{1,0:T(8,128)(2,1)S(1)}, bf16[64,256]{1,0:T(8,128)(2,1)S(1)}, u32[]{:S(2)}, u32[]{:S(2)}) collective-permute-start(bf16[64,256]{1,0:T(8,128)(2,1)S(1)} %convert_element_type.3), channel_id=1, source_target_pairs={{0,8},{2,10},{4,12},{6,14},{8,0},{10,2},{12,4},{14,6},{1,9},{3,11}... | collective-permute-start | bytes 98312 | tf_op jit(solution)/shard_map/cond/branch_1_fun/ppermute | solution.py:372
  97.3 11.1 %collective-permute-start.4 = (bf16[64,256]{1,0:T(8,128)(2,1)S(1)}, bf16[64,256]{1,0:T(8,128)(2,1)S(1)}, u32[]{:S(2)}, u32[]{:S(2)}) collective-permute-start(bf16[64,256]{1,0:T(8,128)(2,1)S(1)} %convert_element_type.3), channel_id=1, source_target_pairs={{0,4},{2,6},{4,0},{6,2},{8,12},{10,14},{12,8},{14,10},{1,5},{3,7},... | collective-permute-start | bytes 98312 | tf_op jit(solution)/shard_map/cond/branch_1_fun/ppermute | solution.py:372

commit v7 on v6

--- a/solution.py
+++ b/solution.py
@@ -293,9 +293,9 @@
     )(array, *after)
 
 
-def finish(latent, adapter, seconds, blocks, y, g):
+def finish(latents, adapter, seconds, blocks, y, g):
     rows, columns = blocks[0][0].shape[1:]
-    rank = latent.shape[0]
+    rank = latents[0].shape[0]
     tp = seconds[0].shape[0] // rank
     half = columns // 2
 
@@ -311,7 +311,14 @@
             left, right, (((0,), (0,)), ((), ())), preferred_element_type=jnp.float32
         )
 
+    def total_of(parts):
+        total = parts[0]
+        for part in parts[1:]:
+            total = total + part.astype(jnp.float32)
+        return total
+
     if half % 128:
+        latent = total_of(latents)
         near, far = spread(latent, adapter, g), spread(latent, adapter, 1 - g)
         mine = product(near, seconds[0]) + product(far, seconds[1])
         other = product(near, seconds[2]) + product(far, seconds[3])
@@ -325,10 +332,12 @@
             total = total + array[i].astype(jnp.float32)
         return total.astype(jnp.bfloat16)
 
-    def kernel(y_ref, g_ref, latent_ref, adapter_ref, *refs):
+    def kernel(y_ref, g_ref, *refs):
+        latent_refs, adapter_ref, refs = refs[: len(latents)], refs[len(latents)], refs[len(latents) + 1 :]
+        latent = total_of([latent_ref[...] for latent_ref in latent_refs])
         second_refs, block_refs, out_ref = refs[:4], refs[4:-1], refs[-1]
-        near = spread(latent_ref[...], adapter_ref[...], g_ref[0])
-        far = spread(latent_ref[...], adapter_ref[...], 1 - g_ref[0])
+        near = spread(latent, adapter_ref[...], g_ref[0])
+        far = spread(latent, adapter_ref[...], 1 - g_ref[0])
         for which in range(2):
             index = y_ref[0] if which == 0 else 1 - y_ref[0]
             lanes = pl.ds(pl.multiple_of(index * half, 128), half)
@@ -347,12 +356,12 @@
         grid=(1,),
         out_shape=jax.ShapeDtypeStruct((rows, columns), jnp.bfloat16),
         in_specs=[SMEM, SMEM]
-        + [whole(array) for array in (latent, adapter, *seconds)]
+        + [whole(array) for array in (*latents, adapter, *seconds)]
         + block_specs(blocks),
         out_specs=pl.BlockSpec((rows, columns), lambda b: (0, 0)),
         compiler_params=PARAMS,
         cost_estimate=COST,
-    )(y.reshape(1), g.reshape(1), latent, adapter, *seconds, *[array for array, _ in blocks])
+    )(y.reshape(1), g.reshape(1), *latents, adapter, *seconds, *[array for array, _ in blocks])
 
 
 def local(
@@ -404,8 +413,7 @@
 
     multiply(odd[:1], [])
     multiply(odd[1:2], [odd[0] - 1])
-    multiply(odd[2:3], [odd[1] - 1])
-    multiply(odd[3:], [j - 1 for j in odd[2:]])
+    multiply(odd[2:], [j - 1 for j in odd[1:]])
     pass_on(stages[0][:1])
 
     blocks = [mine, from_grp, from_rep, from_both]
@@ -429,9 +437,7 @@
     def outer(latent):
         step = tp // 4
         sent = latent.astype(jnp.bfloat16)
-        for i in range(1, 4):
-            latent = latent + across(sent, i * step).astype(jnp.float32)
-        return latent
+        return [across(sent, i * step) for i in range(1, 4)]
 
     def swap(*arrays):
         return [lax.ppermute(array, "grp", SWAP) for array in arrays]
@@ -442,10 +448,12 @@
     second = relay(second, got)
     second_other = relay(lax.ppermute(second, "rep", SWAP), r)
     twins = lax.cond(t < tp, swap, lambda *arrays: list(arrays), second, second_other)
-    latent = lax.cond(t < tp, outer, lambda latent: latent, relay(latent, twins[1]))
+    latent = relay(latent, twins[1])
+    got = lax.cond(t < tp, outer, lambda latent: [latent.astype(jnp.bfloat16)] * 3, latent)
+    latents = [latent, *got]
     seconds = [second, twins[0], second_other, twins[1]]
-    blocks = [kept, (r, i), (relay(late, latent), k), *others]
-    return finish(latent, adapter, seconds, blocks, y, g)
+    blocks = [kept, (r, i), (relay(late, got[2]), k), *others]
+    return finish(latents, adapter, seconds, blocks, y, g)
 
 
 def solution(mesh):

time: 114 us -> 113 us (level)
  waiting for transfers between devices: 22.3 us -> 25.4 us
  Pallas kernels: 59.2 us -> 56.2 us
  other arithmetic: 3.98 us -> 2.47 us
    pallas_call x4 -> x3, Pallas kernels: 36.8 us -> 33.8 us  [block_products(): pl.pallas_call(kernel, name='products', out_shape=out_shape, grid_spec=pl...]
    ppermute x1, waiting for transfers between devices: 0.01 us -> 1.63 us  [local(): from_rep = lax.ppermute(other, 'rep', SWAP)]
    add x1 -> x0, other arithmetic: 1.49 us -> none  [outer(): latent = latent + across(sent, i * step).astype(jnp.float32)]
    all_to_all x1, waiting for transfers between devices: 4.49 us -> 5.83 us  [local(): lax.all_to_all(factors, 'tp', split_axis=0, concat_axis=0, tiled=True)]
  transfers between devices with their start and end apart: 20 -> 20, of which waited for: 9 -> 10; matrix products, arithmetic and copies ran while one was open for 4% -> 2% of each run, Pallas kernels for 46% -> 44%
where the time goes in v7:
time: 113 us; the launch traced here: 112 us
  Pallas kernels  56.2 us (50%)
  starting transfers between devices  28.3 us (25%)
  waiting for transfers between devices  25.4 us (22%)
  other arithmetic  2.47 us (2%)
    pallas_call x3, Pallas kernels, block_products(): pl.pallas_call(kernel, name='products', out_shape=out_shape, grid_spec=pl...  33.8 us
    ppermute x11, starting transfers between devices, across(): return lax.ppermute(array, 'tp', [(i, i ^ step) for i in range(tp)])  15.4 us
    ppermute x11, waiting for transfers between devices, across(): return lax.ppermute(array, 'tp', [(i, i ^ step) for i in range(tp)])  11.9 us
    all_to_all x1, starting transfers between devices, local(): lax.all_to_all(factors, 'tp', split_axis=0, concat_axis=0, tiled=True)  7.26 us
    pallas_call x3, Pallas kernels, fold(): pl.pallas_call(kernel, name='fold', grid=(1,), out_shape=out_shape, in_sp...  6.96 us
    all_to_all x1, waiting for transfers between devices, local(): lax.all_to_all(factors, 'tp', split_axis=0, concat_axis=0, tiled=True)  5.83 us
    pallas_call x1, Pallas kernels, latent_terms(): pl.pallas_call(kernel, name='latent_terms', out_shape=[jax.ShapeDtypeStru...  5.73 us
    pallas_call x1, Pallas kernels, finish(): pl.pallas_call(kernel, name='finish', grid=(1,), out_shape=jax.ShapeDtype...  3.97 us
  transfers between devices with their start and end apart: 20, of which 10 were waited for; matrix products, arithmetic and copies ran while one was open for 2% of the time, Pallas kernels for 44%

profile of v7, /device:TPU:0, one launch (start us, length us, event | category | flops | bytes accessed | tf_op | source)
XLA Modules:
  0.0 112.5 jit_solution(9683147003822466016)
XLA Ops:
  0.0 2.7 %pack_factors.1.after_ref = bf16[8,64,2304]{2,1,0:T(8,128)(2,1)} custom-call(s32[1]{0:T(128)} %bitcast.3.y_ref, bf16[64,28672]{1,0:T(8,128)(2,1)} %bitcast.17, bf16[64,8192]{1,0:T(8,128)(2,1)} %bitcast.18), custom_call_target="tpu_custom_call" | custom-call | flops 1 | bytes 1 | tf_op jit(solution)/shard_map/pack_factors/pallas_call | solution.py:112
  2.7 7.3 %all-to-all-start = ((bf16[8,64,2304]{2,1,0:T(8,128)(2,1)}), bf16[8,64,2304]{2,1,0:T(8,128)(2,1)}, u32[]{:S(2)}, u32[]{:S(2)}) async-start(bf16[8,64,2304]{2,1,0:T(8,128)(2,1)} %pack_factors.1.after_ref), calls=%async_computation | async-start | bytes 4718592 | tf_op jit(solution)/shard_map/all_to_all | solution.py:385
  9.9 3.1 %pack_hidden.1 = (bf16[272,1792]{1,0:T(8,128)(2,1)}, bf16[272,1792]{1,0:T(8,128)(2,1)}) custom-call(s32[1]{0:T(128)} %bitcast.3.y_ref, bf16[256,3584]{1,0:T(8,128)(2,1)} %hidden_ref.7, s32[1,256]{1,0:T(1,128)} %bitcast.19, bf16[8,64,2304]{2,1,0:T(8,128)(2,1)} %pack_factors.1.after_ref), custom_call_target="tpu_custom_call" | custom-call | flops 1 | bytes 1 | tf_op jit(solution)/shard_map/pack_hidden/pallas_call | solution.py:165
  13.1 0.7 collective-permute-start.9
  13.8 0.9 collective-permute-start.8
  14.7 0.3 collective-permute-start.7
  15.0 6.5 %products.3.after_ref = bf16[1,256,1024]{2,1,0:T(8,128)(2,1)} custom-call(s32[1]{0:T(128)} %bitcast.10.t_ref, bf16[256,3584]{1,0:T(8,128)(2,1)} %hidden_ref.7, bf16[3584,8192]{1,0:T(8,128)(2,1)} %weight_ref.5, bf16[272,1792]{1,0:T(8,128)(2,1)} %get-tuple-element.42.after_ref.refs_0_), custom_call_target="tpu_custom_call" | custom-call | flops 1 | bytes 1 | tf_op jit(solution)/shard_map/products/pallas_call | solution.py:54
  21.5 2.0 %collective-permute-start.10 = (bf16[1,256,1024]{2,1,0:T(8,128)(2,1)}, bf16[1,256,1024]{2,1,0:T(8,128)(2,1)}, u32[]{:S(2)}, u32[]{:S(2)}) collective-permute-start(bf16[1,256,1024]{2,1,0:T(8,128)(2,1)} %products.3.after_ref), channel_id=1, source_target_pairs={{0,2},{2,0},{4,6},{6,4},{8,10},{10,8},{12,14},{14,12},{1,3},{3,1},... | collective-permute-start | bytes 1572872 | tf_op jit(solution)/shard_map/ppermute | solution.py:381
  23.5 9.2 %products.4 = (bf16[1,256,1024]{2,1,0:T(8,128)(2,1)}, f32[1,256,1024]{2,1,0:T(8,128)}) custom-call(s32[1]{0:T(128)} %bitcast.10.t_ref, bf16[256,3584]{1,0:T(8,128)(2,1)} %hidden_ref.7, bf16[3584,8192]{1,0:T(8,128)(2,1)} %weight_ref.5, bf16[1,256,1024]{2,1,0:T(8,128)(2,1)} %products.3.after_ref), custom_call_target="tpu_custom_call" | custom-call | flops 1 | bytes 1 | tf_op jit(solution)/shard_map/products/pallas_call | solution.py:54
  32.7 0.0 collective-permute-start.12
  32.7 18.2 %products.5 = (bf16[1,256,1024]{2,1,0:T(8,128)(2,1)}, bf16[1,256,1024]{2,1,0:T(8,128)(2,1)}, f32[3,256,1024]{2,1,0:T(8,128)}) custom-call(s32[1]{0:T(128)} %bitcast.10.t_ref, bf16[256,3584]{1,0:T(8,128)(2,1)} %hidden_ref.7, bf16[3584,8192]{1,0:T(8,128)(2,1)} %weight_ref.5, f32[1,256,1024]{2,1,0:T(8,128)} %get-tuple-element.44.after_ref.refs_0_), custom_call_target="tpu_custom_call" | custom-call | flops 1 | bytes 1 | tf_op jit(solution)/shard_map/products/pallas_call | solution.py:54
  50.8 2.2 %fold.3.refs_4_ = bf16[1,256,1024]{2,1,0:T(8,128)(2,1)} custom-call(f32[1,256,1024]{2,1,0:T(8,128)} %get-tuple-element.44.after_ref.refs_0_, bf16[1,256,1024]{2,1,0:T(8,128)(2,1)} %collective-permute-done.10.refs_1_, f32[3,256,1024]{2,1,0:T(8,128)} %get-tuple-element.45.refs_2_.refs_0_.refs_9_), custom_call_target="tpu_custom_call" | custom-call | flops 1 | bytes 1 | tf_op jit(solution)/shard_map/fold/pallas_call | solution.py:264
  53.1 2.0 %collective-permute-start.13 = (bf16[1,256,1024]{2,1,0:T(8,128)(2,1)}, bf16[1,256,1024]{2,1,0:T(8,128)(2,1)}, u32[]{:S(2)}, u32[]{:S(2)}) collective-permute-start(bf16[1,256,1024]{2,1,0:T(8,128)(2,1)} %fold.3.refs_4_), channel_id=1, source_target_pairs={{0,4},{2,6},{4,0},{6,2},{8,12},{10,14},{12,8},{14,10},{1,5},{3,7},... | collective-permute-start | bytes 1572872 | tf_op jit(solution)/shard_map/ppermute | solution.py:381
  55.1 1.5 %collective-permute-start.11 = (bf16[1,256,1024]{2,1,0:T(8,128)(2,1)}, bf16[1,256,1024]{2,1,0:T(8,128)(2,1)}, u32[]{:S(2)}, u32[]{:S(2)}) collective-permute-start(bf16[1,256,1024]{2,1,0:T(8,128)(2,1)} %get-tuple-element.47), channel_id=1, source_target_pairs={{0,2},{2,0},{4,6},{6,4},{8,10},{10,8},{12,14},{14,12},{1,3},{3,1},... | collective-permute-start | bytes 1572872 | tf_op jit(solution)/shard_map/ppermute | solution.py:381
  56.6 1.6 %collective-permute-done.8.refs_2_ = bf16[272,1792]{1,0:T(8,128)(2,1)} collective-permute-done((bf16[272,1792]{1,0:T(8,128)(2,1)}, bf16[272,1792]{1,0:T(8,128)(2,1)}, u32[]{:S(2)}, u32[]{:S(2)}) %collective-permute-start.8) | collective-permute-done | bytes 974880 | tf_op jit(solution)/shard_map/ppermute | solution.py:388
  58.2 5.8 %all-to-all-done = bf16[8,64,2304]{2,1,0:T(8,128)(2,1)} async-done(((bf16[8,64,2304]{2,1,0:T(8,128)(2,1)}), bf16[8,64,2304]{2,1,0:T(8,128)(2,1)}, u32[]{:S(2)}, u32[]{:S(2)}) %all-to-all-start) | async-done | bytes 2359328 | tf_op jit(solution)/shard_map/all_to_all | solution.py:385
  64.0 5.7 %latent_terms.1 = (f32[2,64,256]{2,1,0:T(8,128)}, f32[2,64,256]{2,1,0:T(8,128)}, bf16[512,512]{1,0:T(8,128)(2,1)}) custom-call(s32[1]{0:T(128)} %bitcast.4.g_ref, bf16[512,2304]{1,0:T(8,128)(2,1)} %bitcast.8.factors_ref, bf16[272,1792]{1,0:T(8,128)(2,1)} %get-tuple-element.42.after_ref.refs_0_, bf16[272,1792]{1,0:T(8,128)(2,1)} %collective-permute-done.7.refs_1_, ...), custom_call_target="tpu_custom_call" | custom-call | flops 1 | bytes 1 | tf_op jit(solution)/shard_map/latent_terms/pallas_call | solution.py:220
  69.8 1.5 %collective-permute-start.14 = (f32[2,64,256]{2,1,0:T(8,128)}, f32[2,64,256]{2,1,0:T(8,128)}, u32[]{:S(2)}, u32[]{:S(2)}) collective-permute-start(f32[2,64,256]{2,1,0:T(8,128)} %get-tuple-element.49), channel_id=1, source_target_pairs={{0,16},{16,0},{1,17},{17,1},{2,18},{18,2},{3,19},{19,3},{4,20},{20... | collective-permute-start | bytes 393224 | tf_op jit(solution)/shard_map/ppermute | solution.py:421
  71.3 1.5 %collective-permute-start.16 = (bf16[1,256,1024]{2,1,0:T(8,128)(2,1)}, bf16[1,256,1024]{2,1,0:T(8,128)(2,1)}, u32[]{:S(2)}, u32[]{:S(2)}) collective-permute-start(bf16[1,256,1024]{2,1,0:T(8,128)(2,1)} %get-tuple-element.51), channel_id=1, source_target_pairs={{0,2},{2,0},{4,6},{6,4},{8,10},{10,8},{12,14},{14,12},{1,3},{3,1},... | collective-permute-start | bytes 1572872 | tf_op jit(solution)/shard_map/ppermute | solution.py:381
  72.8 2.3 %collective-permute-done.14.refs_1_ = f32[2,64,256]{2,1,0:T(8,128)} collective-permute-done((f32[2,64,256]{2,1,0:T(8,128)}, f32[2,64,256]{2,1,0:T(8,128)}, u32[]{:S(2)}, u32[]{:S(2)}) %collective-permute-start.14) | collective-permute-done | bytes 131104 | tf_op jit(solution)/shard_map/ppermute | solution.py:421
  75.1 1.5 %collective-permute-start.15 = (bf16[512,512]{1,0:T(8,128)(2,1)}, bf16[512,512]{1,0:T(8,128)(2,1)}, u32[]{:S(2)}, u32[]{:S(2)}) collective-permute-start(bf16[512,512]{1,0:T(8,128)(2,1)} %relay.7.refs_5_), channel_id=1, source_target_pairs={{0,16},{16,0},{1,17},{17,1},{2,18},{18,2},{3,19},{19,3},{4,20},{20... | collective-permute-start | bytes 1572872 | tf_op jit(solution)/shard_map/ppermute | solution.py:449
  76.6 0.0 collective-permute-done.12.refs_1_
  76.6 0.0 collective-permute-done.13.refs_2_
  76.6 2.5 %fold.4.refs_2_ = bf16[1,256,1024]{2,1,0:T(8,128)(2,1)} custom-call(f32[3,256,1024]{2,1,0:T(8,128)} %get-tuple-element.45.refs_2_.refs_0_.refs_9_, bf16[1,256,1024]{2,1,0:T(8,128)(2,1)} %collective-permute-done.12.refs_1_, bf16[1,256,1024]{2,1,0:T(8,128)(2,1)} %collective-permute-done.13.refs_2_, f32[2,64,256]{2,1,0:T(8,128)} %get-tuple-element.46.refs_3_.refs_0_), custom_call_target="tpu_custom_call" | custom-call | flops 1 | bytes 1 | tf_op jit(solution)/shard_map/fold/pallas_call | solution.py:264
  79.1 0.0 collective-permute-start.17
  79.1 2.3 %fold.5.refs_1_ = bf16[1,256,1024]{2,1,0:T(8,128)(2,1)} custom-call(f32[3,256,1024]{2,1,0:T(8,128)} %get-tuple-element.45.refs_2_.refs_0_.refs_9_, bf16[1,256,1024]{2,1,0:T(8,128)(2,1)} %collective-permute-done.11.refs_1_, bf16[1,256,1024]{2,1,0:T(8,128)(2,1)} %fold.4.refs_2_), custom_call_target="tpu_custom_call" | custom-call | flops 1 | bytes 1 | tf_op jit(solution)/shard_map/fold/pallas_call | solution.py:264
  81.3 3.2 %collective-permute-start.18 = (bf16[1,256,1024]{2,1,0:T(8,128)(2,1)}, bf16[1,256,1024]{2,1,0:T(8,128)(2,1)}, u32[]{:S(2)}, u32[]{:S(2)}) collective-permute-start(bf16[1,256,1024]{2,1,0:T(8,128)(2,1)} %fold.5.refs_1_), channel_id=1, source_target_pairs={{0,4},{2,6},{4,0},{6,2},{8,12},{10,14},{12,8},{14,10},{1,5},{3,7},... | collective-permute-start | bytes 1572872 | tf_op jit(solution)/shard_map/ppermute | solution.py:381
  84.6 7.3 %conditional.3 = (f32[64,256]{1,0:T(8,128)}) conditional(s32[]{:T(128)} %convert_element_type.11, f32[2,64,256]{2,1,0:T(8,128)} %relay.6, (f32[2,64,256]{2,1,0:T(8,128)}, f32[2,64,256]{2,1,0:T(8,128)}) %tuple.26), branch_computations={%region_0.0_spmd, %region_1.0_spmd} | conditional | flops 65536 | bytes 1441880 | solution.py:445
  84.6 1.0 add.6
  85.6 0.1 collective-permute-start.5
  85.6 1.2 %collective-permute-done.5 = f32[64,256]{1,0:T(8,128)S(1)} collective-permute-done((f32[64,256]{1,0:T(8,128)S(1)}, f32[64,256]{1,0:T(8,128)S(1)}, u32[]{:S(2)}, u32[]{:S(2)}) %collective-permute-start.5) | collective-permute-done | bytes 65568 | tf_op jit(solution)/shard_map/cond/branch_1_fun/ppermute | solution.py:430
  86.9 0.8 collective-permute-start.6
  87.7 3.6 %collective-permute-done.6 = f32[64,256]{1,0:T(8,128)S(1)} collective-permute-done((f32[64,256]{1,0:T(8,128)S(1)}, f32[64,256]{1,0:T(8,128)S(1)}, u32[]{:S(2)}, u32[]{:S(2)}) %collective-permute-start.6) | collective-permute-done | bytes 65568 | tf_op jit(solution)/shard_map/cond/branch_1_fun/ppermute | solution.py:381
  91.2 0.6 add.8
  91.9 3.1 %conditional.4 = (bf16[512,512]{1,0:T(8,128)(2,1)}, bf16[512,512]{1,0:T(8,128)(2,1)}) conditional(s32[]{:T(128)} %convert_element_type.11, (bf16[512,512]{1,0:T(8,128)(2,1)}, bf16[512,512]{1,0:T(8,128)(2,1)}) %tuple.27, (bf16[512,512]{1,0:T(8,128)(2,1)}, bf16[512,512]{1,0:T(8,128)(2,1)}) %tuple.27), branch_computations={%region_2.0_spmd, %region_3.0_spmd} | conditional | bytes 4194400 | solution.py:450
  91.9 0.1 collective-permute-start
  92.0 0.5 collective-permute-start.1
  92.5 1.7 %collective-permute-done = bf16[512,512]{1,0:T(8,128)(2,1)} collective-permute-done((bf16[512,512]{1,0:T(8,128)(2,1)}, bf16[512,512]{1,0:T(8,128)(2,1)}, u32[]{:S(2)}, u32[]{:S(2)}) %collective-permute-start) | collective-permute-done | bytes 524320 | tf_op jit(solution)/shard_map/cond/branch_1_fun/ppermute | solution.py:443
  94.2 0.7 collective-permute-done.1
  94.9 13.5 %conditional.5 = (bf16[64,256]{1,0:T(8,128)(2,1)}, bf16[64,256]{1,0:T(8,128)(2,1)}, bf16[64,256]{1,0:T(8,128)(2,1)}) conditional(s32[]{:T(128)} %convert_element_type.11, f32[64,256]{1,0:T(8,128)} %relay.10.refs_0_, f32[64,256]{1,0:T(8,128)} %relay.10.refs_0_), branch_computations={%region_4.0_spmd, %region_5.0_spmd} | conditional | flops 16384 | bytes 491664 | solution.py:452
  94.9 0.8 convert_element_type.3
  95.8 1.1 %collective-permute-start.4 = (bf16[64,256]{1,0:T(8,128)(2,1)S(1)}, bf16[64,256]{1,0:T(8,128)(2,1)}, u32[]{:S(2)}, u32[]{:S(2)}) collective-permute-start(bf16[64,256]{1,0:T(8,128)(2,1)S(1)} %convert_element_type.3), channel_id=1, source_target_pairs={{0,12},{2,14},{4,8},{6,10},{8,4},{10,6},{12,0},{14,2},{1,13},{3,15... | collective-permute-start | bytes 98312 | tf_op jit(solution)/shard_map/cond/branch_1_fun/ppermute | solution.py:381
  96.9 0.3 collective-permute-start.3
  97.3 2.9 %collective-permute-start.2 = (bf16[64,256]{1,0:T(8,128)(2,1)S(1)}, bf16[64,256]{1,0:T(8,128)(2,1)}, u32[]{:S(2)}, u32[]{:S(2)}) collective-permute-start(bf16[64,256]{1,0:T(8,128)(2,1)S(1)} %convert_element_type.3), channel_id=1, source_target_pairs={{0,4},{2,6},{4,0},{6,2},{8,12},{10,14},{12,8},{14,10},{1,5},{3,7},... | collective-permute-start | bytes 98312 | tf_op jit(solution)/shard_map/cond/branch_1_fun/ppermute | solution.py:381
  100.2 5.6 %collective-permute-done.4 = bf16[64,256]{1,0:T(8,128)(2,1)} collective-permute-done((bf16[64,256]{1,0:T(8,128)(2,1)S(1)}, bf16[64,256]{1,0:T(8,128)(2,1)}, u32[]{:S(2)}, u32[]{:S(2)}) %collective-permute-start.4) | collective-permute-done | bytes 32800 | tf_op jit(solution)/shard_map/cond/branch_1_fun/ppermute | solution.py:381
  105.8 1.1 collective-permute-done.3
  106.8 1.7 %collective-permute-done.2 = bf16[64,256]{1,0:T(8,128)(2,1)} collective-permute-done((bf16[64,256]{1,0:T(8,128)(2,1)S(1)}, bf16[64,256]{1,0:T(8,128)(2,1)}, u32[]{:S(2)}, u32[]{:S(2)}) %collective-permute-start.2) | collective-permute-done | bytes 32800 | tf_op jit(solution)/shard_map/cond/branch_1_fun/ppermute | solution.py:381
  108.5 4.0 %finish.1 = bf16[256,1024]{1,0:T(8,128)(2,1)} custom-call(s32[1]{0:T(128)} %bitcast.3.y_ref, s32[1]{0:T(128)} %bitcast.4.g_ref, f32[64,256]{1,0:T(8,128)} %relay.10.refs_0_, bf16[64,256]{1,0:T(8,128)(2,1)} %get-tuple-element.53.refs_1_, bf16[64,256]{1,0:T(8,128)(2,1)} %get-tuple-element.54.refs_2_, bf16[64,256]{1,0:T(8,128)(2,1)} %get-tuple-element.55.refs_1_.refs_3_, ...), custom_call_target="tpu_custom_call" | custom-call | flops 1 | bytes 1 | tf_op jit(solution)/shard_map/finish/pallas_call | solution.py:353
  (16 shorter events, 0.0 us)
Async XLA Ops:
  2.7 61.4 %all-to-all-start = ((bf16[8,64,2304]{2,1,0:T(8,128)(2,1)}), bf16[8,64,2304]{2,1,0:T(8,128)(2,1)}, u32[]{:S(2)}, u32[]{:S(2)}) async-start(bf16[8,64,2304]{2,1,0:T(8,128)(2,1)} %pack_factors.1.after_ref), calls=%async_computation | async-start | bytes 4718592 | tf_op jit(solution)/shard_map/all_to_all | solution.py:385
  13.1 42.1 %collective-permute-start.9 = (bf16[272,1792]{1,0:T(8,128)(2,1)}, bf16[272,1792]{1,0:T(8,128)(2,1)}, u32[]{:S(2)}, u32[]{:S(2)}) collective-permute-start(bf16[272,1792]{1,0:T(8,128)(2,1)} %get-tuple-element.43), channel_id=1, source_target_pairs={{0,17},{1,16},{16,1},{17,0},{2,19},{3,18},{18,3},{19,2},{4,21},{5,... | collective-permute-start | bytes 2924552 | tf_op jit(solution)/shard_map/ppermute | solution.py:390
  13.8 44.4 %collective-permute-start.8 = (bf16[272,1792]{1,0:T(8,128)(2,1)}, bf16[272,1792]{1,0:T(8,128)(2,1)}, u32[]{:S(2)}, u32[]{:S(2)}) collective-permute-start(bf16[272,1792]{1,0:T(8,128)(2,1)} %get-tuple-element.43), channel_id=1, source_target_pairs={{0,16},{16,0},{1,17},{17,1},{2,18},{18,2},{3,19},{19,3},{4,20},{20... | collective-permute-start | bytes 2924552 | tf_op jit(solution)/shard_map/ppermute | solution.py:388
  14.7 43.5 %collective-permute-start.7 = (bf16[272,1792]{1,0:T(8,128)(2,1)}, bf16[272,1792]{1,0:T(8,128)(2,1)}, u32[]{:S(2)}, u32[]{:S(2)}) collective-permute-start(bf16[272,1792]{1,0:T(8,128)(2,1)} %get-tuple-element.42.after_ref.refs_0_), channel_id=1, source_target_pairs={{0,1},{1,0},{2,3},{3,2},{4,5},{5,4},{6,7},{7,6},{8,9},{9,8},{10,11... | collective-permute-start | bytes 2924552 | tf_op jit(solution)/shard_map/ppermute | solution.py:389
  21.5 29.4 %collective-permute-start.10 = (bf16[1,256,1024]{2,1,0:T(8,128)(2,1)}, bf16[1,256,1024]{2,1,0:T(8,128)(2,1)}, u32[]{:S(2)}, u32[]{:S(2)}) collective-permute-start(bf16[1,256,1024]{2,1,0:T(8,128)(2,1)} %products.3.after_ref), channel_id=1, source_target_pairs={{0,2},{2,0},{4,6},{6,4},{8,10},{10,8},{12,14},{14,12},{1,3},{3,1},... | collective-permute-start | bytes 1572872 | tf_op jit(solution)/shard_map/ppermute | solution.py:381
  32.7 43.9 %collective-permute-start.12 = (bf16[1,256,1024]{2,1,0:T(8,128)(2,1)}, bf16[1,256,1024]{2,1,0:T(8,128)(2,1)}, u32[]{:S(2)}, u32[]{:S(2)}) collective-permute-start(bf16[1,256,1024]{2,1,0:T(8,128)(2,1)} %get-tuple-element.48), channel_id=1, source_target_pairs={{0,2},{2,0},{4,6},{6,4},{8,10},{10,8},{12,14},{14,12},{1,3},{3,1},... | collective-permute-start | bytes 1572872 | tf_op jit(solution)/shard_map/ppermute | solution.py:381
  53.1 23.5 %collective-permute-start.13 = (bf16[1,256,1024]{2,1,0:T(8,128)(2,1)}, bf16[1,256,1024]{2,1,0:T(8,128)(2,1)}, u32[]{:S(2)}, u32[]{:S(2)}) collective-permute-start(bf16[1,256,1024]{2,1,0:T(8,128)(2,1)} %fold.3.refs_4_), channel_id=1, source_target_pairs={{0,4},{2,6},{4,0},{6,2},{8,12},{10,14},{12,8},{14,10},{1,5},{3,7},... | collective-permute-start | bytes 1572872 | tf_op jit(solution)/shard_map/ppermute | solution.py:381
  55.1 24.0 %collective-permute-start.11 = (bf16[1,256,1024]{2,1,0:T(8,128)(2,1)}, bf16[1,256,1024]{2,1,0:T(8,128)(2,1)}, u32[]{:S(2)}, u32[]{:S(2)}) collective-permute-start(bf16[1,256,1024]{2,1,0:T(8,128)(2,1)} %get-tuple-element.47), channel_id=1, source_target_pairs={{0,2},{2,0},{4,6},{6,4},{8,10},{10,8},{12,14},{14,12},{1,3},{3,1},... | collective-permute-start | bytes 1572872 | tf_op jit(solution)/shard_map/ppermute | solution.py:381
  69.8 5.3 %collective-permute-start.14 = (f32[2,64,256]{2,1,0:T(8,128)}, f32[2,64,256]{2,1,0:T(8,128)}, u32[]{:S(2)}, u32[]{:S(2)}) collective-permute-start(f32[2,64,256]{2,1,0:T(8,128)} %get-tuple-element.49), channel_id=1, source_target_pairs={{0,16},{16,0},{1,17},{17,1},{2,18},{18,2},{3,19},{19,3},{4,20},{20... | collective-permute-start | bytes 393224 | tf_op jit(solution)/shard_map/ppermute | solution.py:421
  71.3 20.6 %collective-permute-start.16 = (bf16[1,256,1024]{2,1,0:T(8,128)(2,1)}, bf16[1,256,1024]{2,1,0:T(8,128)(2,1)}, u32[]{:S(2)}, u32[]{:S(2)}) collective-permute-start(bf16[1,256,1024]{2,1,0:T(8,128)(2,1)} %get-tuple-element.51), channel_id=1, source_target_pairs={{0,2},{2,0},{4,6},{6,4},{8,10},{10,8},{12,14},{14,12},{1,3},{3,1},... | collective-permute-start | bytes 1572872 | tf_op jit(solution)/shard_map/ppermute | solution.py:381
  75.1 16.8 %collective-permute-start.15 = (bf16[512,512]{1,0:T(8,128)(2,1)}, bf16[512,512]{1,0:T(8,128)(2,1)}, u32[]{:S(2)}, u32[]{:S(2)}) collective-permute-start(bf16[512,512]{1,0:T(8,128)(2,1)} %relay.7.refs_5_), channel_id=1, source_target_pairs={{0,16},{16,0},{1,17},{17,1},{2,18},{18,2},{3,19},{19,3},{4,20},{20... | collective-permute-start | bytes 1572872 | tf_op jit(solution)/shard_map/ppermute | solution.py:449
  79.1 29.4 %collective-permute-start.17 = (bf16[1,256,1024]{2,1,0:T(8,128)(2,1)}, bf16[1,256,1024]{2,1,0:T(8,128)(2,1)}, u32[]{:S(2)}, u32[]{:S(2)}) collective-permute-start(bf16[1,256,1024]{2,1,0:T(8,128)(2,1)} %fold.4.refs_2_), channel_id=1, source_target_pairs={{0,8},{2,10},{4,12},{6,14},{8,0},{10,2},{12,4},{14,6},{1,9},{3,11}... | collective-permute-start | bytes 1572872 | tf_op jit(solution)/shard_map/ppermute | solution.py:381
  81.3 27.2 %collective-permute-start.18 = (bf16[1,256,1024]{2,1,0:T(8,128)(2,1)}, bf16[1,256,1024]{2,1,0:T(8,128)(2,1)}, u32[]{:S(2)}, u32[]{:S(2)}) collective-permute-start(bf16[1,256,1024]{2,1,0:T(8,128)(2,1)} %fold.5.refs_1_), channel_id=1, source_target_pairs={{0,4},{2,6},{4,0},{6,2},{8,12},{10,14},{12,8},{14,10},{1,5},{3,7},... | collective-permute-start | bytes 1572872 | tf_op jit(solution)/shard_map/ppermute | solution.py:381
  85.6 1.3 %collective-permute-start.5 = (f32[64,256]{1,0:T(8,128)S(1)}, f32[64,256]{1,0:T(8,128)S(1)}, u32[]{:S(2)}, u32[]{:S(2)}) collective-permute-start(f32[64,256]{1,0:T(8,128)S(1)} %slice_bitcast_fusion.1), channel_id=1, source_target_pairs={{0,1},{1,0},{2,3},{3,2},{4,5},{5,4},{6,7},{7,6},{8,9},{9,8},{10,11... | collective-permute-start | bytes 196616 | tf_op jit(solution)/shard_map/cond/branch_1_fun/ppermute | solution.py:430
  86.9 4.3 %collective-permute-start.6 = (f32[64,256]{1,0:T(8,128)S(1)}, f32[64,256]{1,0:T(8,128)S(1)}, u32[]{:S(2)}, u32[]{:S(2)}) collective-permute-start(f32[64,256]{1,0:T(8,128)S(1)} %fusion), channel_id=1, source_target_pairs={{0,2},{2,0},{4,6},{6,4},{8,10},{10,8},{12,14},{14,12},{1,3},{3,1},... | collective-permute-start | bytes 196616 | tf_op jit(solution)/shard_map/cond/branch_1_fun/ppermute | solution.py:381
  91.9 2.3 %collective-permute-start = (bf16[512,512]{1,0:T(8,128)(2,1)}, bf16[512,512]{1,0:T(8,128)(2,1)}, u32[]{:S(2)}, u32[]{:S(2)}) collective-permute-start(bf16[512,512]{1,0:T(8,128)(2,1)} %get-tuple-element.25), channel_id=1, source_target_pairs={{0,1},{1,0},{2,3},{3,2},{4,5},{5,4},{6,7},{7,6},{8,9},{9,8},{10,11... | collective-permute-start | bytes 1572872 | tf_op jit(solution)/shard_map/cond/branch_1_fun/ppermute | solution.py:443
  92.0 3.0 %collective-permute-start.1 = (bf16[512,512]{1,0:T(8,128)(2,1)}, bf16[512,512]{1,0:T(8,128)(2,1)}, u32[]{:S(2)}, u32[]{:S(2)}) collective-permute-start(bf16[512,512]{1,0:T(8,128)(2,1)} %get-tuple-element.26), channel_id=1, source_target_pairs={{0,1},{1,0},{2,3},{3,2},{4,5},{5,4},{6,7},{7,6},{8,9},{9,8},{10,11... | collective-permute-start | bytes 1572872 | tf_op jit(solution)/shard_map/cond/branch_1_fun/ppermute | solution.py:443
  95.8 10.0 %collective-permute-start.4 = (bf16[64,256]{1,0:T(8,128)(2,1)S(1)}, bf16[64,256]{1,0:T(8,128)(2,1)}, u32[]{:S(2)}, u32[]{:S(2)}) collective-permute-start(bf16[64,256]{1,0:T(8,128)(2,1)S(1)} %convert_element_type.3), channel_id=1, source_target_pairs={{0,12},{2,14},{4,8},{6,10},{8,4},{10,6},{12,0},{14,2},{1,13},{3,15... | collective-permute-start | bytes 98312 | tf_op jit(solution)/shard_map/cond/branch_1_fun/ppermute | solution.py:381
  96.9 9.9 %collective-permute-start.3 = (bf16[64,256]{1,0:T(8,128)(2,1)S(1)}, bf16[64,256]{1,0:T(8,128)(2,1)}, u32[]{:S(2)}, u32[]{:S(2)}) collective-permute-start(bf16[64,256]{1,0:T(8,128)(2,1)S(1)} %convert_element_type.3), channel_id=1, source_target_pairs={{0,8},{2,10},{4,12},{6,14},{8,0},{10,2},{12,4},{14,6},{1,9},{3,11}... | collective-permute-start | bytes 98312 | tf_op jit(solution)/shard_map/cond/branch_1_fun/ppermute | solution.py:381
  97.3 11.2 %collective-permute-start.2 = (bf16[64,256]{1,0:T(8,128)(2,1)S(1)}, bf16[64,256]{1,0:T(8,128)(2,1)}, u32[]{:S(2)}, u32[]{:S(2)}) collective-permute-start(bf16[64,256]{1,0:T(8,128)(2,1)S(1)} %convert_element_type.3), channel_id=1, source_target_pairs={{0,4},{2,6},{4,0},{6,2},{8,12},{10,14},{12,8},{14,10},{1,5},{3,7},... | collective-permute-start | bytes 98312 | tf_op jit(solution)/shard_map/cond/branch_1_fun/ppermute | solution.py:381

commit v8 on v7

--- a/solution.py
+++ b/solution.py
@@ -419,6 +419,8 @@
     blocks = [mine, from_grp, from_rep, from_both]
     near, away, second = latent_terms(factors, half, blocks, rows, rank, g, order)
     got = lax.ppermute(away, "rep", SWAP)
+    near = relay(near, got)
+    order.last = near
     rest = [stages[0][1:], *stages[1:]]
     if tp <= 8:
         rest = [[item] for items in reversed(rest) for item in items]
@@ -442,11 +444,22 @@
     def swap(*arrays):
         return [lax.ppermute(array, "grp", SWAP) for array in arrays]
 
-    latent = lax.cond(t < tp, inner, lambda near, got: near[0], relay(near, order.last), got)
+    def inner_beside(near, got, second):
+        other = lax.ppermute(second, "rep", SWAP)
+        return lax.cond(t < tp, inner, lambda near, got: near[0], near, got), other
+
+    second = relay(second, order.last)
+    latent, second_other = lax.cond(
+        t < tp,
+        inner_beside,
+        lambda near, got, second: (near[0], second),
+        near,
+        got,
+        second,
+    )
     kept, (r, i), (late, k), *others = terms[0]
     r = relay(r, latent)
-    second = relay(second, got)
-    second_other = relay(lax.ppermute(second, "rep", SWAP), r)
+    second_other = relay(second_other, r)
     twins = lax.cond(t < tp, swap, lambda *arrays: list(arrays), second, second_other)
     latent = relay(latent, twins[1])
     got = lax.cond(t < tp, outer, lambda latent: [latent.astype(jnp.bfloat16)] * 3, latent)

time: 113 us -> 113 us (level)
    ppermute x11, waiting for transfers between devices: 11.9 us -> 7.18 us  [across(): return lax.ppermute(array, 'tp', [(i, i ^ step) for i in range(tp)])]
    ppermute x1, waiting for transfers between devices: 0.01 us -> 4.44 us  [inner_beside(): other = lax.ppermute(second, 'rep', SWAP)]
  transfers between devices with their start and end apart: 20 -> 20, of which waited for: 10 -> 12; matrix products, arithmetic and copies ran while one was open for 2% -> 2% of each run, Pallas kernels for 44% -> 44%
where the time goes in v8:
time: 113 us; the launch traced here: 112 us
  Pallas kernels  56.4 us (50%)
  starting transfers between devices  28.1 us (25%)
  waiting for transfers between devices  25.1 us (22%)
  other arithmetic  2.47 us (2%)
    pallas_call x3, Pallas kernels, block_products(): pl.pallas_call(kernel, name='products', out_shape=out_shape, grid_spec=pl...  33.9 us
    ppermute x11, starting transfers between devices, across(): return lax.ppermute(array, 'tp', [(i, i ^ step) for i in range(tp)])  15.3 us
    all_to_all x1, starting transfers between devices, local(): lax.all_to_all(factors, 'tp', split_axis=0, concat_axis=0, tiled=True)  7.26 us
    ppermute x11, waiting for transfers between devices, across(): return lax.ppermute(array, 'tp', [(i, i ^ step) for i in range(tp)])  7.18 us
    pallas_call x3, Pallas kernels, fold(): pl.pallas_call(kernel, name='fold', grid=(1,), out_shape=out_shape, in_sp...  6.96 us
    all_to_all x1, waiting for transfers between devices, local(): lax.all_to_all(factors, 'tp', split_axis=0, concat_axis=0, tiled=True)  5.82 us
    pallas_call x1, Pallas kernels, latent_terms(): pl.pallas_call(kernel, name='latent_terms', out_shape=[jax.ShapeDtypeStru...  5.78 us
    ppermute x1, waiting for transfers between devices, inner_beside(): other = lax.ppermute(second, 'rep', SWAP)  4.44 us
  transfers between devices with their start and end apart: 20, of which 12 were waited for; matrix products, arithmetic and copies ran while one was open for 2% of the time, Pallas kernels for 44%

profile of v8, /device:TPU:0, one launch (start us, length us, event | category | flops | bytes accessed | tf_op | source)
XLA Modules:
  0.0 112.1 jit_solution(8628176087121788930)
XLA Ops:
  0.0 2.7 %pack_factors.1.after_ref = bf16[8,64,2304]{2,1,0:T(8,128)(2,1)} custom-call(s32[1]{0:T(128)} %bitcast.4.y_ref, bf16[64,28672]{1,0:T(8,128)(2,1)} %bitcast.19, bf16[64,8192]{1,0:T(8,128)(2,1)} %bitcast.20), custom_call_target="tpu_custom_call" | custom-call | flops 1 | bytes 1 | tf_op jit(solution)/shard_map/pack_factors/pallas_call | solution.py:112
  2.7 7.3 %all-to-all-start = ((bf16[8,64,2304]{2,1,0:T(8,128)(2,1)}), bf16[8,64,2304]{2,1,0:T(8,128)(2,1)}, u32[]{:S(2)}, u32[]{:S(2)}) async-start(bf16[8,64,2304]{2,1,0:T(8,128)(2,1)} %pack_factors.1.after_ref), calls=%async_computation | async-start | bytes 4718592 | tf_op jit(solution)/shard_map/all_to_all | solution.py:385
  9.9 3.1 %pack_hidden.1 = (bf16[272,1792]{1,0:T(8,128)(2,1)}, bf16[272,1792]{1,0:T(8,128)(2,1)}) custom-call(s32[1]{0:T(128)} %bitcast.4.y_ref, bf16[256,3584]{1,0:T(8,128)(2,1)} %hidden_ref.7, s32[1,256]{1,0:T(1,128)} %bitcast.21, bf16[8,64,2304]{2,1,0:T(8,128)(2,1)} %pack_factors.1.after_ref), custom_call_target="tpu_custom_call" | custom-call | flops 1 | bytes 1 | tf_op jit(solution)/shard_map/pack_hidden/pallas_call | solution.py:165
  13.1 0.7 collective-permute-start.10
  13.8 0.9 collective-permute-start.9
  14.7 0.3 collective-permute-start.8
  15.0 6.5 %products.3.after_ref = bf16[1,256,1024]{2,1,0:T(8,128)(2,1)} custom-call(s32[1]{0:T(128)} %bitcast.11.t_ref, bf16[256,3584]{1,0:T(8,128)(2,1)} %hidden_ref.7, bf16[3584,8192]{1,0:T(8,128)(2,1)} %weight_ref.5, bf16[272,1792]{1,0:T(8,128)(2,1)} %get-tuple-element.62.after_ref.refs_0_), custom_call_target="tpu_custom_call" | custom-call | flops 1 | bytes 1 | tf_op jit(solution)/shard_map/products/pallas_call | solution.py:54
  21.5 2.0 %collective-permute-start.11 = (bf16[1,256,1024]{2,1,0:T(8,128)(2,1)}, bf16[1,256,1024]{2,1,0:T(8,128)(2,1)}, u32[]{:S(2)}, u32[]{:S(2)}) collective-permute-start(bf16[1,256,1024]{2,1,0:T(8,128)(2,1)} %products.3.after_ref), channel_id=1, source_target_pairs={{0,2},{2,0},{4,6},{6,4},{8,10},{10,8},{12,14},{14,12},{1,3},{3,1},... | collective-permute-start | bytes 1572872 | tf_op jit(solution)/shard_map/ppermute | solution.py:381
  23.5 9.2 %products.4 = (bf16[1,256,1024]{2,1,0:T(8,128)(2,1)}, f32[1,256,1024]{2,1,0:T(8,128)}) custom-call(s32[1]{0:T(128)} %bitcast.11.t_ref, bf16[256,3584]{1,0:T(8,128)(2,1)} %hidden_ref.7, bf16[3584,8192]{1,0:T(8,128)(2,1)} %weight_ref.5, bf16[1,256,1024]{2,1,0:T(8,128)(2,1)} %products.3.after_ref), custom_call_target="tpu_custom_call" | custom-call | flops 1 | bytes 1 | tf_op jit(solution)/shard_map/products/pallas_call | solution.py:54
  32.7 0.0 collective-permute-start.14
  32.7 18.2 %products.5 = (bf16[1,256,1024]{2,1,0:T(8,128)(2,1)}, bf16[1,256,1024]{2,1,0:T(8,128)(2,1)}, f32[3,256,1024]{2,1,0:T(8,128)}) custom-call(s32[1]{0:T(128)} %bitcast.11.t_ref, bf16[256,3584]{1,0:T(8,128)(2,1)} %hidden_ref.7, bf16[3584,8192]{1,0:T(8,128)(2,1)} %weight_ref.5, f32[1,256,1024]{2,1,0:T(8,128)} %get-tuple-element.64.after_ref.refs_0_), custom_call_target="tpu_custom_call" | custom-call | flops 1 | bytes 1 | tf_op jit(solution)/shard_map/products/pallas_call | solution.py:54
  50.9 2.2 %fold.3.refs_4_ = bf16[1,256,1024]{2,1,0:T(8,128)(2,1)} custom-call(f32[1,256,1024]{2,1,0:T(8,128)} %get-tuple-element.64.after_ref.refs_0_, bf16[1,256,1024]{2,1,0:T(8,128)(2,1)} %collective-permute-done.11.refs_1_, f32[3,256,1024]{2,1,0:T(8,128)} %get-tuple-element.65.refs_2_.refs_0_.refs_9_), custom_call_target="tpu_custom_call" | custom-call | flops 1 | bytes 1 | tf_op jit(solution)/shard_map/fold/pallas_call | solution.py:264
  53.2 2.0 %collective-permute-start.15 = (bf16[1,256,1024]{2,1,0:T(8,128)(2,1)}, bf16[1,256,1024]{2,1,0:T(8,128)(2,1)}, u32[]{:S(2)}, u32[]{:S(2)}) collective-permute-start(bf16[1,256,1024]{2,1,0:T(8,128)(2,1)} %fold.3.refs_4_), channel_id=1, source_target_pairs={{0,4},{2,6},{4,0},{6,2},{8,12},{10,14},{12,8},{14,10},{1,5},{3,7},... | collective-permute-start | bytes 1572872 | tf_op jit(solution)/shard_map/ppermute | solution.py:381
  55.2 1.5 %collective-permute-start.13 = (bf16[1,256,1024]{2,1,0:T(8,128)(2,1)}, bf16[1,256,1024]{2,1,0:T(8,128)(2,1)}, u32[]{:S(2)}, u32[]{:S(2)}) collective-permute-start(bf16[1,256,1024]{2,1,0:T(8,128)(2,1)} %get-tuple-element.69), channel_id=1, source_target_pairs={{0,2},{2,0},{4,6},{6,4},{8,10},{10,8},{12,14},{14,12},{1,3},{3,1},... | collective-permute-start | bytes 1572872 | tf_op jit(solution)/shard_map/ppermute | solution.py:381
  56.6 1.6 %collective-permute-done.9.refs_2_ = bf16[272,1792]{1,0:T(8,128)(2,1)} collective-permute-done((bf16[272,1792]{1,0:T(8,128)(2,1)}, bf16[272,1792]{1,0:T(8,128)(2,1)}, u32[]{:S(2)}, u32[]{:S(2)}) %collective-permute-start.9) | collective-permute-done | bytes 974880 | tf_op jit(solution)/shard_map/ppermute | solution.py:388
  58.2 5.8 %all-to-all-done = bf16[8,64,2304]{2,1,0:T(8,128)(2,1)} async-done(((bf16[8,64,2304]{2,1,0:T(8,128)(2,1)}), bf16[8,64,2304]{2,1,0:T(8,128)(2,1)}, u32[]{:S(2)}, u32[]{:S(2)}) %all-to-all-start) | async-done | bytes 2359328 | tf_op jit(solution)/shard_map/all_to_all | solution.py:385
  64.0 5.8 %latent_terms.1 = (f32[2,64,256]{2,1,0:T(8,128)}, f32[2,64,256]{2,1,0:T(8,128)}, bf16[512,512]{1,0:T(8,128)(2,1)}) custom-call(s32[1]{0:T(128)} %bitcast.5.g_ref, bf16[512,2304]{1,0:T(8,128)(2,1)} %bitcast.9.factors_ref, bf16[272,1792]{1,0:T(8,128)(2,1)} %get-tuple-element.62.after_ref.refs_0_, bf16[272,1792]{1,0:T(8,128)(2,1)} %collective-permute-done.8.refs_1_, ...), custom_call_target="tpu_custom_call" | custom-call | flops 1 | bytes 1 | tf_op jit(solution)/shard_map/latent_terms/pallas_call | solution.py:220
  69.8 1.5 %collective-permute-start.12 = (f32[2,64,256]{2,1,0:T(8,128)}, f32[2,64,256]{2,1,0:T(8,128)}, u32[]{:S(2)}, u32[]{:S(2)}) collective-permute-start(f32[2,64,256]{2,1,0:T(8,128)} %get-tuple-element.67), channel_id=1, source_target_pairs={{0,16},{16,0},{1,17},{17,1},{2,18},{18,2},{3,19},{19,3},{4,20},{20... | collective-permute-start | bytes 393224 | tf_op jit(solution)/shard_map/ppermute | solution.py:421
  71.3 1.5 %collective-permute-start.16 = (bf16[1,256,1024]{2,1,0:T(8,128)(2,1)}, bf16[1,256,1024]{2,1,0:T(8,128)(2,1)}, u32[]{:S(2)}, u32[]{:S(2)}) collective-permute-start(bf16[1,256,1024]{2,1,0:T(8,128)(2,1)} %get-tuple-element.73), channel_id=1, source_target_pairs={{0,2},{2,0},{4,6},{6,4},{8,10},{10,8},{12,14},{14,12},{1,3},{3,1},... | collective-permute-start | bytes 1572872 | tf_op jit(solution)/shard_map/ppermute | solution.py:381
  72.8 2.3 %collective-permute-done.12.refs_1_ = f32[2,64,256]{2,1,0:T(8,128)} collective-permute-done((f32[2,64,256]{2,1,0:T(8,128)}, f32[2,64,256]{2,1,0:T(8,128)}, u32[]{:S(2)}, u32[]{:S(2)}) %collective-permute-start.12) | collective-permute-done | bytes 131104 | tf_op jit(solution)/shard_map/ppermute | solution.py:421
  75.1 0.1 collective-permute-done.15.refs_2_
  75.2 2.5 %fold.4.refs_2_ = bf16[1,256,1024]{2,1,0:T(8,128)(2,1)} custom-call(f32[3,256,1024]{2,1,0:T(8,128)} %get-tuple-element.65.refs_2_.refs_0_.refs_9_, bf16[1,256,1024]{2,1,0:T(8,128)(2,1)} %collective-permute-done.14.refs_1_, bf16[1,256,1024]{2,1,0:T(8,128)(2,1)} %collective-permute-done.15.refs_2_, f32[2,64,256]{2,1,0:T(8,128)} %relay.6.refs_3_), custom_call_target="tpu_custom_call" | custom-call | flops 1 | bytes 1 | tf_op jit(solution)/shard_map/fold/pallas_call | solution.py:264
  77.6 0.4 collective-permute-start.17
  78.0 2.3 %fold.5.refs_1_ = bf16[1,256,1024]{2,1,0:T(8,128)(2,1)} custom-call(f32[3,256,1024]{2,1,0:T(8,128)} %get-tuple-element.65.refs_2_.refs_0_.refs_9_, bf16[1,256,1024]{2,1,0:T(8,128)(2,1)} %collective-permute-done.13.refs_1_, bf16[1,256,1024]{2,1,0:T(8,128)(2,1)} %fold.4.refs_2_), custom_call_target="tpu_custom_call" | custom-call | flops 1 | bytes 1 | tf_op jit(solution)/shard_map/fold/pallas_call | solution.py:264
  80.3 2.8 %collective-permute-start.18 = (bf16[1,256,1024]{2,1,0:T(8,128)(2,1)}, bf16[1,256,1024]{2,1,0:T(8,128)(2,1)}, u32[]{:S(2)}, u32[]{:S(2)}) collective-permute-start(bf16[1,256,1024]{2,1,0:T(8,128)(2,1)} %fold.5.refs_1_), channel_id=1, source_target_pairs={{0,4},{2,6},{4,0},{6,2},{8,12},{10,14},{12,8},{14,10},{1,5},{3,7},... | collective-permute-start | bytes 1572872 | tf_op jit(solution)/shard_map/ppermute | solution.py:381
  83.1 13.3 %conditional.4 = (f32[64,256]{1,0:T(8,128)}, bf16[512,512]{1,0:T(8,128)(2,1)}) conditional(s32[]{:T(128)} %convert_element_type.14, (f32[2,64,256]{2,1,0:T(8,128)}, bf16[512,512]{1,0:T(8,128)(2,1)}) %tuple.34, (s32[]{:T(128)}, f32[2,64,256]{2,1,0:T(8,128)}, f32[2,64,256]{2,1,0:T(8,128)}, bf16[512,512]{1,0:T(8,128)(2,1)}) %tuple.35), branch_computations={%region_0.0_spmd, %region_1.0_spmd} | conditional | flops 65538 | bytes 3539118 | solution.py:452
  83.1 1.5 %collective-permute-start.7 = (bf16[512,512]{1,0:T(8,128)(2,1)}, bf16[512,512]{1,0:T(8,128)(2,1)}, u32[]{:S(2)}, u32[]{:S(2)}) collective-permute-start(bf16[512,512]{1,0:T(8,128)(2,1)} %get-tuple-element.42), channel_id=1, source_target_pairs={{0,16},{16,0},{1,17},{17,1},{2,18},{18,2},{3,19},{19,3},{4,20},{20... | collective-permute-start | bytes 1572872 | tf_op jit(solution)/shard_map/cond/branch_1_fun/ppermute | solution.py:448
  84.6 7.3 %conditional = (f32[64,256]{1,0:T(8,128)}) conditional(s32[]{:T(128)} %convert_element_type.3, f32[2,64,256]{2,1,0:T(8,128)} %get-tuple-element.40, (f32[2,64,256]{2,1,0:T(8,128)}, f32[2,64,256]{2,1,0:T(8,128)}) %tuple.25), branch_computations={%region_2.0_spmd, %region_3.0_spmd} | conditional | flops 65536 | bytes 1441880 | solution.py:449
  84.6 1.0 add.6
  85.6 0.1 collective-permute-start.5
  85.7 1.2 %collective-permute-done.5 = f32[64,256]{1,0:T(8,128)S(1)} collective-permute-done((f32[64,256]{1,0:T(8,128)S(1)}, f32[64,256]{1,0:T(8,128)S(1)}, u32[]{:S(2)}, u32[]{:S(2)}) %collective-permute-start.5) | collective-permute-done | bytes 65568 | tf_op jit(solution)/shard_map/cond/branch_1_fun/cond/branch_1_fun/ppermute | solution.py:432
  86.9 0.8 collective-permute-start.6
  87.7 3.6 %collective-permute-done.6 = f32[64,256]{1,0:T(8,128)S(1)} collective-permute-done((f32[64,256]{1,0:T(8,128)S(1)}, f32[64,256]{1,0:T(8,128)S(1)}, u32[]{:S(2)}, u32[]{:S(2)}) %collective-permute-start.6) | collective-permute-done | bytes 65568 | tf_op jit(solution)/shard_map/cond/branch_1_fun/cond/branch_1_fun/ppermute | solution.py:381
  91.3 0.6 add.8
  91.9 4.4 %collective-permute-done.7 = bf16[512,512]{1,0:T(8,128)(2,1)} collective-permute-done((bf16[512,512]{1,0:T(8,128)(2,1)}, bf16[512,512]{1,0:T(8,128)(2,1)}, u32[]{:S(2)}, u32[]{:S(2)}) %collective-permute-start.7) | collective-permute-done | bytes 524320 | tf_op jit(solution)/shard_map/cond/branch_1_fun/ppermute | solution.py:448
  96.4 3.0 %conditional.5 = (bf16[512,512]{1,0:T(8,128)(2,1)}, bf16[512,512]{1,0:T(8,128)(2,1)}) conditional(s32[]{:T(128)} %convert_element_type.14, (bf16[512,512]{1,0:T(8,128)(2,1)}, bf16[512,512]{1,0:T(8,128)(2,1)}) %tuple.36, (bf16[512,512]{1,0:T(8,128)(2,1)}, bf16[512,512]{1,0:T(8,128)(2,1)}) %tuple.36), branch_computations={%region_4.0_spmd, %region_5.0_spmd} | conditional | bytes 4194400 | solution.py:463
  96.4 0.5 collective-permute-start.1
  96.9 1.7 %collective-permute-done = bf16[512,512]{1,0:T(8,128)(2,1)} collective-permute-done((bf16[512,512]{1,0:T(8,128)(2,1)}, bf16[512,512]{1,0:T(8,128)(2,1)}, u32[]{:S(2)}, u32[]{:S(2)}) %collective-permute-start) | collective-permute-done | bytes 524320 | tf_op jit(solution)/shard_map/cond/branch_1_fun/ppermute | solution.py:445
  98.6 0.7 collective-permute-done.1
  99.4 8.8 %conditional.6 = (bf16[64,256]{1,0:T(8,128)(2,1)}, bf16[64,256]{1,0:T(8,128)(2,1)}, bf16[64,256]{1,0:T(8,128)(2,1)}) conditional(s32[]{:T(128)} %convert_element_type.14, f32[64,256]{1,0:T(8,128)} %relay.10.refs_0_, f32[64,256]{1,0:T(8,128)} %relay.10.refs_0_), branch_computations={%region_6.0_spmd, %region_7.0_spmd} | conditional | flops 16384 | bytes 491664 | solution.py:465
  99.4 0.8 convert_element_type.12
  100.2 1.5 %collective-permute-start.4 = (bf16[64,256]{1,0:T(8,128)(2,1)S(1)}, bf16[64,256]{1,0:T(8,128)(2,1)}, u32[]{:S(2)}, u32[]{:S(2)}) collective-permute-start(bf16[64,256]{1,0:T(8,128)(2,1)S(1)} %convert_element_type.12), channel_id=1, source_target_pairs={{0,12},{2,14},{4,8},{6,10},{8,4},{10,6},{12,0},{14,2},{1,13},{3,15... | collective-permute-start | bytes 98312 | tf_op jit(solution)/shard_map/cond/branch_1_fun/ppermute | solution.py:381
  101.8 0.2 collective-permute-start.3
  102.0 2.6 %collective-permute-start.2 = (bf16[64,256]{1,0:T(8,128)(2,1)S(1)}, bf16[64,256]{1,0:T(8,128)(2,1)}, u32[]{:S(2)}, u32[]{:S(2)}) collective-permute-start(bf16[64,256]{1,0:T(8,128)(2,1)S(1)} %convert_element_type.12), channel_id=1, source_target_pairs={{0,4},{2,6},{4,0},{6,2},{8,12},{10,14},{12,8},{14,10},{1,5},{3,7},... | collective-permute-start | bytes 98312 | tf_op jit(solution)/shard_map/cond/branch_1_fun/ppermute | solution.py:381
  104.6 1.5 %collective-permute-done.4 = bf16[64,256]{1,0:T(8,128)(2,1)} collective-permute-done((bf16[64,256]{1,0:T(8,128)(2,1)S(1)}, bf16[64,256]{1,0:T(8,128)(2,1)}, u32[]{:S(2)}, u32[]{:S(2)}) %collective-permute-start.4) | collective-permute-done | bytes 32800 | tf_op jit(solution)/shard_map/cond/branch_1_fun/ppermute | solution.py:381
  106.1 0.9 collective-permute-done.3
  107.0 1.1 %collective-permute-done.2 = bf16[64,256]{1,0:T(8,128)(2,1)} collective-permute-done((bf16[64,256]{1,0:T(8,128)(2,1)S(1)}, bf16[64,256]{1,0:T(8,128)(2,1)}, u32[]{:S(2)}, u32[]{:S(2)}) %collective-permute-start.2) | collective-permute-done | bytes 32800 | tf_op jit(solution)/shard_map/cond/branch_1_fun/ppermute | solution.py:381
  108.1 4.0 %finish.1 = bf16[256,1024]{1,0:T(8,128)(2,1)} custom-call(s32[1]{0:T(128)} %bitcast.4.y_ref, s32[1]{0:T(128)} %bitcast.5.g_ref, f32[64,256]{1,0:T(8,128)} %relay.10.refs_0_, bf16[64,256]{1,0:T(8,128)(2,1)} %get-tuple-element.75.refs_1_, bf16[64,256]{1,0:T(8,128)(2,1)} %get-tuple-element.76.refs_2_, bf16[64,256]{1,0:T(8,128)(2,1)} %get-tuple-element.77.refs_1_.refs_3_, ...), custom_call_target="tpu_custom_call" | custom-call | flops 1 | bytes 1 | tf_op jit(solution)/shard_map/finish/pallas_call | solution.py:353
  (17 shorter events, 0.0 us)
Async XLA Ops:
  2.7 61.4 %all-to-all-start = ((bf16[8,64,2304]{2,1,0:T(8,128)(2,1)}), bf16[8,64,2304]{2,1,0:T(8,128)(2,1)}, u32[]{:S(2)}, u32[]{:S(2)}) async-start(bf16[8,64,2304]{2,1,0:T(8,128)(2,1)} %pack_factors.1.after_ref), calls=%async_computation | async-start | bytes 4718592 | tf_op jit(solution)/shard_map/all_to_all | solution.py:385
  13.1 42.1 %collective-permute-start.10 = (bf16[272,1792]{1,0:T(8,128)(2,1)}, bf16[272,1792]{1,0:T(8,128)(2,1)}, u32[]{:S(2)}, u32[]{:S(2)}) collective-permute-start(bf16[272,1792]{1,0:T(8,128)(2,1)} %get-tuple-element.63), channel_id=1, source_target_pairs={{0,17},{1,16},{16,1},{17,0},{2,19},{3,18},{18,3},{19,2},{4,21},{5,... | collective-permute-start | bytes 2924552 | tf_op jit(solution)/shard_map/ppermute | solution.py:390
  13.8 44.4 %collective-permute-start.9 = (bf16[272,1792]{1,0:T(8,128)(2,1)}, bf16[272,1792]{1,0:T(8,128)(2,1)}, u32[]{:S(2)}, u32[]{:S(2)}) collective-permute-start(bf16[272,1792]{1,0:T(8,128)(2,1)} %get-tuple-element.63), channel_id=1, source_target_pairs={{0,16},{16,0},{1,17},{17,1},{2,18},{18,2},{3,19},{19,3},{4,20},{20... | collective-permute-start | bytes 2924552 | tf_op jit(solution)/shard_map/ppermute | solution.py:388
  14.7 43.5 %collective-permute-start.8 = (bf16[272,1792]{1,0:T(8,128)(2,1)}, bf16[272,1792]{1,0:T(8,128)(2,1)}, u32[]{:S(2)}, u32[]{:S(2)}) collective-permute-start(bf16[272,1792]{1,0:T(8,128)(2,1)} %get-tuple-element.62.after_ref.refs_0_), channel_id=1, source_target_pairs={{0,1},{1,0},{2,3},{3,2},{4,5},{5,4},{6,7},{7,6},{8,9},{9,8},{10,11... | collective-permute-start | bytes 2924552 | tf_op jit(solution)/shard_map/ppermute | solution.py:389
  21.5 29.4 %collective-permute-start.11 = (bf16[1,256,1024]{2,1,0:T(8,128)(2,1)}, bf16[1,256,1024]{2,1,0:T(8,128)(2,1)}, u32[]{:S(2)}, u32[]{:S(2)}) collective-permute-start(bf16[1,256,1024]{2,1,0:T(8,128)(2,1)} %products.3.after_ref), channel_id=1, source_target_pairs={{0,2},{2,0},{4,6},{6,4},{8,10},{10,8},{12,14},{14,12},{1,3},{3,1},... | collective-permute-start | bytes 1572872 | tf_op jit(solution)/shard_map/ppermute | solution.py:381
  32.7 42.5 %collective-permute-start.14 = (bf16[1,256,1024]{2,1,0:T(8,128)(2,1)}, bf16[1,256,1024]{2,1,0:T(8,128)(2,1)}, u32[]{:S(2)}, u32[]{:S(2)}) collective-permute-start(bf16[1,256,1024]{2,1,0:T(8,128)(2,1)} %get-tuple-element.70), channel_id=1, source_target_pairs={{0,2},{2,0},{4,6},{6,4},{8,10},{10,8},{12,14},{14,12},{1,3},{3,1},... | collective-permute-start | bytes 1572872 | tf_op jit(solution)/shard_map/ppermute | solution.py:381
  53.2 22.0 %collective-permute-start.15 = (bf16[1,256,1024]{2,1,0:T(8,128)(2,1)}, bf16[1,256,1024]{2,1,0:T(8,128)(2,1)}, u32[]{:S(2)}, u32[]{:S(2)}) collective-permute-start(bf16[1,256,1024]{2,1,0:T(8,128)(2,1)} %fold.3.refs_4_), channel_id=1, source_target_pairs={{0,4},{2,6},{4,0},{6,2},{8,12},{10,14},{12,8},{14,10},{1,5},{3,7},... | collective-permute-start | bytes 1572872 | tf_op jit(solution)/shard_map/ppermute | solution.py:381
  55.2 22.9 %collective-permute-start.13 = (bf16[1,256,1024]{2,1,0:T(8,128)(2,1)}, bf16[1,256,1024]{2,1,0:T(8,128)(2,1)}, u32[]{:S(2)}, u32[]{:S(2)}) collective-permute-start(bf16[1,256,1024]{2,1,0:T(8,128)(2,1)} %get-tuple-element.69), channel_id=1, source_target_pairs={{0,2},{2,0},{4,6},{6,4},{8,10},{10,8},{12,14},{14,12},{1,3},{3,1},... | collective-permute-start | bytes 1572872 | tf_op jit(solution)/shard_map/ppermute | solution.py:381
  69.8 5.3 %collective-permute-start.12 = (f32[2,64,256]{2,1,0:T(8,128)}, f32[2,64,256]{2,1,0:T(8,128)}, u32[]{:S(2)}, u32[]{:S(2)}) collective-permute-start(f32[2,64,256]{2,1,0:T(8,128)} %get-tuple-element.67), channel_id=1, source_target_pairs={{0,16},{16,0},{1,17},{17,1},{2,18},{18,2},{3,19},{19,3},{4,20},{20... | collective-permute-start | bytes 393224 | tf_op jit(solution)/shard_map/ppermute | solution.py:421
  71.3 25.0 %collective-permute-start.16 = (bf16[1,256,1024]{2,1,0:T(8,128)(2,1)}, bf16[1,256,1024]{2,1,0:T(8,128)(2,1)}, u32[]{:S(2)}, u32[]{:S(2)}) collective-permute-start(bf16[1,256,1024]{2,1,0:T(8,128)(2,1)} %get-tuple-element.73), channel_id=1, source_target_pairs={{0,2},{2,0},{4,6},{6,4},{8,10},{10,8},{12,14},{14,12},{1,3},{3,1},... | collective-permute-start | bytes 1572872 | tf_op jit(solution)/shard_map/ppermute | solution.py:381
  77.6 30.5 %collective-permute-start.17 = (bf16[1,256,1024]{2,1,0:T(8,128)(2,1)}, bf16[1,256,1024]{2,1,0:T(8,128)(2,1)}, u32[]{:S(2)}, u32[]{:S(2)}) collective-permute-start(bf16[1,256,1024]{2,1,0:T(8,128)(2,1)} %fold.4.refs_2_), channel_id=1, source_target_pairs={{0,8},{2,10},{4,12},{6,14},{8,0},{10,2},{12,4},{14,6},{1,9},{3,11}... | collective-permute-start | bytes 1572872 | tf_op jit(solution)/shard_map/ppermute | solution.py:381
  80.3 27.9 %collective-permute-start.18 = (bf16[1,256,1024]{2,1,0:T(8,128)(2,1)}, bf16[1,256,1024]{2,1,0:T(8,128)(2,1)}, u32[]{:S(2)}, u32[]{:S(2)}) collective-permute-start(bf16[1,256,1024]{2,1,0:T(8,128)(2,1)} %fold.5.refs_1_), channel_id=1, source_target_pairs={{0,4},{2,6},{4,0},{6,2},{8,12},{10,14},{12,8},{14,10},{1,5},{3,7},... | collective-permute-start | bytes 1572872 | tf_op jit(solution)/shard_map/ppermute | solution.py:381
  83.1 13.3 %collective-permute-start.7 = (bf16[512,512]{1,0:T(8,128)(2,1)}, bf16[512,512]{1,0:T(8,128)(2,1)}, u32[]{:S(2)}, u32[]{:S(2)}) collective-permute-start(bf16[512,512]{1,0:T(8,128)(2,1)} %get-tuple-element.42), channel_id=1, source_target_pairs={{0,16},{16,0},{1,17},{17,1},{2,18},{18,2},{3,19},{19,3},{4,20},{20... | collective-permute-start | bytes 1572872 | tf_op jit(solution)/shard_map/cond/branch_1_fun/ppermute | solution.py:448
  85.6 1.3 %collective-permute-start.5 = (f32[64,256]{1,0:T(8,128)S(1)}, f32[64,256]{1,0:T(8,128)S(1)}, u32[]{:S(2)}, u32[]{:S(2)}) collective-permute-start(f32[64,256]{1,0:T(8,128)S(1)} %slice_bitcast_fusion.2), channel_id=1, source_target_pairs={{0,1},{1,0},{2,3},{3,2},{4,5},{5,4},{6,7},{7,6},{8,9},{9,8},{10,11... | collective-permute-start | bytes 196616 | tf_op jit(solution)/shard_map/cond/branch_1_fun/cond/branch_1_fun/ppermute | solution.py:432
  86.9 4.3 %collective-permute-start.6 = (f32[64,256]{1,0:T(8,128)S(1)}, f32[64,256]{1,0:T(8,128)S(1)}, u32[]{:S(2)}, u32[]{:S(2)}) collective-permute-start(f32[64,256]{1,0:T(8,128)S(1)} %fusion), channel_id=1, source_target_pairs={{0,2},{2,0},{4,6},{6,4},{8,10},{10,8},{12,14},{14,12},{1,3},{3,1},... | collective-permute-start | bytes 196616 | tf_op jit(solution)/shard_map/cond/branch_1_fun/cond/branch_1_fun/ppermute | solution.py:381
  96.4 2.3 %collective-permute-start = (bf16[512,512]{1,0:T(8,128)(2,1)}, bf16[512,512]{1,0:T(8,128)(2,1)}, u32[]{:S(2)}, u32[]{:S(2)}) collective-permute-start(bf16[512,512]{1,0:T(8,128)(2,1)} %get-tuple-element.43), channel_id=1, source_target_pairs={{0,1},{1,0},{2,3},{3,2},{4,5},{5,4},{6,7},{7,6},{8,9},{9,8},{10,11... | collective-permute-start | bytes 1572872 | tf_op jit(solution)/shard_map/cond/branch_1_fun/ppermute | solution.py:445
  96.4 3.0 %collective-permute-start.1 = (bf16[512,512]{1,0:T(8,128)(2,1)}, bf16[512,512]{1,0:T(8,128)(2,1)}, u32[]{:S(2)}, u32[]{:S(2)}) collective-permute-start(bf16[512,512]{1,0:T(8,128)(2,1)} %get-tuple-element.44), channel_id=1, source_target_pairs={{0,1},{1,0},{2,3},{3,2},{4,5},{5,4},{6,7},{7,6},{8,9},{9,8},{10,11... | collective-permute-start | bytes 1572872 | tf_op jit(solution)/shard_map/cond/branch_1_fun/ppermute | solution.py:445
  100.2 5.9 %collective-permute-start.4 = (bf16[64,256]{1,0:T(8,128)(2,1)S(1)}, bf16[64,256]{1,0:T(8,128)(2,1)}, u32[]{:S(2)}, u32[]{:S(2)}) collective-permute-start(bf16[64,256]{1,0:T(8,128)(2,1)S(1)} %convert_element_type.12), channel_id=1, source_target_pairs={{0,12},{2,14},{4,8},{6,10},{8,4},{10,6},{12,0},{14,2},{1,13},{3,15... | collective-permute-start | bytes 98312 | tf_op jit(solution)/shard_map/cond/branch_1_fun/ppermute | solution.py:381
  101.8 5.2 %collective-permute-start.3 = (bf16[64,256]{1,0:T(8,128)(2,1)S(1)}, bf16[64,256]{1,0:T(8,128)(2,1)}, u32[]{:S(2)}, u32[]{:S(2)}) collective-permute-start(bf16[64,256]{1,0:T(8,128)(2,1)S(1)} %convert_element_type.12), channel_id=1, source_target_pairs={{0,8},{2,10},{4,12},{6,14},{8,0},{10,2},{12,4},{14,6},{1,9},{3,11}... | collective-permute-start | bytes 98312 | tf_op jit(solution)/shard_map/cond/branch_1_fun/ppermute | solution.py:381
  102.0 6.2 %collective-permute-start.2 = (bf16[64,256]{1,0:T(8,128)(2,1)S(1)}, bf16[64,256]{1,0:T(8,128)(2,1)}, u32[]{:S(2)}, u32[]{:S(2)}) collective-permute-start(bf16[64,256]{1,0:T(8,128)(2,1)S(1)} %convert_element_type.12), channel_id=1, source_target_pairs={{0,4},{2,6},{4,0},{6,2},{8,12},{10,14},{12,8},{14,10},{1,5},{3,7},... | collective-permute-start | bytes 98312 | tf_op jit(solution)/shard_map/cond/branch_1_fun/ppermute | solution.py:381

commit v9 on v8

--- a/solution.py
+++ b/solution.py
@@ -427,6 +427,9 @@
     for items in rest:
         pass_on(items)
 
+    def swap(*arrays):
+        return [lax.ppermute(array, "grp", SWAP) for array in arrays]
+
     def inner(near, got):
         held = near + got
         latent = held[0] + lax.ppermute(held[1], "grp", SWAP)
@@ -441,18 +444,16 @@
         sent = latent.astype(jnp.bfloat16)
         return [across(sent, i * step) for i in range(1, 4)]
 
-    def swap(*arrays):
-        return [lax.ppermute(array, "grp", SWAP) for array in arrays]
-
     def inner_beside(near, got, second):
         other = lax.ppermute(second, "rep", SWAP)
-        return lax.cond(t < tp, inner, lambda near, got: near[0], near, got), other
+        held = lax.cond(t < tp, swap, lambda *arrays: list(arrays), second)
+        return lax.cond(t < tp, inner, lambda near, got: near[0], near, got), other, held[0]
 
     second = relay(second, order.last)
-    latent, second_other = lax.cond(
+    latent, second_other, twin = lax.cond(
         t < tp,
         inner_beside,
-        lambda near, got, second: (near[0], second),
+        lambda near, got, second: (near[0], second, second),
         near,
         got,
         second,
@@ -460,7 +461,7 @@
     kept, (r, i), (late, k), *others = terms[0]
     r = relay(r, latent)
     second_other = relay(second_other, r)
-    twins = lax.cond(t < tp, swap, lambda *arrays: list(arrays), second, second_other)
+    twins = [twin, *lax.cond(t < tp, swap, lambda *arrays: list(arrays), second_other)]
     latent = relay(latent, twins[1])
     got = lax.cond(t < tp, outer, lambda latent: [latent.astype(jnp.bfloat16)] * 3, latent)
     latents = [latent, *got]

time: 113 us -> 113 us (level)
    ppermute x1, waiting for transfers between devices: 4.44 us -> 2.19 us  [inner_beside(): other = lax.ppermute(second, 'rep', SWAP)]
    ppermute x2, waiting for transfers between devices: 2.49 us -> 4.49 us  [swap(): return [lax.ppermute(array, 'grp', SWAP) for array in arrays]]
where the time goes in v9:
time: 113 us; the launch traced here: 112 us
  Pallas kernels  56.4 us (50%)
  starting transfers between devices  27.7 us (25%)
  waiting for transfers between devices  25.4 us (22%)
  other arithmetic  2.47 us (2%)
    pallas_call x3, Pallas kernels, block_products(): pl.pallas_call(kernel, name='products', out_shape=out_shape, grid_spec=pl...  33.9 us
    ppermute x11, starting transfers between devices, across(): return lax.ppermute(array, 'tp', [(i, i ^ step) for i in range(tp)])  15.3 us
    ppermute x11, waiting for transfers between devices, across(): return lax.ppermute(array, 'tp', [(i, i ^ step) for i in range(tp)])  7.93 us
    all_to_all x1, starting transfers between devices, local(): lax.all_to_all(factors, 'tp', split_axis=0, concat_axis=0, tiled=True)  7.26 us
    pallas_call x3, Pallas kernels, fold(): pl.pallas_call(kernel, name='fold', grid=(1,), out_shape=out_shape, in_sp...  6.96 us
    all_to_all x1, waiting for transfers between devices, local(): lax.all_to_all(factors, 'tp', split_axis=0, concat_axis=0, tiled=True)  5.82 us
    pallas_call x1, Pallas kernels, latent_terms(): pl.pallas_call(kernel, name='latent_terms', out_shape=[jax.ShapeDtypeStru...  5.78 us
    ppermute x2, waiting for transfers between devices, swap(): return [lax.ppermute(array, 'grp', SWAP) for array in arrays]  4.49 us
  transfers between devices with their start and end apart: 20, of which 12 were waited for; matrix products, arithmetic and copies ran while one was open for 2% of the time, Pallas kernels for 44%

profile of v9, /device:TPU:0, one launch (start us, length us, event | category | flops | bytes accessed | tf_op | source)
XLA Modules:
  0.0 112.1 jit_solution(8655716646518836278)
XLA Ops:
  0.0 2.7 %pack_factors.1.after_ref = bf16[8,64,2304]{2,1,0:T(8,128)(2,1)} custom-call(s32[1]{0:T(128)} %bitcast.4.y_ref, bf16[64,28672]{1,0:T(8,128)(2,1)} %bitcast.19, bf16[64,8192]{1,0:T(8,128)(2,1)} %bitcast.20), custom_call_target="tpu_custom_call" | custom-call | flops 1 | bytes 1 | tf_op jit(solution)/shard_map/pack_factors/pallas_call | solution.py:112
  2.7 7.3 %all-to-all-start = ((bf16[8,64,2304]{2,1,0:T(8,128)(2,1)}), bf16[8,64,2304]{2,1,0:T(8,128)(2,1)}, u32[]{:S(2)}, u32[]{:S(2)}) async-start(bf16[8,64,2304]{2,1,0:T(8,128)(2,1)} %pack_factors.1.after_ref), calls=%async_computation | async-start | bytes 4718592 | tf_op jit(solution)/shard_map/all_to_all | solution.py:385
  9.9 3.1 %pack_hidden.1 = (bf16[272,1792]{1,0:T(8,128)(2,1)}, bf16[272,1792]{1,0:T(8,128)(2,1)}) custom-call(s32[1]{0:T(128)} %bitcast.4.y_ref, bf16[256,3584]{1,0:T(8,128)(2,1)} %hidden_ref.7, s32[1,256]{1,0:T(1,128)} %bitcast.21, bf16[8,64,2304]{2,1,0:T(8,128)(2,1)} %pack_factors.1.after_ref), custom_call_target="tpu_custom_call" | custom-call | flops 1 | bytes 1 | tf_op jit(solution)/shard_map/pack_hidden/pallas_call | solution.py:165
  13.1 0.7 collective-permute-start.10
  13.8 0.9 collective-permute-start.9
  14.7 0.3 collective-permute-start.8
  15.0 6.5 %products.3.after_ref = bf16[1,256,1024]{2,1,0:T(8,128)(2,1)} custom-call(s32[1]{0:T(128)} %bitcast.11.t_ref, bf16[256,3584]{1,0:T(8,128)(2,1)} %hidden_ref.7, bf16[3584,8192]{1,0:T(8,128)(2,1)} %weight_ref.5, bf16[272,1792]{1,0:T(8,128)(2,1)} %get-tuple-element.61.after_ref.refs_0_), custom_call_target="tpu_custom_call" | custom-call | flops 1 | bytes 1 | tf_op jit(solution)/shard_map/products/pallas_call | solution.py:54
  21.5 2.0 %collective-permute-start.11 = (bf16[1,256,1024]{2,1,0:T(8,128)(2,1)}, bf16[1,256,1024]{2,1,0:T(8,128)(2,1)}, u32[]{:S(2)}, u32[]{:S(2)}) collective-permute-start(bf16[1,256,1024]{2,1,0:T(8,128)(2,1)} %products.3.after_ref), channel_id=1, source_target_pairs={{0,2},{2,0},{4,6},{6,4},{8,10},{10,8},{12,14},{14,12},{1,3},{3,1},... | collective-permute-start | bytes 1572872 | tf_op jit(solution)/shard_map/ppermute | solution.py:381
  23.5 9.2 %products.4 = (bf16[1,256,1024]{2,1,0:T(8,128)(2,1)}, f32[1,256,1024]{2,1,0:T(8,128)}) custom-call(s32[1]{0:T(128)} %bitcast.11.t_ref, bf16[256,3584]{1,0:T(8,128)(2,1)} %hidden_ref.7, bf16[3584,8192]{1,0:T(8,128)(2,1)} %weight_ref.5, bf16[1,256,1024]{2,1,0:T(8,128)(2,1)} %products.3.after_ref), custom_call_target="tpu_custom_call" | custom-call | flops 1 | bytes 1 | tf_op jit(solution)/shard_map/products/pallas_call | solution.py:54
  32.7 0.0 collective-permute-start.14
  32.7 18.2 %products.5 = (bf16[1,256,1024]{2,1,0:T(8,128)(2,1)}, bf16[1,256,1024]{2,1,0:T(8,128)(2,1)}, f32[3,256,1024]{2,1,0:T(8,128)}) custom-call(s32[1]{0:T(128)} %bitcast.11.t_ref, bf16[256,3584]{1,0:T(8,128)(2,1)} %hidden_ref.7, bf16[3584,8192]{1,0:T(8,128)(2,1)} %weight_ref.5, f32[1,256,1024]{2,1,0:T(8,128)} %get-tuple-element.63.after_ref.refs_0_), custom_call_target="tpu_custom_call" | custom-call | flops 1 | bytes 1 | tf_op jit(solution)/shard_map/products/pallas_call | solution.py:54
  50.9 2.2 %fold.3.refs_4_ = bf16[1,256,1024]{2,1,0:T(8,128)(2,1)} custom-call(f32[1,256,1024]{2,1,0:T(8,128)} %get-tuple-element.63.after_ref.refs_0_, bf16[1,256,1024]{2,1,0:T(8,128)(2,1)} %collective-permute-done.11.refs_1_, f32[3,256,1024]{2,1,0:T(8,128)} %get-tuple-element.64.refs_2_.refs_0_.refs_9_), custom_call_target="tpu_custom_call" | custom-call | flops 1 | bytes 1 | tf_op jit(solution)/shard_map/fold/pallas_call | solution.py:264
  53.2 2.0 %collective-permute-start.15 = (bf16[1,256,1024]{2,1,0:T(8,128)(2,1)}, bf16[1,256,1024]{2,1,0:T(8,128)(2,1)}, u32[]{:S(2)}, u32[]{:S(2)}) collective-permute-start(bf16[1,256,1024]{2,1,0:T(8,128)(2,1)} %fold.3.refs_4_), channel_id=1, source_target_pairs={{0,4},{2,6},{4,0},{6,2},{8,12},{10,14},{12,8},{14,10},{1,5},{3,7},... | collective-permute-start | bytes 1572872 | tf_op jit(solution)/shard_map/ppermute | solution.py:381
  55.2 1.5 %collective-permute-start.13 = (bf16[1,256,1024]{2,1,0:T(8,128)(2,1)}, bf16[1,256,1024]{2,1,0:T(8,128)(2,1)}, u32[]{:S(2)}, u32[]{:S(2)}) collective-permute-start(bf16[1,256,1024]{2,1,0:T(8,128)(2,1)} %get-tuple-element.68), channel_id=1, source_target_pairs={{0,2},{2,0},{4,6},{6,4},{8,10},{10,8},{12,14},{14,12},{1,3},{3,1},... | collective-permute-start | bytes 1572872 | tf_op jit(solution)/shard_map/ppermute | solution.py:381
  56.6 1.6 %collective-permute-done.9.refs_2_ = bf16[272,1792]{1,0:T(8,128)(2,1)} collective-permute-done((bf16[272,1792]{1,0:T(8,128)(2,1)}, bf16[272,1792]{1,0:T(8,128)(2,1)}, u32[]{:S(2)}, u32[]{:S(2)}) %collective-permute-start.9) | collective-permute-done | bytes 974880 | tf_op jit(solution)/shard_map/ppermute | solution.py:388
  58.2 5.8 %all-to-all-done = bf16[8,64,2304]{2,1,0:T(8,128)(2,1)} async-done(((bf16[8,64,2304]{2,1,0:T(8,128)(2,1)}), bf16[8,64,2304]{2,1,0:T(8,128)(2,1)}, u32[]{:S(2)}, u32[]{:S(2)}) %all-to-all-start) | async-done | bytes 2359328 | tf_op jit(solution)/shard_map/all_to_all | solution.py:385
  64.0 5.8 %latent_terms.1 = (f32[2,64,256]{2,1,0:T(8,128)}, f32[2,64,256]{2,1,0:T(8,128)}, bf16[512,512]{1,0:T(8,128)(2,1)}) custom-call(s32[1]{0:T(128)} %bitcast.5.g_ref, bf16[512,2304]{1,0:T(8,128)(2,1)} %bitcast.9.factors_ref, bf16[272,1792]{1,0:T(8,128)(2,1)} %get-tuple-element.61.after_ref.refs_0_, bf16[272,1792]{1,0:T(8,128)(2,1)} %collective-permute-done.8.refs_1_, ...), custom_call_target="tpu_custom_call" | custom-call | flops 1 | bytes 1 | tf_op jit(solution)/shard_map/latent_terms/pallas_call | solution.py:220
  69.8 1.5 %collective-permute-start.12 = (f32[2,64,256]{2,1,0:T(8,128)}, f32[2,64,256]{2,1,0:T(8,128)}, u32[]{:S(2)}, u32[]{:S(2)}) collective-permute-start(f32[2,64,256]{2,1,0:T(8,128)} %get-tuple-element.66), channel_id=1, source_target_pairs={{0,16},{16,0},{1,17},{17,1},{2,18},{18,2},{3,19},{19,3},{4,20},{20... | collective-permute-start | bytes 393224 | tf_op jit(solution)/shard_map/ppermute | solution.py:421
  71.3 1.5 %collective-permute-start.16 = (bf16[1,256,1024]{2,1,0:T(8,128)(2,1)}, bf16[1,256,1024]{2,1,0:T(8,128)(2,1)}, u32[]{:S(2)}, u32[]{:S(2)}) collective-permute-start(bf16[1,256,1024]{2,1,0:T(8,128)(2,1)} %get-tuple-element.72), channel_id=1, source_target_pairs={{0,2},{2,0},{4,6},{6,4},{8,10},{10,8},{12,14},{14,12},{1,3},{3,1},... | collective-permute-start | bytes 1572872 | tf_op jit(solution)/shard_map/ppermute | solution.py:381
  72.8 2.3 %collective-permute-done.12.refs_1_ = f32[2,64,256]{2,1,0:T(8,128)} collective-permute-done((f32[2,64,256]{2,1,0:T(8,128)}, f32[2,64,256]{2,1,0:T(8,128)}, u32[]{:S(2)}, u32[]{:S(2)}) %collective-permute-start.12) | collective-permute-done | bytes 131104 | tf_op jit(solution)/shard_map/ppermute | solution.py:421
  75.1 0.1 collective-permute-done.15.refs_2_
  75.2 2.5 %fold.4.refs_2_ = bf16[1,256,1024]{2,1,0:T(8,128)(2,1)} custom-call(f32[3,256,1024]{2,1,0:T(8,128)} %get-tuple-element.64.refs_2_.refs_0_.refs_9_, bf16[1,256,1024]{2,1,0:T(8,128)(2,1)} %collective-permute-done.14.refs_1_, bf16[1,256,1024]{2,1,0:T(8,128)(2,1)} %collective-permute-done.15.refs_2_, f32[2,64,256]{2,1,0:T(8,128)} %relay.6.refs_3_), custom_call_target="tpu_custom_call" | custom-call | flops 1 | bytes 1 | tf_op jit(solution)/shard_map/fold/pallas_call | solution.py:264
  77.6 0.4 collective-permute-start.17
  78.0 2.3 %fold.5.refs_1_ = bf16[1,256,1024]{2,1,0:T(8,128)(2,1)} custom-call(f32[3,256,1024]{2,1,0:T(8,128)} %get-tuple-element.64.refs_2_.refs_0_.refs_9_, bf16[1,256,1024]{2,1,0:T(8,128)(2,1)} %collective-permute-done.13.refs_1_, bf16[1,256,1024]{2,1,0:T(8,128)(2,1)} %fold.4.refs_2_), custom_call_target="tpu_custom_call" | custom-call | flops 1 | bytes 1 | tf_op jit(solution)/shard_map/fold/pallas_call | solution.py:264
  80.3 2.8 %collective-permute-start.18 = (bf16[1,256,1024]{2,1,0:T(8,128)(2,1)}, bf16[1,256,1024]{2,1,0:T(8,128)(2,1)}, u32[]{:S(2)}, u32[]{:S(2)}) collective-permute-start(bf16[1,256,1024]{2,1,0:T(8,128)(2,1)} %fold.5.refs_1_), channel_id=1, source_target_pairs={{0,4},{2,6},{4,0},{6,2},{8,12},{10,14},{12,8},{14,10},{1,5},{3,7},... | collective-permute-start | bytes 1572872 | tf_op jit(solution)/shard_map/ppermute | solution.py:381
  83.1 13.3 %conditional.5 = (f32[64,256]{1,0:T(8,128)}, bf16[512,512]{1,0:T(8,128)(2,1)}, bf16[512,512]{1,0:T(8,128)(2,1)}) conditional(s32[]{:T(128)} %convert_element_type.15, (f32[2,64,256]{2,1,0:T(8,128)}, bf16[512,512]{1,0:T(8,128)(2,1)}) %tuple.39, (s32[]{:T(128)}, f32[2,64,256]{2,1,0:T(8,128)}, f32[2,64,256]{2,1,0:T(8,128)}, ...), branch_computations={%region_0.0_spmd, %region_1.0_spmd} | conditional | flops 65538 | bytes 5636326 | solution.py:453
  83.1 1.5 %collective-permute-start.7 = (bf16[512,512]{1,0:T(8,128)(2,1)}, bf16[512,512]{1,0:T(8,128)(2,1)}, u32[]{:S(2)}, u32[]{:S(2)}) collective-permute-start(bf16[512,512]{1,0:T(8,128)(2,1)} %get-tuple-element.44), channel_id=1, source_target_pairs={{0,16},{16,0},{1,17},{17,1},{2,18},{18,2},{3,19},{19,3},{4,20},{20... | collective-permute-start | bytes 1572872 | tf_op jit(solution)/shard_map/cond/branch_1_fun/ppermute | solution.py:448
  84.6 2.3 %conditional.1 = (bf16[512,512]{1,0:T(8,128)(2,1)}) conditional(s32[]{:T(128)} %convert_element_type.1, bf16[512,512]{1,0:T(8,128)(2,1)} %get-tuple-element.44, bf16[512,512]{1,0:T(8,128)(2,1)} %get-tuple-element.44), branch_computations={%region_4.0_spmd, %region_5.0_spmd} | conditional | bytes 2097200 | solution.py:449
  84.6 2.2 %collective-permute-done = bf16[512,512]{1,0:T(8,128)(2,1)} collective-permute-done((bf16[512,512]{1,0:T(8,128)(2,1)}, bf16[512,512]{1,0:T(8,128)(2,1)}, u32[]{:S(2)}, u32[]{:S(2)}) %collective-permute-start) | collective-permute-done | bytes 524320 | tf_op jit(solution)/shard_map/cond/branch_1_fun/cond/branch_1_fun/ppermute | solution.py:431
  86.9 7.3 %conditional = (f32[64,256]{1,0:T(8,128)}) conditional(s32[]{:T(128)} %convert_element_type.1, f32[2,64,256]{2,1,0:T(8,128)} %get-tuple-element.42, (f32[2,64,256]{2,1,0:T(8,128)}, f32[2,64,256]{2,1,0:T(8,128)}) %tuple.33), branch_computations={%region_2.0_spmd, %region_3.0_spmd} | conditional | flops 65536 | bytes 1441880 | solution.py:450
  86.9 1.0 add.6
  87.9 0.2 collective-permute-start.5
  88.1 1.1 collective-permute-done.5
  89.2 0.8 collective-permute-start.6
  90.0 3.6 %collective-permute-done.6 = f32[64,256]{1,0:T(8,128)S(1)} collective-permute-done((f32[64,256]{1,0:T(8,128)S(1)}, f32[64,256]{1,0:T(8,128)S(1)}, u32[]{:S(2)}, u32[]{:S(2)}) %collective-permute-start.6) | collective-permute-done | bytes 65568 | tf_op jit(solution)/shard_map/cond/branch_1_fun/cond/branch_1_fun/ppermute | solution.py:381
  93.5 0.6 add.8
  94.2 2.2 %collective-permute-done.7 = bf16[512,512]{1,0:T(8,128)(2,1)} collective-permute-done((bf16[512,512]{1,0:T(8,128)(2,1)}, bf16[512,512]{1,0:T(8,128)(2,1)}, u32[]{:S(2)}, u32[]{:S(2)}) %collective-permute-start.7) | collective-permute-done | bytes 524320 | tf_op jit(solution)/shard_map/cond/branch_1_fun/ppermute | solution.py:448
  96.4 2.3 %conditional.6 = (bf16[512,512]{1,0:T(8,128)(2,1)}) conditional(s32[]{:T(128)} %convert_element_type.15, bf16[512,512]{1,0:T(8,128)(2,1)} %relay.9.refs_7_, bf16[512,512]{1,0:T(8,128)(2,1)} %relay.9.refs_7_), branch_computations={%region_6.0_spmd, %region_7.0_spmd} | conditional | bytes 2097200 | solution.py:464
  96.4 2.2 %collective-permute-done.1 = bf16[512,512]{1,0:T(8,128)(2,1)} collective-permute-done((bf16[512,512]{1,0:T(8,128)(2,1)}, bf16[512,512]{1,0:T(8,128)(2,1)}, u32[]{:S(2)}, u32[]{:S(2)}) %collective-permute-start.1) | collective-permute-done | bytes 524320 | tf_op jit(solution)/shard_map/cond/branch_1_fun/ppermute | solution.py:431
  98.6 9.5 %conditional.7 = (bf16[64,256]{1,0:T(8,128)(2,1)}, bf16[64,256]{1,0:T(8,128)(2,1)}, bf16[64,256]{1,0:T(8,128)(2,1)}) conditional(s32[]{:T(128)} %convert_element_type.15, f32[64,256]{1,0:T(8,128)} %relay.10.refs_0_, f32[64,256]{1,0:T(8,128)} %relay.10.refs_0_), branch_computations={%region_8.0_spmd, %region_9.0_spmd} | conditional | flops 16384 | bytes 491664 | solution.py:466
  98.6 0.8 convert_element_type.9
  99.5 1.5 %collective-permute-start.4 = (bf16[64,256]{1,0:T(8,128)(2,1)S(1)}, bf16[64,256]{1,0:T(8,128)(2,1)}, u32[]{:S(2)}, u32[]{:S(2)}) collective-permute-start(bf16[64,256]{1,0:T(8,128)(2,1)S(1)} %convert_element_type.9), channel_id=1, source_target_pairs={{0,12},{2,14},{4,8},{6,10},{8,4},{10,6},{12,0},{14,2},{1,13},{3,15... | collective-permute-start | bytes 98312 | tf_op jit(solution)/shard_map/cond/branch_1_fun/ppermute | solution.py:381
  101.0 0.2 collective-permute-start.3
  101.2 2.6 %collective-permute-start.2 = (bf16[64,256]{1,0:T(8,128)(2,1)S(1)}, bf16[64,256]{1,0:T(8,128)(2,1)}, u32[]{:S(2)}, u32[]{:S(2)}) collective-permute-start(bf16[64,256]{1,0:T(8,128)(2,1)S(1)} %convert_element_type.9), channel_id=1, source_target_pairs={{0,4},{2,6},{4,0},{6,2},{8,12},{10,14},{12,8},{14,10},{1,5},{3,7},... | collective-permute-start | bytes 98312 | tf_op jit(solution)/shard_map/cond/branch_1_fun/ppermute | solution.py:381
  103.8 1.5 %collective-permute-done.4 = bf16[64,256]{1,0:T(8,128)(2,1)} collective-permute-done((bf16[64,256]{1,0:T(8,128)(2,1)S(1)}, bf16[64,256]{1,0:T(8,128)(2,1)}, u32[]{:S(2)}, u32[]{:S(2)}) %collective-permute-start.4) | collective-permute-done | bytes 32800 | tf_op jit(solution)/shard_map/cond/branch_1_fun/ppermute | solution.py:381
  105.3 1.2 %collective-permute-done.3 = bf16[64,256]{1,0:T(8,128)(2,1)} collective-permute-done((bf16[64,256]{1,0:T(8,128)(2,1)S(1)}, bf16[64,256]{1,0:T(8,128)(2,1)}, u32[]{:S(2)}, u32[]{:S(2)}) %collective-permute-start.3) | collective-permute-done | bytes 32800 | tf_op jit(solution)/shard_map/cond/branch_1_fun/ppermute | solution.py:381
  106.5 1.6 %collective-permute-done.2 = bf16[64,256]{1,0:T(8,128)(2,1)} collective-permute-done((bf16[64,256]{1,0:T(8,128)(2,1)S(1)}, bf16[64,256]{1,0:T(8,128)(2,1)}, u32[]{:S(2)}, u32[]{:S(2)}) %collective-permute-start.2) | collective-permute-done | bytes 32800 | tf_op jit(solution)/shard_map/cond/branch_1_fun/ppermute | solution.py:381
  108.1 4.0 %finish.1 = bf16[256,1024]{1,0:T(8,128)(2,1)} custom-call(s32[1]{0:T(128)} %bitcast.4.y_ref, s32[1]{0:T(128)} %bitcast.5.g_ref, f32[64,256]{1,0:T(8,128)} %relay.10.refs_0_, bf16[64,256]{1,0:T(8,128)(2,1)} %get-tuple-element.73.refs_1_, bf16[64,256]{1,0:T(8,128)(2,1)} %get-tuple-element.74.refs_2_, bf16[64,256]{1,0:T(8,128)(2,1)} %get-tuple-element.75.refs_1_.refs_3_, ...), custom_call_target="tpu_custom_call" | custom-call | flops 1 | bytes 1 | tf_op jit(solution)/shard_map/finish/pallas_call | solution.py:353
  (18 shorter events, 0.0 us)
Async XLA Ops:
  2.7 61.4 %all-to-all-start = ((bf16[8,64,2304]{2,1,0:T(8,128)(2,1)}), bf16[8,64,2304]{2,1,0:T(8,128)(2,1)}, u32[]{:S(2)}, u32[]{:S(2)}) async-start(bf16[8,64,2304]{2,1,0:T(8,128)(2,1)} %pack_factors.1.after_ref), calls=%async_computation | async-start | bytes 4718592 | tf_op jit(solution)/shard_map/all_to_all | solution.py:385
  13.1 42.1 %collective-permute-start.10 = (bf16[272,1792]{1,0:T(8,128)(2,1)}, bf16[272,1792]{1,0:T(8,128)(2,1)}, u32[]{:S(2)}, u32[]{:S(2)}) collective-permute-start(bf16[272,1792]{1,0:T(8,128)(2,1)} %get-tuple-element.62), channel_id=1, source_target_pairs={{0,17},{1,16},{16,1},{17,0},{2,19},{3,18},{18,3},{19,2},{4,21},{5,... | collective-permute-start | bytes 2924552 | tf_op jit(solution)/shard_map/ppermute | solution.py:390
  13.8 44.4 %collective-permute-start.9 = (bf16[272,1792]{1,0:T(8,128)(2,1)}, bf16[272,1792]{1,0:T(8,128)(2,1)}, u32[]{:S(2)}, u32[]{:S(2)}) collective-permute-start(bf16[272,1792]{1,0:T(8,128)(2,1)} %get-tuple-element.62), channel_id=1, source_target_pairs={{0,16},{16,0},{1,17},{17,1},{2,18},{18,2},{3,19},{19,3},{4,20},{20... | collective-permute-start | bytes 2924552 | tf_op jit(solution)/shard_map/ppermute | solution.py:388
  14.7 43.5 %collective-permute-start.8 = (bf16[272,1792]{1,0:T(8,128)(2,1)}, bf16[272,1792]{1,0:T(8,128)(2,1)}, u32[]{:S(2)}, u32[]{:S(2)}) collective-permute-start(bf16[272,1792]{1,0:T(8,128)(2,1)} %get-tuple-element.61.after_ref.refs_0_), channel_id=1, source_target_pairs={{0,1},{1,0},{2,3},{3,2},{4,5},{5,4},{6,7},{7,6},{8,9},{9,8},{10,11... | collective-permute-start | bytes 2924552 | tf_op jit(solution)/shard_map/ppermute | solution.py:389
  21.5 29.4 %collective-permute-start.11 = (bf16[1,256,1024]{2,1,0:T(8,128)(2,1)}, bf16[1,256,1024]{2,1,0:T(8,128)(2,1)}, u32[]{:S(2)}, u32[]{:S(2)}) collective-permute-start(bf16[1,256,1024]{2,1,0:T(8,128)(2,1)} %products.3.after_ref), channel_id=1, source_target_pairs={{0,2},{2,0},{4,6},{6,4},{8,10},{10,8},{12,14},{14,12},{1,3},{3,1},... | collective-permute-start | bytes 1572872 | tf_op jit(solution)/shard_map/ppermute | solution.py:381
  32.7 42.5 %collective-permute-start.14 = (bf16[1,256,1024]{2,1,0:T(8,128)(2,1)}, bf16[1,256,1024]{2,1,0:T(8,128)(2,1)}, u32[]{:S(2)}, u32[]{:S(2)}) collective-permute-start(bf16[1,256,1024]{2,1,0:T(8,128)(2,1)} %get-tuple-element.69), channel_id=1, source_target_pairs={{0,2},{2,0},{4,6},{6,4},{8,10},{10,8},{12,14},{14,12},{1,3},{3,1},... | collective-permute-start | bytes 1572872 | tf_op jit(solution)/shard_map/ppermute | solution.py:381
  53.2 22.0 %collective-permute-start.15 = (bf16[1,256,1024]{2,1,0:T(8,128)(2,1)}, bf16[1,256,1024]{2,1,0:T(8,128)(2,1)}, u32[]{:S(2)}, u32[]{:S(2)}) collective-permute-start(bf16[1,256,1024]{2,1,0:T(8,128)(2,1)} %fold.3.refs_4_), channel_id=1, source_target_pairs={{0,4},{2,6},{4,0},{6,2},{8,12},{10,14},{12,8},{14,10},{1,5},{3,7},... | collective-permute-start | bytes 1572872 | tf_op jit(solution)/shard_map/ppermute | solution.py:381
  55.2 22.9 %collective-permute-start.13 = (bf16[1,256,1024]{2,1,0:T(8,128)(2,1)}, bf16[1,256,1024]{2,1,0:T(8,128)(2,1)}, u32[]{:S(2)}, u32[]{:S(2)}) collective-permute-start(bf16[1,256,1024]{2,1,0:T(8,128)(2,1)} %get-tuple-element.68), channel_id=1, source_target_pairs={{0,2},{2,0},{4,6},{6,4},{8,10},{10,8},{12,14},{14,12},{1,3},{3,1},... | collective-permute-start | bytes 1572872 | tf_op jit(solution)/shard_map/ppermute | solution.py:381
  69.8 5.3 %collective-permute-start.12 = (f32[2,64,256]{2,1,0:T(8,128)}, f32[2,64,256]{2,1,0:T(8,128)}, u32[]{:S(2)}, u32[]{:S(2)}) collective-permute-start(f32[2,64,256]{2,1,0:T(8,128)} %get-tuple-element.66), channel_id=1, source_target_pairs={{0,16},{16,0},{1,17},{17,1},{2,18},{18,2},{3,19},{19,3},{4,20},{20... | collective-permute-start | bytes 393224 | tf_op jit(solution)/shard_map/ppermute | solution.py:421
  71.3 25.0 %collective-permute-start.16 = (bf16[1,256,1024]{2,1,0:T(8,128)(2,1)}, bf16[1,256,1024]{2,1,0:T(8,128)(2,1)}, u32[]{:S(2)}, u32[]{:S(2)}) collective-permute-start(bf16[1,256,1024]{2,1,0:T(8,128)(2,1)} %get-tuple-element.72), channel_id=1, source_target_pairs={{0,2},{2,0},{4,6},{6,4},{8,10},{10,8},{12,14},{14,12},{1,3},{3,1},... | collective-permute-start | bytes 1572872 | tf_op jit(solution)/shard_map/ppermute | solution.py:381
  77.6 30.5 %collective-permute-start.17 = (bf16[1,256,1024]{2,1,0:T(8,128)(2,1)}, bf16[1,256,1024]{2,1,0:T(8,128)(2,1)}, u32[]{:S(2)}, u32[]{:S(2)}) collective-permute-start(bf16[1,256,1024]{2,1,0:T(8,128)(2,1)} %fold.4.refs_2_), channel_id=1, source_target_pairs={{0,8},{2,10},{4,12},{6,14},{8,0},{10,2},{12,4},{14,6},{1,9},{3,11}... | collective-permute-start | bytes 1572872 | tf_op jit(solution)/shard_map/ppermute | solution.py:381
  80.3 27.9 %collective-permute-start.18 = (bf16[1,256,1024]{2,1,0:T(8,128)(2,1)}, bf16[1,256,1024]{2,1,0:T(8,128)(2,1)}, u32[]{:S(2)}, u32[]{:S(2)}) collective-permute-start(bf16[1,256,1024]{2,1,0:T(8,128)(2,1)} %fold.5.refs_1_), channel_id=1, source_target_pairs={{0,4},{2,6},{4,0},{6,2},{8,12},{10,14},{12,8},{14,10},{1,5},{3,7},... | collective-permute-start | bytes 1572872 | tf_op jit(solution)/shard_map/ppermute | solution.py:381
  83.1 13.3 %collective-permute-start.7 = (bf16[512,512]{1,0:T(8,128)(2,1)}, bf16[512,512]{1,0:T(8,128)(2,1)}, u32[]{:S(2)}, u32[]{:S(2)}) collective-permute-start(bf16[512,512]{1,0:T(8,128)(2,1)} %get-tuple-element.44), channel_id=1, source_target_pairs={{0,16},{16,0},{1,17},{17,1},{2,18},{18,2},{3,19},{19,3},{4,20},{20... | collective-permute-start | bytes 1572872 | tf_op jit(solution)/shard_map/cond/branch_1_fun/ppermute | solution.py:448
  84.6 2.3 %collective-permute-start = (bf16[512,512]{1,0:T(8,128)(2,1)}, bf16[512,512]{1,0:T(8,128)(2,1)}, u32[]{:S(2)}, u32[]{:S(2)}) collective-permute-start(bf16[512,512]{1,0:T(8,128)(2,1)} %param.4), channel_id=1, source_target_pairs={{0,1},{1,0},{2,3},{3,2},{4,5},{5,4},{6,7},{7,6},{8,9},{9,8},{10,11... | collective-permute-start | bytes 1572872 | tf_op jit(solution)/shard_map/cond/branch_1_fun/cond/branch_1_fun/ppermute | solution.py:431
  87.9 1.3 %collective-permute-start.5 = (f32[64,256]{1,0:T(8,128)S(1)}, f32[64,256]{1,0:T(8,128)S(1)}, u32[]{:S(2)}, u32[]{:S(2)}) collective-permute-start(f32[64,256]{1,0:T(8,128)S(1)} %slice_bitcast_fusion.2), channel_id=1, source_target_pairs={{0,1},{1,0},{2,3},{3,2},{4,5},{5,4},{6,7},{7,6},{8,9},{9,8},{10,11... | collective-permute-start | bytes 196616 | tf_op jit(solution)/shard_map/cond/branch_1_fun/cond/branch_1_fun/ppermute | solution.py:435
  89.2 4.3 %collective-permute-start.6 = (f32[64,256]{1,0:T(8,128)S(1)}, f32[64,256]{1,0:T(8,128)S(1)}, u32[]{:S(2)}, u32[]{:S(2)}) collective-permute-start(f32[64,256]{1,0:T(8,128)S(1)} %fusion), channel_id=1, source_target_pairs={{0,2},{2,0},{4,6},{6,4},{8,10},{10,8},{12,14},{14,12},{1,3},{3,1},... | collective-permute-start | bytes 196616 | tf_op jit(solution)/shard_map/cond/branch_1_fun/cond/branch_1_fun/ppermute | solution.py:381
  96.4 2.3 %collective-permute-start.1 = (bf16[512,512]{1,0:T(8,128)(2,1)}, bf16[512,512]{1,0:T(8,128)(2,1)}, u32[]{:S(2)}, u32[]{:S(2)}) collective-permute-start(bf16[512,512]{1,0:T(8,128)(2,1)} %param.7), channel_id=1, source_target_pairs={{0,1},{1,0},{2,3},{3,2},{4,5},{5,4},{6,7},{7,6},{8,9},{9,8},{10,11... | collective-permute-start | bytes 1572872 | tf_op jit(solution)/shard_map/cond/branch_1_fun/ppermute | solution.py:431
  99.5 5.9 %collective-permute-start.4 = (bf16[64,256]{1,0:T(8,128)(2,1)S(1)}, bf16[64,256]{1,0:T(8,128)(2,1)}, u32[]{:S(2)}, u32[]{:S(2)}) collective-permute-start(bf16[64,256]{1,0:T(8,128)(2,1)S(1)} %convert_element_type.9), channel_id=1, source_target_pairs={{0,12},{2,14},{4,8},{6,10},{8,4},{10,6},{12,0},{14,2},{1,13},{3,15... | collective-permute-start | bytes 98312 | tf_op jit(solution)/shard_map/cond/branch_1_fun/ppermute | solution.py:381
  101.0 5.5 %collective-permute-start.3 = (bf16[64,256]{1,0:T(8,128)(2,1)S(1)}, bf16[64,256]{1,0:T(8,128)(2,1)}, u32[]{:S(2)}, u32[]{:S(2)}) collective-permute-start(bf16[64,256]{1,0:T(8,128)(2,1)S(1)} %convert_element_type.9), channel_id=1, source_target_pairs={{0,8},{2,10},{4,12},{6,14},{8,0},{10,2},{12,4},{14,6},{1,9},{3,11}... | collective-permute-start | bytes 98312 | tf_op jit(solution)/shard_map/cond/branch_1_fun/ppermute | solution.py:381
  101.2 6.9 %collective-permute-start.2 = (bf16[64,256]{1,0:T(8,128)(2,1)S(1)}, bf16[64,256]{1,0:T(8,128)(2,1)}, u32[]{:S(2)}, u32[]{:S(2)}) collective-permute-start(bf16[64,256]{1,0:T(8,128)(2,1)S(1)} %convert_element_type.9), channel_id=1, source_target_pairs={{0,4},{2,6},{4,0},{6,2},{8,12},{10,14},{12,8},{14,10},{1,5},{3,7},... | collective-permute-start | bytes 98312 | tf_op jit(solution)/shard_map/cond/branch_1_fun/ppermute | solution.py:381
